TPU v7x, 32 devices: a whole 2x2x4 slice. The times are simulated.
32 devices in a mesh: dp: 4 (over z), blk: 4 (over y, core), uly: 2 (over x).
Axes of the slice: x: 2, y: 2, z: 4, core: 2. Of those that a mesh axis runs over, the one named last changes fastest.
Arguments:
- layer_input: bfloat16 [4096, 2048], P(('dp', 'blk', 'uly')), may hold values from -16 to 16
- span_order: int32 [4, 8], P('dp'), may hold values from 0 to 7, each once within a row
- qkv_weight: bfloat16 [2048, 4096], P(('dp', 'blk', 'uly')), may hold values from -0.125 to 0.125
- out_weight: bfloat16 [2048, 2048], P(('dp', 'blk', 'uly')), may hold values from -1.5 to 1.5
- gate_up_weight: bfloat16 [2048, 2, 8192], P(('dp', 'blk'), None, 'uly'), may hold values from -0.125 to 0.125
- down_weight: bfloat16 [2048, 8192], P(('dp', 'blk'), 'uly'), may hold values from -0.0625 to 0.0625
- attn_gain: bfloat16 [2048], P(('dp', 'blk', 'uly')), may hold values from 0.099609375 to 1.8984375
- mlp_gain: bfloat16 [2048], P(('dp', 'blk', 'uly')), may hold values from 0.099609375 to 1.8984375
- output_cotangent: bfloat16 [4096, 2048], P(('dp', 'blk', 'uly')), may hold values from -6 to 6
Outputs:
- layer_output: bfloat16 [4096, 2048], P(('dp', 'blk', 'uly'))
- input_grad: float32 [4096, 2048], P(('dp', 'blk', 'uly'))
- qkv_grad: float32 [2048, 4096], P(('dp', 'blk', 'uly'))
- out_weight_grad: float32 [2048, 2048], P(('dp', 'blk', 'uly'))
- gate_up_grad: float32 [2048, 2, 8192], P(('dp', 'blk'), None, 'uly')
- down_grad: float32 [2048, 8192], P(('dp', 'blk'), 'uly')
- attn_gain_grad: float32 [2048], P(('dp', 'blk', 'uly'))
- mlp_gain_grad: float32 [2048], P(('dp', 'blk', 'uly'))
- rms_values: float32 [5], replicated
Inputs may be any that keep to these rules, and one draw needn't show every extreme that they name: `span_order`: each row names each of the 8 position blocks of its sequence once.
All inputs are finite; a program needn't handle non-finite values.
Results may differ from a plain program's by a relative error of at most 0.023.
Values may be sent and summed in bfloat16 or wider, within the bound.
No kernel may reach another device: no remote copies, remote signals or barrier semaphores. Data moves between devices by JAX's collectives and lax.ppermute only.
A program may use at most 384 MiB of HBM per device.

v0:
```python
import jax
import jax.numpy as jnp
from jax import lax
from jax.sharding import PartitionSpec as P

D = 2048
H = 16
KV = 8
HD = 128


EPSILON = 1e-06
ROPE_BASE = 1000000.0
MASKED = -1e30


def rms_scale(values, gain):
    return values * lax.rsqrt(jnp.mean(values * values, axis=-1, keepdims=True) + EPSILON) * gain


def rope_angles(positions):
    freq_index = jnp.arange(HD // 2, dtype=jnp.float32)
    inverse_freq = ROPE_BASE ** (-2.0 * freq_index / HD)
    return positions.astype(jnp.float32)[:, None] * inverse_freq[None, :]


def rotate_pairs(values, angles):
    half_size = values.shape[-1] // 2
    first_half = values[..., :half_size]
    second_half = values[..., half_size:]
    cosine = jnp.cos(angles)[:, None, :]
    sine = jnp.sin(angles)[:, None, :]
    return jnp.concatenate(
        [first_half * cosine - second_half * sine, second_half * cosine + first_half * sine],
        axis=-1,
    )


def sequence_positions(row_index, span_size, order_row):
    block_index = row_index // span_size
    picks = block_index[:, None] == jnp.arange(order_row.shape[0], dtype=jnp.int32)[None, :]
    chosen = jnp.sum(jnp.where(picks, order_row[None, :], 0), axis=1)
    return chosen * span_size + row_index % span_size


def contract_rows(left_side, right_side):
    return lax.dot_general(
        left_side, right_side, (((0,), (0,)), ((), ())), preferred_element_type=jnp.float32
    )


def contract_cols(left_side, right_side):
    return lax.dot_general(
        left_side, right_side, (((1,), (1,)), ((), ())), preferred_element_type=jnp.float32
    )


def per_device(
    layer_input,
    span_order,
    qkv_weight,
    out_weight,
    gate_up_weight,
    down_weight,
    attn_gain,
    mlp_gain,
    output_cotangent,
):
    tok_rows = layer_input.shape[0]
    uly_size = lax.axis_size("uly")
    blk_size = lax.axis_size("blk")
    group_rows = tok_rows * uly_size
    seq_rows = group_rows * blk_size
    span_size = group_rows // 2
    order_row = span_order[0]
    local_kv = KV // uly_size
    local_heads = H // uly_size
    group_size = H // KV
    ff_local = down_weight.shape[1]
    score_scale = HD ** (-0.5)
    token_start = (lax.axis_index("blk") * uly_size + lax.axis_index("uly")) * tok_rows
    token_pos = sequence_positions(
        token_start + jnp.arange(tok_rows, dtype=jnp.int32), span_size, order_row
    )
    token_angles = rope_angles(token_pos)
    query_pos = sequence_positions(
        lax.axis_index("blk") * group_rows + jnp.arange(group_rows, dtype=jnp.int32),
        span_size,
        order_row,
    )
    stream_in = layer_input.astype(jnp.float32)
    qkv_full, out_full, attn_gain_full, mlp_gain_full = (
        lax.all_gather(qkv_weight, ("dp", "blk", "uly"), axis=0, tiled=True),
        lax.all_gather(out_weight, ("dp", "blk", "uly"), axis=0, tiled=True),
        lax.all_gather(attn_gain, ("dp", "blk", "uly"), axis=0, tiled=True),
        lax.all_gather(mlp_gain, ("dp", "blk", "uly"), axis=0, tiled=True),
    )
    gate_up_cols, down_cols = (
        lax.all_gather(gate_up_weight, ("dp", "blk"), axis=0, tiled=True),
        lax.all_gather(down_weight, ("dp", "blk"), axis=0, tiled=True),
    )
    attn_gain_wide = attn_gain_full.astype(jnp.float32)
    mlp_gain_wide = mlp_gain_full.astype(jnp.float32)
    normed_attn = rms_scale(stream_in, attn_gain_wide).astype(jnp.bfloat16)
    qkv_all = jnp.dot(normed_attn, qkv_full, preferred_element_type=jnp.float32)
    query_tok = (
        rotate_pairs(qkv_all[:, : H * HD].reshape(tok_rows, H, HD), token_angles)
        .reshape(tok_rows, H * HD)
        .astype(jnp.bfloat16)
    )
    key_tok = (
        rotate_pairs(qkv_all[:, H * HD : (H + KV) * HD].reshape(tok_rows, KV, HD), token_angles)
        .reshape(tok_rows, KV * HD)
        .astype(jnp.bfloat16)
    )
    value_tok = qkv_all[:, (H + KV) * HD :].astype(jnp.bfloat16)
    query_grp, key_grp, value_grp = (
        lax.all_to_all(query_tok, "uly", split_axis=1, concat_axis=0, tiled=True),
        lax.all_to_all(key_tok, "uly", split_axis=1, concat_axis=0, tiled=True),
        lax.all_to_all(value_tok, "uly", split_axis=1, concat_axis=0, tiled=True),
    )
    query_four = query_grp.reshape(group_rows, local_kv, group_size, HD)
    key_whole, value_whole = (
        lax.all_gather(key_grp, "blk", axis=0, tiled=True),
        lax.all_gather(value_grp, "blk", axis=0, tiled=True),
    )
    block_count = seq_rows // group_rows

    def take_block(block_index):
        offset = block_index * group_rows
        key_block = lax.dynamic_slice_in_dim(key_whole, offset, group_rows, 0).reshape(
            group_rows, local_kv, HD
        )
        value_block = lax.dynamic_slice_in_dim(value_whole, offset, group_rows, 0).reshape(
            group_rows, local_kv, HD
        )
        key_pos = sequence_positions(
            offset + jnp.arange(group_rows, dtype=jnp.int32), span_size, order_row
        )
        return (offset, key_block, value_block, key_pos)

    def attend_step(block_index, running):
        top_run, total_run, acc_run = running
        offset, key_block, value_block, key_pos = take_block(block_index)
        scores = (
            jnp.einsum("rkgd,pkd->kgrp", query_four, key_block, preferred_element_type=jnp.float32)
            * score_scale
        )
        allowed = key_pos[None, :] <= query_pos[:, None]
        scores = jnp.where(allowed, scores, MASKED)
        top_new = jnp.maximum(top_run, jnp.max(scores, axis=-1))
        weights = jnp.where(allowed, jnp.exp(scores - top_new[..., None]), 0.0)
        shrink_factor = jnp.exp(top_run - top_new)
        total_new = total_run * shrink_factor + jnp.sum(weights, axis=-1)
        acc_new = acc_run * shrink_factor[..., None] + jnp.einsum(
            "kgrp,pkd->kgrd",
            weights.astype(jnp.bfloat16),
            value_block,
            preferred_element_type=jnp.float32,
        )
        return (top_new, total_new, acc_new)

    start_state = (
        jnp.full((local_kv, group_size, group_rows), MASKED, jnp.float32),
        jnp.zeros((local_kv, group_size, group_rows), jnp.float32),
        jnp.zeros((local_kv, group_size, group_rows, HD), jnp.float32),
    )
    top_end, total_end, acc_end = lax.fori_loop(0, block_count, attend_step, start_state)
    log_total = top_end + jnp.log(total_end)
    head_rows = jnp.transpose(acc_end / total_end[..., None], (2, 0, 1, 3))
    heads_group = head_rows.reshape(group_rows, local_heads * HD).astype(jnp.bfloat16)
    heads_tok = lax.all_to_all(heads_group, "uly", split_axis=0, concat_axis=1, tiled=True)
    attn_out = contract_cols(heads_tok, out_full)
    middle = stream_in + attn_out
    normed_mlp = rms_scale(middle, mlp_gain_wide).astype(jnp.bfloat16)
    normed_grp, cotangent_grp = (
        lax.all_gather(normed_mlp, "uly", axis=0, tiled=True),
        lax.all_gather(output_cotangent, "uly", axis=0, tiled=True),
    )
    gate_up = jnp.einsum(
        "rd,dcf->rcf", normed_grp, gate_up_cols, preferred_element_type=jnp.float32
    )
    gate_part = gate_up[:, 0, :]
    up_part = gate_up[:, 1, :]
    hidden = (jax.nn.silu(gate_part) * up_part).astype(jnp.bfloat16)
    mlp_part = contract_cols(hidden, down_cols)
    mlp_out = lax.psum_scatter(
        mlp_part.astype(jnp.bfloat16), "uly", scatter_dimension=0, tiled=True
    ).astype(jnp.float32)
    final_stream = middle + mlp_out
    local_squares = jnp.stack(
        [
            jnp.sum(stream_in * stream_in),
            jnp.sum(attn_out * attn_out),
            jnp.sum(middle * middle),
            jnp.sum(mlp_out * mlp_out),
            jnp.sum(final_stream * final_stream),
        ]
    )
    total_squares = lax.psum(local_squares, ("dp", "blk", "uly"))
    entry_count = tok_rows * lax.axis_size("dp") * blk_size * uly_size * D
    rms_values = jnp.sqrt(total_squares / entry_count)
    grad_hidden = jnp.dot(cotangent_grp, down_cols, preferred_element_type=jnp.float32)
    sigmoid_gate = jax.nn.sigmoid(gate_part)
    grad_gate = grad_hidden * up_part * sigmoid_gate * (1.0 + gate_part * (1.0 - sigmoid_gate))
    grad_up = grad_hidden * gate_part * sigmoid_gate
    grad_gate_up = jnp.stack([grad_gate, grad_up], axis=1).astype(jnp.bfloat16)
    grad_normed_part = jnp.einsum(
        "rcf,dcf->rd", grad_gate_up, gate_up_cols, preferred_element_type=jnp.float32
    )
    grad_normed_mlp = lax.psum_scatter(
        grad_normed_part.astype(jnp.bfloat16), "uly", scatter_dimension=0, tiled=True
    ).astype(jnp.float32)
    gate_term = jnp.einsum(
        "rd,rcf->dcf", normed_grp, grad_gate_up, preferred_element_type=jnp.float32
    ).reshape(lax.axis_size(("dp", "blk")) * gate_up_weight.shape[0], 2 * ff_local)
    mlp_grads = lax.psum_scatter(
        jnp.concatenate([gate_term, contract_rows(cotangent_grp, hidden)], axis=1).astype(
            jnp.bfloat16
        ),
        ("dp", "blk"),
        scatter_dimension=0,
        tiled=True,
    ).astype(jnp.float32)
    gate_up_grad = mlp_grads[:, : 2 * ff_local].reshape(mlp_grads.shape[0], 2, ff_local)
    down_grad = mlp_grads[:, 2 * ff_local :]
    mlp_value, mlp_pull = jax.vjp(rms_scale, middle, mlp_gain_wide)
    grad_middle_norm, mlp_gain_grad_full = mlp_pull(grad_normed_mlp)
    grad_middle = output_cotangent.astype(jnp.float32) + grad_middle_norm
    grad_attn_out = grad_middle.astype(jnp.bfloat16)
    grad_heads_tok = jnp.dot(grad_attn_out, out_full, preferred_element_type=jnp.float32).astype(
        jnp.bfloat16
    )
    out_weight_term = contract_rows(grad_attn_out, heads_tok)
    grad_heads = lax.all_to_all(grad_heads_tok, "uly", split_axis=1, concat_axis=0, tiled=True)
    grad_four = grad_heads.reshape(group_rows, local_kv, group_size, HD)
    row_delta = jnp.transpose(
        jnp.sum(grad_four.astype(jnp.float32) * head_rows, axis=-1), (1, 2, 0)
    )

    def backward_step(block_index, running):
        grad_query_run, grad_key_all, grad_value_all = running
        offset, key_block, value_block, key_pos = take_block(block_index)
        scores = (
            jnp.einsum("rkgd,pkd->kgrp", query_four, key_block, preferred_element_type=jnp.float32)
            * score_scale
        )
        allowed = key_pos[None, :] <= query_pos[:, None]
        soft_probs = jnp.where(
            allowed, jnp.exp(jnp.where(allowed, scores, MASKED) - log_total[..., None]), 0.0
        )
        grad_probs = jnp.einsum(
            "rkgd,pkd->kgrp", grad_four, value_block, preferred_element_type=jnp.float32
        )
        grad_scores = (soft_probs * (grad_probs - row_delta[..., None])).astype(jnp.bfloat16)
        grad_query_run = (
            grad_query_run
            + jnp.einsum(
                "kgrp,pkd->kgrd", grad_scores, key_block, preferred_element_type=jnp.float32
            )
            * score_scale
        )
        grad_key_block = (
            jnp.einsum(
                "kgrp,rkgd->pkd", grad_scores, query_four, preferred_element_type=jnp.float32
            )
            * score_scale
        ).reshape(group_rows, local_kv * HD)
        grad_value_block = jnp.einsum(
            "kgrp,rkgd->pkd",
            soft_probs.astype(jnp.bfloat16),
            grad_four,
            preferred_element_type=jnp.float32,
        ).reshape(group_rows, local_kv * HD)
        grad_key_all = lax.dynamic_update_slice_in_dim(grad_key_all, grad_key_block, offset, 0)
        grad_value_all = lax.dynamic_update_slice_in_dim(
            grad_value_all, grad_value_block, offset, 0
        )
        return (grad_query_run, grad_key_all, grad_value_all)

    back_state = (
        jnp.zeros((local_kv, group_size, group_rows, HD), jnp.float32),
        jnp.zeros((seq_rows, local_kv * HD), jnp.float32),
        jnp.zeros((seq_rows, local_kv * HD), jnp.float32),
    )
    grad_query_end, grad_key_whole, grad_value_whole = lax.fori_loop(
        0, block_count, backward_step, back_state
    )
    grad_key_own, grad_value_own = (
        lax.psum_scatter(
            grad_key_whole.astype(jnp.bfloat16), "blk", scatter_dimension=0, tiled=True
        ).astype(jnp.float32),
        lax.psum_scatter(
            grad_value_whole.astype(jnp.bfloat16), "blk", scatter_dimension=0, tiled=True
        ).astype(jnp.float32),
    )
    grad_query_rows = (
        jnp.transpose(grad_query_end, (2, 0, 1, 3))
        .reshape(group_rows, local_heads * HD)
        .astype(jnp.bfloat16)
    )
    grad_query_tok, grad_key_tok, grad_value_tok = (
        lax.all_to_all(grad_query_rows, "uly", split_axis=0, concat_axis=1, tiled=True),
        lax.all_to_all(
            grad_key_own.astype(jnp.bfloat16), "uly", split_axis=0, concat_axis=1, tiled=True
        ),
        lax.all_to_all(
            grad_value_own.astype(jnp.bfloat16), "uly", split_axis=0, concat_axis=1, tiled=True
        ),
    )
    back_angles = rope_angles(-token_pos)
    grad_query_plain = rotate_pairs(
        grad_query_tok.astype(jnp.float32).reshape(tok_rows, H, HD), back_angles
    ).reshape(tok_rows, H * HD)
    grad_key_plain = rotate_pairs(
        grad_key_tok.astype(jnp.float32).reshape(tok_rows, KV, HD), back_angles
    ).reshape(tok_rows, KV * HD)
    grad_qkv = jnp.concatenate(
        [grad_query_plain, grad_key_plain, grad_value_tok.astype(jnp.float32)], axis=1
    ).astype(jnp.bfloat16)
    grad_normed_attn = contract_cols(grad_qkv, qkv_full)
    qkv_term = contract_rows(normed_attn, grad_qkv)
    attn_value, attn_pull = jax.vjp(rms_scale, stream_in, attn_gain_wide)
    grad_input_norm, attn_gain_grad_full = attn_pull(grad_normed_attn)
    input_grad = grad_middle + grad_input_norm
    qkv_grad, out_weight_grad, attn_gain_grad, mlp_gain_grad = (
        lax.psum_scatter(qkv_term, ("dp", "blk", "uly"), scatter_dimension=0, tiled=True),
        lax.psum_scatter(out_weight_term, ("dp", "blk", "uly"), scatter_dimension=0, tiled=True),
        lax.psum_scatter(
            attn_gain_grad_full, ("dp", "blk", "uly"), scatter_dimension=0, tiled=True
        ),
        lax.psum_scatter(mlp_gain_grad_full, ("dp", "blk", "uly"), scatter_dimension=0, tiled=True),
    )
    return (
        final_stream.astype(jnp.bfloat16),
        input_grad,
        qkv_grad,
        out_weight_grad,
        gate_up_grad,
        down_grad,
        attn_gain_grad,
        mlp_gain_grad,
        rms_values,
    )


def solution(mesh):
    return jax.shard_map(
        per_device,
        mesh=mesh,
        in_specs=(
            P(("dp", "blk", "uly"), None),
            P("dp", None),
            P(("dp", "blk", "uly"), None),
            P(("dp", "blk", "uly"), None),
            P(("dp", "blk"), None, "uly"),
            P(("dp", "blk"), "uly"),
            P(("dp", "blk", "uly")),
            P(("dp", "blk", "uly")),
            P(("dp", "blk", "uly"), None),
        ),
        out_specs=(
            P(("dp", "blk", "uly"), None),
            P(("dp", "blk", "uly"), None),
            P(("dp", "blk", "uly"), None),
            P(("dp", "blk", "uly"), None),
            P(("dp", "blk"), None, "uly"),
            P(("dp", "blk"), "uly"),
            P(("dp", "blk", "uly")),
            P(("dp", "blk", "uly")),
            P(),
        ),
        check_vma=False,
    )
```

profile of v0, /device:TPU:0, one launch (start us, length us, event | category | flops | bytes accessed | tf_op | source)
XLA Modules:
  0.0 2767.4 jit_solution(13440144659682024762)
XLA Ops:
  10.5 42.9 %all-reduce.6 = (bf16[2048]{0:T(1024)(128)(2,1)S(1)}, bf16[2048]{0:T(1024)(128)(2,1)S(1)}) all-reduce(bf16[2048]{0:T(1024)(128)(2,1)S(1)} %dynamic-update-slice, bf16[2048]{0:T(1024)(128)(2,1)S(1)} %dynamic-update-slice.1), channel_id=1, replica_groups=mesh['dp'=4,'blk'=4,'uly'=2] {'dp','blk','uly'}, use_global_device_ids=true, to_apply=%add | all-reduce | flops 4096 | bytes 16384
  55.8 74.2 %all-gather.9.cloned.1.call-done = bf16[2048,4096]{1,0:T(8,128)(2,1)} async-done(((bf16[64,4096]{1,0:T(8,128)(2,1)}), bf16[2048,4096]{1,0:T(8,128)(2,1)}) %all-gather.9.cloned.1.call-update) | async-done | bytes 16777232 | tf_op jit(solution)/shard_map/all_gather | solution.py:93
  182.5 14.2 while.40
  211.2 51.6 %all-gather.15.cloned.1.call-done = bf16[2048,2048]{1,0:T(8,128)(2,1)} async-done(((bf16[64,2048]{1,0:T(8,128)(2,1)}), bf16[2048,2048]{1,0:T(8,128)(2,1)}) %all-gather.15.cloned.1.call-update) | async-done | bytes 8388624 | tf_op jit(solution)/shard_map/all_gather | solution.py:94
  276.6 14.2 all-gather.17.cloned.1.call-done
  290.8 170.1 %all-gather.19.cloned.1.call-done = bf16[2048,2,4096]{2,0,1:T(8,128)(2,1)} async-done(((bf16[128,2,4096]{2,0,1:T(8,128)(2,1)}), bf16[2048,2,4096]{2,0,1:T(8,128)(2,1)}) %all-gather.19.cloned.1.call-update) | async-done | bytes 33554448 | tf_op jit(solution)/shard_map/all_gather | solution.py:99
  460.9 17.8 fusion.45
  483.8 129.1 %all-gather.21.cloned.1.call-done = bf16[2048,4096]{1,0:T(8,128)(2,1)} async-done(((bf16[128,4096]{1,0:T(8,128)(2,1)}), bf16[2048,4096]{1,0:T(8,128)(2,1)}) %all-gather.21.cloned.1.call-update) | async-done | bytes 16777232 | tf_op jit(solution)/shard_map/all_gather | solution.py:100
  612.9 13.1 fusion.29
  626.0 16.7 fusion.27
  643.0 12.3 convolution_convert_fusion.1
  661.4 23.1 reduce-scatter.8.cloned.1.call-done
  712.5 33.4 %while.41 = (s32[]{:T(128)}, f32[4,2,256,128]{3,2,1,0:T(8,128)S(1)}, bf16[1024,512]{1,0:T(8,128)(2,1)}, bf16[1024,512]{1,0:T(8,128)(2,1)}, s32[1,8]{1,0:T(1,128)...) while((s32[]{:T(128)}, ...), condition=%wide.region_15.16_spmd.clone, body=%wide.region_13.15_spmd.clone.sunk | while | flops 676410624 | bytes 18242824 | solution.py:286
  746.1 16.7 convolution_convert_fusion
  762.8 42.0 %copy.210 = bf16[2048,2,4096]{0,2,1:T(8,128)(2,1)} copy(bf16[2048,2,4096]{2,0,1:T(8,128)(2,1)} %convolution_convert_fusion) | data formatting | bytes 67108864 | tf_op jit(solution)/shard_map/convert.9
  804.9 9.8 convert_bitcast_fusion
  814.7 43.5 %pad_maximum_fusion = bf16[2048,12288]{0,1:T(8,128)(2,1)} fusion(bf16[2048,4096]{0,1:T(8,128)(2,1)} %convert_bitcast_fusion, bf16[2048,8192]{0,1:T(8,128)(2,1)} %bitcast.236), kind=kLoop, calls=%fused_computation.63 | loop fusion | flops 100663296 | bytes 100663296 | tf_op jit(solution)/shard_map/concatenate | solution.py:218
  869.8 9.9 all_to_all.118
  899.1 14.3 fusion.49
  915.3 13.3 fusion.37
  932.0 41.4 %all-reduce.5 = (f32[2048]{0:T(1024)S(1)}, f32[2048]{0:T(1024)S(1)}, f32[5]{0:T(128)S(1)}) all-reduce(f32[2048]{0:T(1024)S(1)} %get-tuple-element.737, f32[2048]{0:T(1024)S(1)} %copy-done.17, f32[5]{0:T(128)S(1)} %stack.38), channel_id=9, replica_groups=mesh['dp'=4,'blk'=4,'uly'=2] {'dp','blk','uly'}, use_global_device_ids=true, to_apply=%region_23.24.clone | all-reduce | flops 4101 | bytes 32808
  977.6 713.1 %all-reduce.9.cloned.1.call-done = bf16[2048,12288]{0,1:T(8,128)(2,1)} async-done(((bf16[2048,12288]{0,1:T(8,128)(2,1)}), bf16[2048,12288]{0,1:T(8,128)(2,1)}) %all-reduce.9.cloned.1.call-update) | async-done | bytes 50331664
  1706.1 344.5 %reduce-scatter.18.cloned.1.call-done = f32[64,2048]{1,0:T(8,128)} async-done(((f32[2048,2048]{1,0:T(8,128)}), f32[64,2048]{1,0:T(8,128)}) %reduce-scatter.18.cloned.1.call-update) | async-done | bytes 524304 | tf_op jit(solution)/shard_map/reduce_scatter | solution.py:328
  2050.5 710.0 %reduce-scatter.16.cloned.1.call-done = f32[64,4096]{1,0:T(8,128)} async-done(((f32[2048,4096]{1,0:T(8,128)}), f32[64,4096]{1,0:T(8,128)}) %reduce-scatter.16.cloned.1.call-update) | async-done | bytes 1048592 | tf_op jit(solution)/shard_map/reduce_scatter | solution.py:327
  (282 shorter events, 227.5 us)
Async XLA Ops:
  7.2 122.8 %all-gather.9.cloned.1.call-start = ((), (), s32[]{:S(2)}) async-start(), calls=%async_computation.14 | async-start | bytes 17301504 | tf_op jit(solution)/shard_map/all_gather | solution.py:93
  7.9 162.9 %all-gather.11.cloned.1.call-start = ((), (), s32[]{:S(2)}) async-start(), calls=%async_computation.15 | async-start | bytes 1310720 | tf_op jit(solution)/shard_map/all_gather | solution.py:124
  53.4 85.0 %copy-start.12 = (f32[2048]{0:T(1024)}, f32[2048]{0:T(1024)S(1)}, u32[]{:S(2)}) copy-start(f32[2048]{0:T(1024)S(1)} %convert_element_type.161) | copy-start | bytes 24580
  55.8 82.6 %copy-start.20 = (f32[128]{0:T(128)}, f32[128]{0:T(128)S(1)}, u32[]{:S(2)}) copy-start(f32[128]{0:T(128)S(1)} %fusion.33) | copy-start | bytes 1540
  55.8 82.6 %copy-start.18 = (f32[128]{0:T(128)}, f32[128]{0:T(128)S(1)}, u32[]{:S(2)}) copy-start(f32[128]{0:T(128)S(1)} %fusion.60) | copy-start | bytes 1540
  148.4 34.1 %all-gather.13.cloned.1.call-start = ((), (), s32[]{:S(2)}) async-start(), calls=%async_computation.16 | async-start | bytes 1310720 | tf_op jit(solution)/shard_map/all_gather | solution.py:125
  156.9 105.9 %all-gather.15.cloned.1.call-start = ((), (), s32[]{:S(2)}) async-start(), calls=%async_computation.17 | async-start | bytes 8650752 | tf_op jit(solution)/shard_map/all_gather | solution.py:94
  159.9 10.2 all-to-all-start.1
  196.7 66.1 %copy-start.3 = (bf16[128,2048]{1,0:T(8,128)(2,1)S(1)}, bf16[128,2048]{1,0:T(8,128)(2,1)}, u32[]{:S(2)}) copy-start(bf16[128,2048]{1,0:T(8,128)(2,1)} %param.13) | copy-start | bytes 1572868
  198.8 12.2 all-to-all-start.3
  202.3 88.6 %all-gather.17.cloned.1.call-start = ((), (), s32[]{:S(2)}) async-start(), calls=%async_computation.18 | async-start | bytes 1572864 | tf_op jit(solution)/shard_map/all_gather | solution.py:177
  270.8 190.1 %all-gather.19.cloned.1.call-start = ((), (), s32[]{:S(2)}) async-start(), calls=%async_computation.19 | async-start | bytes 35651584 | tf_op jit(solution)/shard_map/all_gather | solution.py:99
  275.1 208.7 %all-gather.23.cloned.1.call-start = ((), (), s32[]{:S(2)}) async-start(), calls=%async_computation.22 | async-start | bytes 1572864 | tf_op jit(solution)/shard_map/all_gather | solution.py:178
  275.8 337.0 %all-gather.21.cloned.1.call-start = ((), (), s32[]{:S(2)}) async-start(), calls=%async_computation.20 | async-start | bytes 17825792 | tf_op jit(solution)/shard_map/all_gather | solution.py:100
  276.6 384.8 %reduce-scatter.10.cloned.1.call-start = ((), (), s32[]{:S(2)}) async-start(), calls=%async_computation.23 | async-start | bytes 1572864 | tf_op jit(solution)/shard_map/reduce_scatter | solution.py:211
  642.7 41.8 %reduce-scatter.8.cloned.1.call-start = ((), (), s32[]{:S(2)}) async-start(), calls=%async_computation.21 | async-start | bytes 1572864 | tf_op jit(solution)/shard_map/reduce_scatter | solution.py:187
  695.1 11.7 all-to-all-start.4
  698.6 181.1 %reduce-scatter.14.cloned.1.call-start = ((), (), s32[]{:S(2)}) async-start(), calls=%async_computation.25 | async-start | bytes 1310720 | tf_op jit(solution)/shard_map/reduce_scatter | solution.py:293
  745.9 140.1 %reduce-scatter.12.cloned.1.call-start = ((), (), s32[]{:S(2)}) async-start(), calls=%async_computation.24 | async-start | bytes 1310720 | tf_op jit(solution)/shard_map/reduce_scatter | solution.py:290
  814.7 876.0 %all-reduce.9.cloned.1.call-start = ((), (), s32[]{:S(2)}) async-start(), calls=%async_computation.28 | async-start | bytes 100663296
  858.3 1192.2 %reduce-scatter.18.cloned.1.call-start = ((), (), s32[]{:S(2)}) async-start(), calls=%async_computation.27 | async-start | bytes 17301504 | tf_op jit(solution)/shard_map/reduce_scatter | solution.py:328
  879.8 8.6 all-to-all-start.7
  888.4 9.4 all-to-all-start.6
  892.5 1868.0 %reduce-scatter.16.cloned.1.call-start = ((), (), s32[]{:S(2)}) async-start(), calls=%async_computation.26 | async-start | bytes 34603008 | tf_op jit(solution)/shard_map/reduce_scatter | solution.py:327
  (20 other events, 369.5 us)
Sparse Core Ops, SparseCore 0:
  11.0 118.9 all-gather.8
  148.5 14.8 all-gather.10
  165.6 16.8 all-gather.12
  185.3 77.3 all-gather.14
  270.9 19.8 all-gather.16
  292.8 168.0 all-gather.18
  462.4 21.2 all-gather.22
  485.9 126.8 all-gather.20
  642.8 18.4 reduce-scatter.9
  664.1 20.3 reduce-scatter.7
  746.0 24.8 reduce-scatter.13
  814.8 24.9 reduce-scatter.11
  858.4 832.2 all-reduce.8
  1693.4 357.0 reduce-scatter.17
  2053.2 707.1 reduce-scatter.15
where the time goes:
time: 2780 us; the launch traced here: 2770 us
  waiting for transfers between devices  2280 us (82%)
  matrix products  170 us (6%)
  blocking collectives  110 us (4%)
  local copies, waits for them, and re-layouts  103 us (4%)
  other arithmetic  66.1 us (2%)
    unnamed x16, waiting for transfers between devices  716 us
    reduce_scatter x1, waiting for transfers between devices, per_device(): lax.psum_scatter(qkv_term, ('dp', 'blk', 'uly'), scatter_dimension=0, til...  710 us
    reduce_scatter x1, waiting for transfers between devices, per_device(): lax.psum_scatter(out_weight_term, ('dp', 'blk', 'uly'), scatter_dimension...  344 us
    all_gather x1, waiting for transfers between devices, per_device(): lax.all_gather(gate_up_weight, ('dp', 'blk'), axis=0, tiled=True)  170 us
    all_gather x1, waiting for transfers between devices, per_device(): lax.all_gather(down_weight, ('dp', 'blk'), axis=0, tiled=True)  129 us
    unnamed x2, blocking collectives  84.3 us
    all_gather x1, waiting for transfers between devices, per_device(): lax.all_gather(qkv_weight, ('dp', 'blk', 'uly'), axis=0, tiled=True)  74.2 us
  transfers between devices with their start and end apart: 20, of which 17 were waited for; matrix products, arithmetic and copies ran while one was open for 9% of the time, Pallas kernels for 0%

commit v1 on v0

--- a/solution.py
+++ b/solution.py
@@ -1,6 +1,7 @@
 import jax
 import jax.numpy as jnp
 from jax import lax
+from jax.sharding import Mesh
 from jax.sharding import PartitionSpec as P
 
 D = 2048
@@ -55,7 +56,7 @@
     )
 
 
-def per_device(
+def general_plan(
     layer_input,
     span_order,
     qkv_weight,
@@ -344,30 +345,273 @@
     )
 
 
+ALL_AXES = ("dp", "yy", "cc", "uly")
+SIDE_AXES = ("yy", "uly")
+SWAP = [(0, 1), (1, 0)]
+
+
+def unit_scale(values):
+    return lax.rsqrt(jnp.mean(values * values, axis=-1, keepdims=True) + EPSILON)
+
+
+def norm_pull(values, scale, grad_scaled):
+    return scale * grad_scaled - values * scale**3 * jnp.mean(
+        grad_scaled * values, axis=-1, keepdims=True
+    )
+
+
+def exchange(values, axes):
+    return lax.all_to_all(values, axes, split_axis=0, concat_axis=0, tiled=True)
+
+
+def gather_rows(rows, axis_names):
+    group = lax.axis_size(axis_names)
+    copies = jnp.broadcast_to(rows[None], (group, *rows.shape)).reshape(-1, rows.shape[1])
+    own = exchange(copies, axis_names)
+    other = lax.ppermute(own, "cc", SWAP)
+    return jnp.concatenate([own, other], axis=0)
+
+
+def scatter_sum(partial, axis_names):
+    group = lax.axis_size(axis_names)
+    half = partial.shape[0] // 2
+    arrived = lax.ppermute(partial[half:].astype(jnp.bfloat16), "cc", SWAP)
+    mine = (partial[:half].astype(jnp.float32) + arrived.astype(jnp.float32)).astype(jnp.bfloat16)
+    parts = exchange(mine, axis_names).reshape(group, half // group, -1)
+    return jnp.sum(parts.astype(jnp.float32), axis=0)
+
+
+def plane_plan(
+    layer_input,
+    span_order,
+    qkv_weight,
+    out_weight,
+    gate_up_weight,
+    down_weight,
+    attn_gain,
+    mlp_gain,
+    output_cotangent,
+):
+    tok = layer_input.shape[0]
+    nz = lax.axis_size("dp")
+    ndev = lax.axis_size(ALL_AXES)
+    plane = ndev // nz
+    seq_rows = tok * plane
+    span_size = seq_rows // span_order.shape[1]
+    y_at, c_at, x_at = lax.axis_index("yy"), lax.axis_index("cc"), lax.axis_index("uly")
+    group = H // KV
+    q_cols, kv_cols = H * HD // plane, KV * HD // plane
+    own_cols = q_cols + 2 * kv_cols
+    d_rows = qkv_weight.shape[0]
+    score_scale = HD ** (-0.5)
+
+    gain_a = attn_gain.astype(jnp.float32)[:, None]
+    folded = (qkv_weight.astype(jnp.float32) * gain_a).astype(jnp.bfloat16)
+    cuts = [H * HD, (H + KV) * HD]
+    by_group = jnp.concatenate(
+        [part.reshape(d_rows, plane, -1) for part in jnp.split(folded, cuts, axis=1)], axis=2
+    ).transpose(1, 0, 2)
+    wq = exchange(
+        jnp.broadcast_to(by_group[None], (nz, plane, d_rows, own_cols)).reshape(-1, own_cols),
+        ALL_AXES,
+    )
+    out_by_group = out_weight.reshape(d_rows, plane, q_cols).transpose(1, 0, 2)
+    wo = exchange(
+        jnp.broadcast_to(out_by_group[None], (nz, plane, d_rows, q_cols)).reshape(-1, q_cols),
+        ALL_AXES,
+    )
+
+    stream_in = layer_input.astype(jnp.float32)
+    scale_a = unit_scale(stream_in)
+    normed_all = gather_rows((stream_in * scale_a).astype(jnp.bfloat16), SIDE_AXES)
+
+    mlp_rows, ff_local = down_weight.shape
+    hgroups = nz * lax.axis_size("cc")
+    hchunk = ff_local // hgroups
+    gain_own = mlp_gain.astype(jnp.float32)[None, :]
+    gain_peer = lax.ppermute(mlp_gain[None, :], "uly", SWAP).astype(jnp.float32)
+    gain_m = jnp.where(
+        x_at == 0,
+        jnp.concatenate([gain_own, gain_peer], axis=1),
+        jnp.concatenate([gain_peer, gain_own], axis=1),
+    ).reshape(mlp_rows, 1)
+    folded_gu = (gate_up_weight.astype(jnp.float32) * gain_m[:, :, None]).astype(jnp.bfloat16)
+    mlp_w = jnp.concatenate([folded_gu, down_weight[:, None, :]], axis=1)
+    mlp_w = mlp_w.reshape(mlp_rows, 3, hgroups, hchunk).transpose(2, 0, 1, 3)
+    mlp_w = exchange(mlp_w.reshape(hgroups * mlp_rows, 3 * hchunk), ("dp", "cc"))
+    mlp_w = lax.all_gather(mlp_w, SIDE_AXES, axis=0, tiled=True)
+    half_d = hgroups * mlp_rows
+    mlp_w = mlp_w.reshape(2, 2, half_d, 3, hchunk).transpose(3, 0, 2, 1, 4)
+    mlp_w = mlp_w.reshape(3, 2 * half_d, 2 * hchunk)
+
+    def to_split(rows):
+        return rows.reshape(tok, nz, 2, 2, mlp_rows).transpose(0, 2, 1, 3, 4).reshape(tok, D)
+
+    def from_split(rows):
+        return rows.reshape(tok, 2, nz, 2, mlp_rows).transpose(0, 2, 1, 3, 4).reshape(tok, D)
+
+    cot_all = gather_rows(to_split(output_cotangent), ("dp",))
+
+    block = jnp.arange(plane, dtype=jnp.int32)
+    core_of, y_of, x_of = (block // 4) ^ c_at, (block // 2) % 2, block % 2
+    stored = (y_of * 2 + core_of) * 2 + x_of
+    row_at = (stored[:, None] * tok + jnp.arange(tok, dtype=jnp.int32)[None, :]).reshape(-1)
+    positions = sequence_positions(row_at, span_size, span_order[0])
+    angles = rope_angles(positions)
+    allowed = (positions[None, :] <= positions[:, None])[None]
+
+    qkv = jnp.dot(normed_all, wq, preferred_element_type=jnp.float32)
+    query = rotate_pairs(qkv[:, :q_cols].reshape(seq_rows, group, HD), angles).astype(jnp.bfloat16)
+    key = rotate_pairs(qkv[:, None, q_cols : q_cols + kv_cols], angles)[:, 0].astype(jnp.bfloat16)
+    value = qkv[:, q_cols + kv_cols :].astype(jnp.bfloat16)
+
+    scores = jnp.einsum("rgd,pd->grp", query, key, preferred_element_type=jnp.float32) * score_scale
+    scores = jnp.where(allowed, scores, MASKED)
+    top = jnp.max(scores, axis=-1, keepdims=True)
+    weights = jnp.where(allowed, jnp.exp(scores - top), 0.0)
+    total = jnp.sum(weights, axis=-1, keepdims=True)
+    probs = weights / total
+    probs_low = probs.astype(jnp.bfloat16)
+    heads_f = jnp.einsum("grp,pd->rgd", probs_low, value, preferred_element_type=jnp.float32)
+    heads = heads_f.reshape(seq_rows, q_cols).astype(jnp.bfloat16)
+    attn_out = scatter_sum(contract_cols(heads, wo), SIDE_AXES)
+
+    middle = stream_in + attn_out
+    scale_m = unit_scale(middle)
+    zhat_all = gather_rows(to_split((middle * scale_m).astype(jnp.bfloat16)), ("dp",))
+    gate = jnp.dot(zhat_all, mlp_w[0], preferred_element_type=jnp.float32)
+    up = jnp.dot(zhat_all, mlp_w[1], preferred_element_type=jnp.float32)
+    grad_hidden = jnp.dot(cot_all, mlp_w[2], preferred_element_type=jnp.float32)
+    sig = jax.nn.sigmoid(gate)
+    hidden = (gate * sig * up).astype(jnp.bfloat16)
+    grad_gate = (grad_hidden * up * sig * (1.0 + gate * (1.0 - sig))).astype(jnp.bfloat16)
+    grad_up = (grad_hidden * gate * sig).astype(jnp.bfloat16)
+    grad_zhat = from_split(
+        scatter_sum(contract_cols(grad_gate, mlp_w[0]) + contract_cols(grad_up, mlp_w[1]), ("dp",))
+    )
+    mlp_out = from_split(scatter_sum(contract_cols(hidden, mlp_w[2]), ("dp",)))
+    final_stream = middle + mlp_out
+
+    terms = jnp.stack(
+        [
+            contract_rows(zhat_all, grad_gate),
+            contract_rows(zhat_all, grad_up),
+            contract_rows(cot_all, hidden),
+        ]
+    ).astype(jnp.bfloat16)
+    terms = terms.reshape(3, 2, half_d, 2, hchunk).transpose(1, 3, 2, 0, 4)
+    terms = exchange(terms.reshape(4 * half_d, 3 * hchunk), SIDE_AXES)
+    terms = jnp.sum(terms.reshape(4, half_d, 3 * hchunk).astype(jnp.float32), axis=0)
+    terms = exchange(terms.astype(jnp.bfloat16), ("dp", "cc"))
+    terms = terms.reshape(hgroups, mlp_rows, 3, hchunk).transpose(1, 2, 0, 3).astype(jnp.float32)
+    terms = terms.reshape(mlp_rows, 3, ff_local)
+    gate_up_grad = terms[:, :2] * gain_m[:, :, None]
+    down_grad = terms[:, 2]
+    gain_sum = jnp.sum(terms[:, :2] * gate_up_weight.astype(jnp.float32), axis=(1, 2))
+    gain_halves = gain_sum.reshape(2, -1)
+    gain_keep = jnp.where(x_at == 0, gain_halves[0], gain_halves[1])
+    gain_send = jnp.where(x_at == 0, gain_halves[1], gain_halves[0])
+    mlp_gain_grad = gain_keep + lax.ppermute(gain_send[None, :], "uly", SWAP)[0]
+
+    cot = output_cotangent.astype(jnp.float32)
+    grad_middle = cot + norm_pull(middle, scale_m, grad_zhat)
+    grad_out_all = gather_rows(grad_middle.astype(jnp.bfloat16), SIDE_AXES)
+    grad_heads = jnp.dot(grad_out_all, wo, preferred_element_type=jnp.float32).astype(jnp.bfloat16)
+    out_term = contract_rows(grad_out_all, heads)
+    grad_four = grad_heads.reshape(seq_rows, group, HD)
+    row_delta = jnp.sum(grad_four.astype(jnp.float32) * heads_f, axis=-1).T
+    grad_probs = jnp.einsum("rgd,pd->grp", grad_four, value, preferred_element_type=jnp.float32)
+    grad_scores = (probs * (grad_probs - row_delta[..., None])).astype(jnp.bfloat16)
+    grad_query = (
+        jnp.einsum("grp,pd->rgd", grad_scores, key, preferred_element_type=jnp.float32)
+        * score_scale
+    )
+    grad_key = (
+        jnp.einsum("grp,rgd->pd", grad_scores, query, preferred_element_type=jnp.float32)
+        * score_scale
+    )
+    grad_value = jnp.einsum("grp,rgd->pd", probs_low, grad_four, preferred_element_type=jnp.float32)
+    grad_query, grad_key = (v.astype(jnp.bfloat16).astype(jnp.float32) for v in (grad_query, grad_key))
+    grad_qkv = jnp.concatenate(
+        [
+            rotate_pairs(grad_query, -angles).reshape(seq_rows, q_cols),
+            rotate_pairs(grad_key[:, None], -angles)[:, 0],
+            grad_value,
+        ],
+        axis=1,
+    ).astype(jnp.bfloat16)
+    grad_xhat = scatter_sum(contract_cols(grad_qkv, wq), SIDE_AXES)
+    input_grad = grad_middle + norm_pull(stream_in, scale_a, grad_xhat)
+    qkv_term = contract_rows(normed_all, grad_qkv)
+
+    qkv_sum = exchange(qkv_term.astype(jnp.bfloat16), ALL_AXES)
+    qkv_sum = jnp.sum(qkv_sum.reshape(nz, plane, d_rows, own_cols).astype(jnp.float32), axis=0)
+    qkv_sum = qkv_sum.transpose(1, 0, 2)
+    qkv_sum = jnp.concatenate(
+        [
+            qkv_sum[:, :, :q_cols].reshape(d_rows, -1),
+            qkv_sum[:, :, q_cols : q_cols + kv_cols].reshape(d_rows, -1),
+            qkv_sum[:, :, q_cols + kv_cols :].reshape(d_rows, -1),
+        ],
+        axis=1,
+    )
+    qkv_grad = qkv_sum * gain_a
+    attn_gain_grad = jnp.sum(qkv_sum * qkv_weight.astype(jnp.float32), axis=1)
+    out_sum = exchange(out_term.astype(jnp.bfloat16), ALL_AXES)
+    out_sum = jnp.sum(out_sum.reshape(nz, plane, d_rows, q_cols).astype(jnp.float32), axis=0)
+    out_weight_grad = out_sum.transpose(1, 0, 2).reshape(d_rows, -1)
+
+    squares = jnp.stack(
+        [jnp.sum(v * v) for v in (stream_in, attn_out, middle, mlp_out, final_stream)]
+    )
+    lanes = jnp.zeros((1, 128), jnp.float32).at[0, :5].set(squares)
+    gathered = exchange(jnp.broadcast_to(lanes, (ndev, 128)), ALL_AXES)
+    rms_values = jnp.sqrt(jnp.sum(gathered, axis=0)[:5] / (tok * ndev * D))
+    return (
+        final_stream.astype(jnp.bfloat16),
+        input_grad,
+        qkv_grad,
+        out_weight_grad,
+        gate_up_grad,
+        down_grad,
+        attn_gain_grad,
+        mlp_gain_grad,
+        rms_values,
+    )
+
+
 def solution(mesh):
+    sizes = dict(mesh.shape)
+    if sizes["blk"] == 4 and sizes["uly"] == 2:
+        mesh = Mesh(mesh.devices.reshape(sizes["dp"], 2, 2, 2), ALL_AXES)
+        body, blk = plane_plan, ("yy", "cc")
+    else:
+        body, blk = general_plan, ("blk",)
+    every = ("dp", *blk, "uly")
+    rows = ("dp", *blk)
     return jax.shard_map(
-        per_device,
+        body,
         mesh=mesh,
         in_specs=(
-            P(("dp", "blk", "uly"), None),
+            P(every, None),
             P("dp", None),
-            P(("dp", "blk", "uly"), None),
-            P(("dp", "blk", "uly"), None),
-            P(("dp", "blk"), None, "uly"),
-            P(("dp", "blk"), "uly"),
-            P(("dp", "blk", "uly")),
-            P(("dp", "blk", "uly")),
-            P(("dp", "blk", "uly"), None),
+            P(every, None),
+            P(every, None),
+            P(rows, None, "uly"),
+            P(rows, "uly"),
+            P(every),
+            P(every),
+            P(every, None),
         ),
         out_specs=(
-            P(("dp", "blk", "uly"), None),
-            P(("dp", "blk", "uly"), None),
-            P(("dp", "blk", "uly"), None),
-            P(("dp", "blk", "uly"), None),
-            P(("dp", "blk"), None, "uly"),
-            P(("dp", "blk"), "uly"),
-            P(("dp", "blk", "uly")),
-            P(("dp", "blk", "uly")),
+            P(every, None),
+            P(every, None),
+            P(every, None),
+            P(every, None),
+            P(rows, None, "uly"),
+            P(rows, "uly"),
+            P(every),
+            P(every),
             P(),
         ),
         check_vma=False,

time: 2780 us -> 1100 us (0.40)
  waiting for transfers between devices: 2280 us -> 516 us
  local copies, waits for them, and re-layouts: 103 us -> 241 us
  blocking collectives: 110 us -> 52.3 us
  starting transfers between devices: 19.7 us -> 73.9 us
  matrix products: 170 us -> 121 us
    reduce_scatter x6 -> x0, waiting for transfers between devices: 1080 us -> none  [the longest x1 710 us: per_device(): lax.psum_scatter(qkv_term, ('dp', 'blk', 'uly'), scatter_dimension=0, til...]
    unnamed x16 -> x1, waiting for transfers between devices: 716 us -> 0.02 us
    all_gather x8 -> x1, waiting for transfers between devices: 454 us -> 0.01 us  [plane_plan(): mlp_w = lax.all_gather(mlp_w, SIDE_AXES, axis=0, tiled=True)]
    all_to_all x5 -> x15, waiting for transfers between devices: 28.6 us -> 479 us  [exchange(): return lax.all_to_all(values, axes, split_axis=0, concat_axis=0, tiled=True)]
    unnamed x2 -> x0, blocking collectives: 84.3 us -> none
    slice x4 -> x10, local copies, waits for them, and re-layouts: 2.51 us -> 60.9 us  [the longest x2 27.3 us: plane_plan(): mlp_out = from_split(scatter_sum(contract_cols(hidden, mlp_w[2]), ('dp',)))]
    dot_general x34 -> x10, matrix products: 104 us -> 48.7 us  [the longest x1 10.1 us: plane_plan(): grad_hidden = jnp.dot(cot_all, mlp_w[2], preferred_element_type=jnp.float32)]
    all_to_all x5 -> x15, starting transfers between devices: 18 us -> 69 us  [exchange(): return lax.all_to_all(values, axes, split_axis=0, concat_axis=0, tiled=True)]
  transfers between devices with their start and end apart: 20 -> 26, of which waited for: 17 -> 17; matrix products, arithmetic and copies ran while one was open for 9% -> 34% of each run, Pallas kernels for 0% -> 0%
where the time goes in v1:
time: 1100 us; the launch traced here: 1090 us
  waiting for transfers between devices  516 us (47%)
  local copies, waits for them, and re-layouts  241 us (22%)
  matrix products  121 us (11%)
  other arithmetic  74 us (7%)
  starting transfers between devices  73.9 us (7%)
  blocking collectives  52.3 us (5%)
  between operations  15.7 us (1%)
    all_to_all x15, waiting for transfers between devices, exchange(): return lax.all_to_all(values, axes, split_axis=0, concat_axis=0, tiled=True)  479 us
    all_to_all x15, starting transfers between devices, exchange(): return lax.all_to_all(values, axes, split_axis=0, concat_axis=0, tiled=True)  69 us
    another operation x6, local copies, waits for them, and re-layouts, plane_plan(): jnp.stack([contract_rows(zhat_all, grad_gate), contract_rows(zhat_all, gr...  57.2 us
    all_to_all x1, blocking collectives, exchange(): return lax.all_to_all(values, axes, split_axis=0, concat_axis=0, tiled=True)  52.3 us
    unnamed x121, local copies, waits for them, and re-layouts  39 us
    dot_general x5, matrix products, contract_rows(): lax.dot_general(left_side, right_side, (((0,), (0,)), ((), ())), preferre...  38.2 us
    slice x2, local copies, waits for them, and re-layouts, plane_plan(): mlp_out = from_split(scatter_sum(contract_cols(hidden, mlp_w[2]), ('dp',)))  27.3 us
    dot_general x5, matrix products, contract_cols(): lax.dot_general(left_side, right_side, (((1,), (1,)), ((), ())), preferre...  26.2 us
  transfers between devices with their start and end apart: 26, of which 17 were waited for; matrix products, arithmetic and copies ran while one was open for 34% of the time, Pallas kernels for 0%

profile of v1, /device:TPU:0, one launch (start us, length us, event | category | flops | bytes accessed | tf_op | source)
XLA Modules:
  0.0 1093.6 jit_solution(4018514293657377361)
XLA Ops:
  26.9 16.2 %collective-permute-done.3 = bf16[1,64]{1,0:T(2,128)(2,1)S(1)} collective-permute-done((bf16[1,64]{1,0:T(2,128)(2,1)S(1)}, bf16[1,64]{1,0:T(2,128)(2,1)S(1)}, u32[]{:S(2)}, u32[]{:S(2)}) %collective-permute-start.3) | collective-permute-done | bytes 160 | tf_op jit(solution)/shard_map/ppermute | solution.py:432
  53.8 69.1 %all-to-all-done.5 = bf16[8,128,1536]{1,2,0:T(8,128)(2,1)S(1)} async-done(((bf16[8,128,1536]{1,2,0:T(8,128)(2,1)}), bf16[8,128,1536]{1,2,0:T(8,128)(2,1)S(1)}, u32[]{:S(2)}, u32[]{:S(2)}) %all-to-all-start.5) | async-done | bytes 3145760 | tf_op jit(solution)/shard_map/all_to_all | solution.py:364
  138.7 39.0 %all-to-all-done.1 = bf16[32,64,512]{2,1,0:T(8,128)(2,1)} async-done(((bf16[32,64,512]{2,1,0:T(8,128)(2,1)}), bf16[32,64,512]{2,1,0:T(8,128)(2,1)}, u32[]{:S(2)}, u32[]{:S(2)}) %all-to-all-start.1) | async-done | bytes 2097184 | tf_op jit(solution)/shard_map/all_to_all | solution.py:364
  219.8 52.3 %all_to_all.150 = bf16[4,128,2048]{2,1,0:T(8,128)(2,1)S(1)} all-to-all(bf16[4,128,2048]{2,1,0:T(8,128)(2,1)S(1)} %bitcast.259), channel_id=1, replica_groups=mesh['dp'=4,'yy'=2,'cc'=2,'uly'=2] {'yy','uly'}, dimensions={0} | all-to-all | bytes 4194304 | tf_op jit(solution)/shard_map/all_to_all | solution.py:364
  281.2 47.1 %all-to-all-done.4 = bf16[4,128,2048]{2,1,0:T(8,128)(2,1)} async-done(((bf16[4,128,2048]{2,1,0:T(8,128)(2,1)}), bf16[4,128,2048]{2,1,0:T(8,128)(2,1)}, u32[]{:S(2)}, u32[]{:S(2)}) %all-to-all-start.4) | async-done | bytes 2097184 | tf_op jit(solution)/shard_map/all_to_all | solution.py:364
  333.7 47.6 %all-to-all-done.7 = bf16[4,128,2048]{2,1,0:T(8,128)(2,1)S(1)} async-done(((bf16[4,128,2048]{2,1,0:T(8,128)(2,1)}), bf16[4,128,2048]{2,1,0:T(8,128)(2,1)S(1)}, u32[]{:S(2)}, u32[]{:S(2)}) %all-to-all-start.7) | async-done | bytes 2097184 | tf_op jit(solution)/shard_map/all_to_all | solution.py:364
  381.3 17.4 %copy.301 = bf16[4096,1536]{0,1:T(8,128)(2,1)} copy(bf16[4096,1536]{1,0:T(8,128)(2,1)} %all-gather.2.cloned.1.call-done) | data formatting | bytes 25165824 | tf_op jit(solution)/shard_map/all_gather | solution.py:442
  398.7 21.1 %reshape.715 = bf16[2,2,1024,3,512]{2,1,0,4,3:T(2,128)(2,1)} reshape(bf16[4096,1536]{0,1:T(8,128)(2,1)} %copy.301) | data formatting | bytes 25165824 | tf_op jit(solution)/shard_map/reshape | solution.py:444
  419.8 11.2 %fusion.98 = (bf16[1,2,1024,2,512]{2,3,1,4,0:T(2,128)(2,1)}, bf16[1,2,1024,2,512]{2,3,1,4,0:T(2,128)(2,1)}, bf16[1,2,1024,2,512]{2,3,1,4,0:T(2,128)(2,1)}) fusion(bf16[3,2,1024,2,512]{2,3,1,4,0:T(2,128)(2,1)} %bitcast.243), kind=kLoop, calls=%fused_computation.214 | loop fusion | bytes 25165824 | tf_op jit(solution)/shard_map/slice | solution.py:492
  431.0 16.1 %copy.303 = bf16[1,2,1024,2,512]{4,3,2,1,0:T(2,128)(2,1)} copy(bf16[1,2,1024,2,512]{2,3,1,4,0:T(2,128)(2,1)} %get-tuple-element.105) | data formatting | bytes 8388608 | tf_op jit(solution)/shard_map/slice | solution.py:483
  452.5 16.1 %copy.302 = bf16[1,2,1024,2,512]{4,3,2,1,0:T(2,128)(2,1)} copy(bf16[1,2,1024,2,512]{2,3,1,4,0:T(2,128)(2,1)} %get-tuple-element.106) | data formatting | bytes 8388608 | tf_op jit(solution)/shard_map/slice | solution.py:482
  473.9 16.1 %copy.304 = bf16[1,2,1024,2,512]{4,3,2,1,0:T(2,128)(2,1)} copy(bf16[1,2,1024,2,512]{2,3,1,4,0:T(2,128)(2,1)} %get-tuple-element.104) | data formatting | bytes 8388608 | tf_op jit(solution)/shard_map/slice | solution.py:492
  511.7 10.1 multiply_convert_fusion
  559.7 35.1 %all-to-all-done.8 = bf16[4,128,2048]{2,1,0:T(8,128)(2,1)S(1)} async-done(((bf16[4,128,2048]{2,1,0:T(8,128)(2,1)}), bf16[4,128,2048]{2,1,0:T(8,128)(2,1)S(1)}, u32[]{:S(2)}, u32[]{:S(2)}) %all-to-all-start.8) | async-done | bytes 2097184 | tf_op jit(solution)/shard_map/all_to_all | solution.py:364
  616.9 11.2 %copy.325 = bf16[1,2,1024,2,512]{2,4,0,3,1:T(8,128)(2,1)} copy(bf16[1,2,1024,2,512]{4,3,2,1,0:T(2,128)(2,1)} %stack.30) | data formatting | bytes 8388608 | tf_op jit(solution)/shard_map/stack | solution.py:495
  645.4 11.3 %copy.326 = bf16[1,2,1024,2,512]{2,4,0,3,1:T(8,128)(2,1)} copy(bf16[1,2,1024,2,512]{4,3,2,1,0:T(2,128)(2,1)} %stack.31) | data formatting | bytes 8388608 | tf_op jit(solution)/shard_map/stack | solution.py:495
  696.3 11.1 %copy.327 = bf16[1,2,1024,2,512]{2,4,0,3,1:T(8,128)(2,1)} copy(bf16[1,2,1024,2,512]{4,3,2,1,0:T(2,128)(2,1)} %stack.32) | data formatting | bytes 8388608 | tf_op jit(solution)/shard_map/stack | solution.py:495
  707.4 10.5 pad_maximum_fusion
  755.7 106.0 %all-to-all-done.13 = bf16[4,1024,1536]{1,2,0:T(8,128)(2,1)} async-done(((bf16[4,1024,1536]{1,2,0:T(8,128)(2,1)}), bf16[4,1024,1536]{1,2,0:T(8,128)(2,1)}, u32[]{:S(2)}, u32[]{:S(2)}) %all-to-all-start.13) | async-done | bytes 12582944 | tf_op jit(solution)/shard_map/all_to_all | solution.py:364
  870.6 19.8 %all-to-all-done.10 = bf16[4,128,2048]{2,1,0:T(8,128)(2,1)} async-done(((bf16[4,128,2048]{2,1,0:T(8,128)(2,1)}), bf16[4,128,2048]{2,1,0:T(8,128)(2,1)}, u32[]{:S(2)}, u32[]{:S(2)}) %all-to-all-start.10) | async-done | bytes 2097184 | tf_op jit(solution)/shard_map/all_to_all | solution.py:364
  904.2 17.6 %all-to-all-done.12 = bf16[32,64,256]{2,1,0:T(8,128)(2,1)} async-done(((bf16[32,64,256]{2,1,0:T(8,128)(2,1)}), bf16[32,64,256]{2,1,0:T(8,128)(2,1)}, u32[]{:S(2)}, u32[]{:S(2)}) %all-to-all-start.12) | async-done | bytes 1048608 | tf_op jit(solution)/shard_map/all_to_all | solution.py:364
  938.0 10.5 reduce_sum.214
  953.2 33.5 %all-to-all-done.11 = bf16[32,64,512]{2,1,0:T(8,128)(2,1)} async-done(((bf16[32,64,512]{2,1,0:T(8,128)(2,1)}), bf16[32,64,512]{2,1,0:T(8,128)(2,1)}, u32[]{:S(2)}, u32[]{:S(2)}) %all-to-all-start.11) | async-done | bytes 2097184 | tf_op jit(solution)/shard_map/all_to_all | solution.py:364
  1000.0 63.1 %all-to-all-done.14 = bf16[8,128,1536]{2,1,0:T(8,128)(2,1)} async-done(((bf16[8,128,1536]{2,1,0:T(8,128)(2,1)}), bf16[8,128,1536]{2,1,0:T(8,128)(2,1)}, u32[]{:S(2)}, u32[]{:S(2)}) %all-to-all-start.14) | async-done | bytes 3145760 | tf_op jit(solution)/shard_map/all_to_all | solution.py:364
  (280 shorter events, 368.6 us)
Async XLA Ops:
  12.3 33.8 %all-to-all-start = ((bf16[4,128,2048]{2,1,0:T(8,128)(2,1)}), bf16[4,128,2048]{2,1,0:T(8,128)(2,1)}, u32[]{:S(2)}, u32[]{:S(2)}) async-start(bf16[4,128,2048]{2,1,0:T(8,128)(2,1)} %broadcast_in_dim.63), calls=%async_computation | async-start | bytes 4194304 | tf_op jit(solution)/shard_map/all_to_all | solution.py:364
  17.5 25.7 %collective-permute-start.3 = (bf16[1,64]{1,0:T(2,128)(2,1)S(1)}, bf16[1,64]{1,0:T(2,128)(2,1)S(1)}, u32[]{:S(2)}, u32[]{:S(2)}) collective-permute-start(bf16[1,64]{1,0:T(2,128)(2,1)S(1)} %bitcast.298), channel_id=1, source_target_pairs={{0,1},{1,0},{2,3},{3,2},{4,5},{5,4},{6,7},{7,6},{8,9},{9,8},{10,11... | collective-permute-start | bytes 392 | tf_op jit(solution)/shard_map/ppermute | solution.py:432
  46.1 76.8 %all-to-all-start.5 = ((bf16[8,128,1536]{1,2,0:T(8,128)(2,1)}), bf16[8,128,1536]{1,2,0:T(8,128)(2,1)S(1)}, u32[]{:S(2)}, u32[]{:S(2)}) async-start(bf16[8,128,1536]{1,2,0:T(8,128)(2,1)} %bitcast.252), calls=%async_computation.5 | async-start | bytes 6291456 | tf_op jit(solution)/shard_map/all_to_all | solution.py:364
  125.5 52.2 %all-to-all-start.1 = ((bf16[32,64,512]{2,1,0:T(8,128)(2,1)}), bf16[32,64,512]{2,1,0:T(8,128)(2,1)}, u32[]{:S(2)}, u32[]{:S(2)}) async-start(bf16[32,64,512]{2,1,0:T(8,128)(2,1)} %bitcast.256), calls=%async_computation.1 | async-start | bytes 4194304 | tf_op jit(solution)/shard_map/all_to_all | solution.py:364
  129.0 252.3 %all-gather.2.cloned.1.call-start = ((), (), s32[]{:S(2)}) async-start(), calls=%async_computation.16 | async-start | bytes 15728640 | tf_op jit(solution)/shard_map/all_gather | solution.py:442
  131.8 51.1 %collective-permute-start = (bf16[512,2048]{1,0:T(8,128)(2,1)}, bf16[512,2048]{1,0:T(8,128)(2,1)}, u32[]{:S(2)}, u32[]{:S(2)}) collective-permute-start(bf16[512,2048]{1,0:T(8,128)(2,1)} %bitcast), channel_id=1, source_target_pairs={{0,2},{2,0},{1,3},{3,1},{4,6},{6,4},{5,7},{7,5},{8,10},{10,8},{9,1... | collective-permute-start | bytes 6291464 | tf_op jit(solution)/shard_map/ppermute | solution.py:371
  178.8 34.4 %all-to-all-start.2 = ((bf16[32,64,256]{2,1,0:T(8,128)(2,1)}), bf16[32,64,256]{2,1,0:T(8,128)(2,1)S(1)}, u32[]{:S(2)}, u32[]{:S(2)}) async-start(bf16[32,64,256]{2,1,0:T(8,128)(2,1)} %bitcast.15), calls=%async_computation.2 | async-start | bytes 2097152 | tf_op jit(solution)/shard_map/all_to_all | solution.py:364
  214.8 4.2 collective-permute-start.1
  275.8 52.5 %all-to-all-start.4 = ((bf16[4,128,2048]{2,1,0:T(8,128)(2,1)}), bf16[4,128,2048]{2,1,0:T(8,128)(2,1)}, u32[]{:S(2)}, u32[]{:S(2)}) async-start(bf16[4,128,2048]{2,1,0:T(8,128)(2,1)} %broadcast_in_dim.131), calls=%async_computation.4 | async-start | bytes 4194304 | tf_op jit(solution)/shard_map/all_to_all | solution.py:364
  330.0 51.3 %all-to-all-start.7 = ((bf16[4,128,2048]{2,1,0:T(8,128)(2,1)}), bf16[4,128,2048]{2,1,0:T(8,128)(2,1)S(1)}, u32[]{:S(2)}, u32[]{:S(2)}) async-start(bf16[4,128,2048]{2,1,0:T(8,128)(2,1)} %broadcast_in_dim.134), calls=%async_computation.7 | async-start | bytes 4194304 | tf_op jit(solution)/shard_map/all_to_all | solution.py:364
  333.6 160.0 %collective-permute-start.2 = (bf16[512,2048]{1,0:T(8,128)(2,1)}, bf16[512,2048]{1,0:T(8,128)(2,1)}, u32[]{:S(2)}, u32[]{:S(2)}) collective-permute-start(bf16[512,2048]{1,0:T(8,128)(2,1)} %bitcast.21), channel_id=1, source_target_pairs={{0,2},{2,0},{1,3},{3,1},{4,6},{6,4},{5,7},{7,5},{8,10},{10,8},{9,1... | collective-permute-start | bytes 6291464 | tf_op jit(solution)/shard_map/ppermute | solution.py:371
  381.2 130.5 %collective-permute-start.5 = (bf16[512,2048]{1,0:T(8,128)(2,1)S(1)}, bf16[512,2048]{1,0:T(8,128)(2,1)}, u32[]{:S(2)}, u32[]{:S(2)}) collective-permute-start(bf16[512,2048]{1,0:T(8,128)(2,1)S(1)} %bitcast.278), channel_id=1, source_target_pairs={{0,2},{2,0},{1,3},{3,1},{4,6},{6,4},{5,7},{7,5},{8,10},{10,8},{9,1... | collective-permute-start | bytes 6291464 | tf_op jit(solution)/shard_map/ppermute | solution.py:371
  536.1 4.2 collective-permute-start.6
  542.4 52.4 %all-to-all-start.8 = ((bf16[4,128,2048]{2,1,0:T(8,128)(2,1)}), bf16[4,128,2048]{2,1,0:T(8,128)(2,1)S(1)}, u32[]{:S(2)}, u32[]{:S(2)}) async-start(bf16[4,128,2048]{2,1,0:T(8,128)(2,1)} %bitcast.258), calls=%async_computation.8 | async-start | bytes 4194304 | tf_op jit(solution)/shard_map/all_to_all | solution.py:364
  594.8 65.3 %all-to-all-start.6 = ((bf16[4,128,2048]{2,1,0:T(8,128)(2,1)}), bf16[4,128,2048]{2,1,0:T(8,128)(2,1)}, u32[]{:S(2)}, u32[]{:S(2)}) async-start(bf16[4,128,2048]{2,1,0:T(8,128)(2,1)} %bitcast.257), calls=%async_computation.6 | async-start | bytes 4194304 | tf_op jit(solution)/shard_map/all_to_all | solution.py:364
  675.1 42.8 %all-to-all-start.9 = ((bf16[4,128,2048]{2,1,0:T(8,128)(2,1)}), bf16[4,128,2048]{2,1,0:T(8,128)(2,1)}, u32[]{:S(2)}, u32[]{:S(2)}) async-start(bf16[4,128,2048]{2,1,0:T(8,128)(2,1)} %broadcast_in_dim.135), calls=%async_computation.9 | async-start | bytes 4194304 | tf_op jit(solution)/shard_map/all_to_all | solution.py:364
  717.9 143.7 %all-to-all-start.13 = ((bf16[4,1024,1536]{1,2,0:T(8,128)(2,1)}), bf16[4,1024,1536]{1,2,0:T(8,128)(2,1)}, u32[]{:S(2)}, u32[]{:S(2)}) async-start(bf16[4,1024,1536]{1,2,0:T(8,128)(2,1)} %bitcast.242), calls=%async_computation.13 | async-start | bytes 25165824 | tf_op jit(solution)/shard_map/all_to_all | solution.py:364
  724.6 4.4 collective-permute-start.7
  861.6 28.8 %all-to-all-start.10 = ((bf16[4,128,2048]{2,1,0:T(8,128)(2,1)}), bf16[4,128,2048]{2,1,0:T(8,128)(2,1)}, u32[]{:S(2)}, u32[]{:S(2)}) async-start(bf16[4,128,2048]{2,1,0:T(8,128)(2,1)} %bitcast.56), calls=%async_computation.10 | async-start | bytes 4194304 | tf_op jit(solution)/shard_map/all_to_all | solution.py:364
  890.5 31.4 %all-to-all-start.12 = ((bf16[32,64,256]{2,1,0:T(8,128)(2,1)}), bf16[32,64,256]{2,1,0:T(8,128)(2,1)}, u32[]{:S(2)}, u32[]{:S(2)}) async-start(bf16[32,64,256]{2,1,0:T(8,128)(2,1)} %bitcast.60), calls=%async_computation.12 | async-start | bytes 2097152 | tf_op jit(solution)/shard_map/all_to_all | solution.py:364
  922.4 10.8 all-to-all-start.15
  933.2 53.5 %all-to-all-start.11 = ((bf16[32,64,512]{2,1,0:T(8,128)(2,1)}), bf16[32,64,512]{2,1,0:T(8,128)(2,1)}, u32[]{:S(2)}, u32[]{:S(2)}) async-start(bf16[32,64,512]{2,1,0:T(8,128)(2,1)} %bitcast.281), calls=%async_computation.11 | async-start | bytes 4194304 | tf_op jit(solution)/shard_map/all_to_all | solution.py:364
  986.7 76.4 %all-to-all-start.14 = ((bf16[8,128,1536]{2,1,0:T(8,128)(2,1)}), bf16[8,128,1536]{2,1,0:T(8,128)(2,1)}, u32[]{:S(2)}, u32[]{:S(2)}) async-start(bf16[8,128,1536]{2,1,0:T(8,128)(2,1)} %bitcast.251), calls=%async_computation.14 | async-start | bytes 6291456 | tf_op jit(solution)/shard_map/all_to_all | solution.py:364
  1075.0 10.6 collective-permute-start.9
  (53 other events, 690.4 us)
Sparse Core Ops, SparseCore 0:
  132.2 166.8 all-gather.1

commit v2 on v0

--- a/solution.py
+++ b/solution.py
@@ -1,6 +1,11 @@
+import functools
+
 import jax
 import jax.numpy as jnp
 from jax import lax
+from jax.experimental import pallas as pl
+from jax.experimental.pallas import tpu as pltpu
+from jax.sharding import Mesh
 from jax.sharding import PartitionSpec as P
 
 D = 2048
@@ -55,7 +60,7 @@
     )
 
 
-def per_device(
+def general_plan(
     layer_input,
     span_order,
     qkv_weight,
@@ -344,30 +349,775 @@
     )
 
 
+ALL_AXES = ("dp", "yy", "cc", "uly")
+SIDE_AXES = ("yy", "uly")
+PLANE_AXES = ("yy", "cc", "uly")
+GROUP_AXES = ("dp", "cc")
+SWAP = [(0, 1), (1, 0)]
+DIAGONAL = [(0, 3), (1, 2), (2, 1), (3, 0)]
+VMEM_SPEC = pl.BlockSpec(memory_space=pltpu.VMEM)
+KERNEL = dict(
+    compiler_params=pltpu.CompilerParams(vmem_limit_bytes=58 * 1024 * 1024),
+    cost_estimate=pl.CostEstimate(flops=1000, bytes_accessed=1000, transcendentals=0),
+)
+ROWS = 256
+BY_ROWS = (((0,), (0,)), ((), ()))
+BY_COLS = (((1,), (1,)), ((), ()))
+PLAIN = (((1,), (0,)), ((), ()))
+
+
+def wide(values):
+    return values.astype(jnp.float32)
+
+
+def low(values):
+    return values.astype(jnp.bfloat16)
+
+
+def dot32(left, right, dims=PLAIN):
+    return lax.dot_general(left, right, dims, preferred_element_type=jnp.float32)
+
+
+def low_shape(rows, cols):
+    return jax.ShapeDtypeStruct((rows, cols), jnp.bfloat16)
+
+
+def wide_shape(rows, cols):
+    return jax.ShapeDtypeStruct((rows, cols), jnp.float32)
+
+
+def once(shape):
+    return pl.BlockSpec(shape, lambda *i: (0,) * len(shape), pipeline_mode=pl.Buffered(1))
+
+
+def row_block(step):
+    return pl.ds(pl.multiple_of(step * ROWS, ROWS), ROWS)
+
+
+def head_cut(head):
+    return slice(head * HD, (head + 1) * HD)
+
+
+def join_rows(pieces, out):
+    rows = pieces[0].shape[0]
+    for number, piece in enumerate(pieces):
+        out[number * rows : (number + 1) * rows, :] = piece[...]
+
+
+def turn(values, cosine, sine):
+    return values * cosine + pltpu.roll(values, HD // 2, 1) * sine
+
+
+def softmax_rows(query, key, key_pos, query_pos):
+    scores = dot32(query, key, BY_COLS) * HD ** (-0.5)
+    allowed = key_pos <= query_pos
+    scores = jnp.where(allowed, scores, MASKED)
+    top = jnp.max(scores, axis=1, keepdims=True)
+    weights = jnp.where(allowed, jnp.exp(scores - top), 0.0)
+    return weights / jnp.sum(weights, axis=1, keepdims=True)
+
+
+def attention_forward_body(group, weight, cosine, sine, pos_col, pos_row, *refs):
+    pieces, (query_out, key_out, value_out, heads_out, normed) = refs[:-5], refs[-5:]
+    join_rows(pieces, normed)
+    steps = normed.shape[0] // ROWS
+
+    def project(step, carry):
+        at = row_block(step)
+        qkv = dot32(normed[at, :], weight[...])
+        for head in range(group):
+            turned = turn(qkv[:, head_cut(head)], cosine[at, :], sine[at, :])
+            query_out[at, head_cut(head)] = low(turned)
+        key_out[at, :] = low(turn(qkv[:, head_cut(group)], cosine[at, :], sine[at, :]))
+        value_out[at, :] = low(qkv[:, head_cut(group + 1)])
+        return carry
+
+    def attend(step, carry):
+        at = row_block(step)
+        for head in range(group):
+            probs = softmax_rows(
+                query_out[at, head_cut(head)], key_out[...], pos_row[...], pos_col[at, :]
+            )
+            heads_out[at, head_cut(head)] = low(dot32(low(probs), value_out[...]))
+        return carry
+
+    lax.fori_loop(0, steps, project, 0)
+    lax.fori_loop(0, steps, attend, 0)
+
+
+def attention_forward(pieces, weight, cosine, sine, positions):
+    rows, group = positions.shape[0], weight.shape[1] // HD - 2
+    return pl.pallas_call(
+        functools.partial(attention_forward_body, group),
+        out_shape=(
+            low_shape(rows, group * HD),
+            low_shape(rows, HD),
+            low_shape(rows, HD),
+            low_shape(rows, group * HD),
+        ),
+        in_specs=[VMEM_SPEC] * (5 + len(pieces)),
+        out_specs=(VMEM_SPEC,) * 4,
+        scratch_shapes=[pltpu.VMEM((rows, weight.shape[0]), jnp.bfloat16)],
+        name="attention_forward",
+        **KERNEL,
+    )(weight, cosine, sine, positions[:, None], positions[None, :], *pieces)
+
+
+def attention_backward_body(group, weight, query, key, value, cosine, sine, pos_col, pos_row, *refs):
+    pieces, (grad_qkv, grad_out, key_sum, value_sum) = refs[:-4], refs[-4:]
+    join_rows(pieces, grad_out)
+    steps = query.shape[0] // ROWS
+    key_sum[...] = jnp.zeros_like(key_sum)
+    value_sum[...] = jnp.zeros_like(value_sum)
+
+    def block(step, carry):
+        at = row_block(step)
+        grad_heads = low(dot32(grad_out[at, :], weight[...]))
+        for head in range(group):
+            cut = head_cut(head)
+            probs = softmax_rows(query[at, cut], key[...], pos_row[...], pos_col[at, :])
+            grad_probs = dot32(grad_heads[:, cut], value[...], BY_COLS)
+            delta = jnp.sum(probs * grad_probs, axis=1, keepdims=True)
+            grad_scores = low(probs * (grad_probs - delta))
+            grad_query = wide(low(dot32(grad_scores, key[...]) * HD ** (-0.5)))
+            grad_qkv[at, cut] = low(turn(grad_query, cosine[at, :], -sine[at, :]))
+            key_sum[...] += dot32(grad_scores, query[at, cut], BY_ROWS)
+            value_sum[...] += dot32(low(probs), grad_heads[:, cut], BY_ROWS)
+        return carry
+
+    def finish(step, carry):
+        at = row_block(step)
+        grad_key = wide(low(key_sum[at, :] * HD ** (-0.5)))
+        grad_qkv[at, head_cut(group)] = low(turn(grad_key, cosine[at, :], -sine[at, :]))
+        grad_qkv[at, head_cut(group + 1)] = low(value_sum[at, :])
+        return carry
+
+    lax.fori_loop(0, steps, block, 0)
+    lax.fori_loop(0, steps, finish, 0)
+
+
+def attention_backward(pieces, weight, query, key, value, cosine, sine, positions):
+    rows, group = query.shape[0], query.shape[1] // HD
+    return pl.pallas_call(
+        functools.partial(attention_backward_body, group),
+        out_shape=low_shape(rows, (group + 2) * HD),
+        in_specs=[VMEM_SPEC] * (8 + len(pieces)),
+        out_specs=VMEM_SPEC,
+        scratch_shapes=[pltpu.VMEM((rows, weight.shape[0]), jnp.bfloat16)]
+        + [pltpu.VMEM((rows, HD), jnp.float32)] * 2,
+        name="attention_backward",
+        **KERNEL,
+    )(weight, query, key, value, cosine, sine, positions[:, None], positions[None, :], *pieces)
+
+
+def halves_specs(steps, rows, cols):
+    half = steps // 2
+    return (
+        pl.BlockSpec((rows, cols), lambda i: (jnp.minimum(i, half - 1), 0)),
+        pl.BlockSpec((rows, cols), lambda i: (jnp.maximum(i - half, 0), 0)),
+    )
+
+
+def store_half(first, second, values):
+    step, half = pl.program_id(0), pl.num_programs(0) // 2
+
+    @pl.when(step < half)
+    def _():
+        first[...] = values
+
+    @pl.when(step >= half)
+    def _():
+        second[...] = values
+
+
+def by_cols_body(parts, rows, weight, first, second):
+    depth, chunk = weight.shape[0] // parts**2, weight.shape[1]
+    out = []
+    for y in range(parts):
+        total = 0.0
+        for x in range(parts):
+            at = (y * parts + x) * depth
+            cut = slice(x * chunk, (x + 1) * chunk)
+            total += dot32(rows[:, cut], weight[at : at + depth, :], BY_COLS)
+        out.append(low(total))
+    store_half(first, second, out[0] if parts == 1 else jnp.concatenate(out, axis=1))
+
+
+def by_cols_pass(rows, weight, parts, name):
+    count, width = rows.shape[0], weight.shape[0] // parts
+    steps = count // ROWS
+    return pl.pallas_call(
+        functools.partial(by_cols_body, parts),
+        grid=(steps,),
+        out_shape=(low_shape(count // 2, width),) * 2,
+        in_specs=[pl.BlockSpec((ROWS, rows.shape[1]), lambda i: (i, 0)), once(weight.shape)],
+        out_specs=halves_specs(steps, ROWS, width),
+        name=name,
+        **KERNEL,
+    )(rows, weight)
+
+
+def square_dot(rows, weight):
+    depth = weight.shape[0] // 4
+    near, far = rows[:, :depth], rows[:, depth:]
+    out = [
+        dot32(near, weight[x * depth : (x + 1) * depth, :])
+        + dot32(far, weight[(2 + x) * depth : (3 + x) * depth, :])
+        for x in (0, 1)
+    ]
+    return jnp.concatenate(out, axis=1)
+
+
+def hidden_body(gate_w, up_w, *refs):
+    normed_p, (hidden_out, gate_slope, up_slope, normed) = refs[:-4], refs[-4:]
+
+    @pl.when(pl.program_id(0) == 0)
+    def _():
+        join_rows(normed_p, normed)
+
+    rows = normed[row_block(pl.program_id(0)), :]
+    gate, up = square_dot(rows, gate_w), square_dot(rows, up_w)
+    sig = jax.nn.sigmoid(gate)
+    hidden_out[...] = low(gate * sig * up)
+    gate_slope[...] = low(up * sig * (1.0 + gate * (1.0 - sig)))
+    up_slope[...] = low(gate * sig)
+
+
+def hidden_pass(normed_p, gate_w, up_w):
+    rows, width = len(normed_p) * normed_p[0].shape[0], normed_p[0].shape[1]
+    units = 2 * gate_w.shape[1]
+    by_rows = pl.BlockSpec((ROWS, units), lambda i: (i, 0))
+    return pl.pallas_call(
+        hidden_body,
+        grid=(rows // ROWS,),
+        out_shape=(low_shape(rows, units),) * 3,
+        in_specs=[once(v.shape) for v in (gate_w, up_w, *normed_p)],
+        out_specs=(by_rows,) * 3,
+        scratch_shapes=[pltpu.VMEM((rows, width), jnp.bfloat16)],
+        name="hidden_pass",
+        **KERNEL,
+    )(gate_w, up_w, *normed_p)
+
+
+def grad_hidden_body(gate_w, up_w, down_w, gate_slope, up_slope, *refs):
+    cot_p, (grad_gate, grad_up, first, second, cot) = refs[:-5], refs[-5:]
+
+    @pl.when(pl.program_id(0) == 0)
+    def _():
+        join_rows(cot_p, cot)
+
+    grad_hidden = square_dot(cot[row_block(pl.program_id(0)), :], down_w)
+    grad_gate[...] = low(grad_hidden * wide(gate_slope[...]))
+    grad_up[...] = low(grad_hidden * wide(up_slope[...]))
+    depth, chunk = gate_w.shape[0] // 4, gate_w.shape[1]
+    out = []
+    for y in (0, 1):
+        total = 0.0
+        for x in (0, 1):
+            at, cut = (2 * y + x) * depth, slice(x * chunk, (x + 1) * chunk)
+            total += dot32(grad_gate[:, cut], gate_w[at : at + depth, :], BY_COLS)
+            total += dot32(grad_up[:, cut], up_w[at : at + depth, :], BY_COLS)
+        out.append(low(total))
+    store_half(first, second, jnp.concatenate(out, axis=1))
+
+
+def grad_hidden_pass(cot_p, gate_slope, up_slope, gate_w, up_w, down_w):
+    rows, width = len(cot_p) * cot_p[0].shape[0], cot_p[0].shape[1]
+    units = 2 * gate_w.shape[1]
+    by_rows = pl.BlockSpec((ROWS, units), lambda i: (i, 0))
+    steps = rows // ROWS
+    return pl.pallas_call(
+        grad_hidden_body,
+        grid=(steps,),
+        out_shape=(low_shape(rows, units),) * 2 + (low_shape(rows // 2, width),) * 2,
+        in_specs=[once(v.shape) for v in (gate_w, up_w, down_w)]
+        + [by_rows] * 2
+        + [once(v.shape) for v in cot_p],
+        out_specs=(by_rows,) * 2 + halves_specs(steps, ROWS, width),
+        scratch_shapes=[pltpu.VMEM((rows, width), jnp.bfloat16)],
+        name="grad_hidden_pass",
+        **KERNEL,
+    )(gate_w, up_w, down_w, gate_slope, up_slope, *cot_p)
+
+
+def term_body(*refs):
+    pieces, columns, out = refs[:-2], refs[-2], refs[-1]
+    rows = jnp.concatenate([piece[...] for piece in pieces], axis=0)
+    out[...] = low(dot32(rows, columns[...], BY_ROWS))
+
+
+def term_pass(pieces, columns, row_parts, col_parts):
+    tokens, width = pieces[0].shape
+    depth, chunk = width // row_parts, columns.shape[1] // col_parts
+    return pl.pallas_call(
+        term_body,
+        grid=(row_parts, col_parts),
+        out_shape=low_shape(width * col_parts, chunk),
+        in_specs=[pl.BlockSpec((tokens, depth), lambda y, x: (0, y))] * len(pieces)
+        + [pl.BlockSpec((columns.shape[0], chunk), lambda y, x: (0, x))],
+        out_specs=pl.BlockSpec((depth, chunk), lambda y, x: (y * col_parts + x, 0)),
+        name="term_pass",
+        **KERNEL,
+    )(*pieces, columns)
+
+
+def unit_scale(values):
+    return lax.rsqrt(jnp.mean(values * values, axis=-1, keepdims=True) + EPSILON)
+
+
+def norm_pull(values, grad_scaled):
+    scale = unit_scale(values)
+    mean = jnp.mean(grad_scaled * values, axis=-1, keepdims=True)
+    return scale * grad_scaled - values * (scale * scale * scale) * mean
+
+
+def pick(bit, near, far):
+    return jnp.where(bit == 0, near, far)
+
+
+def to_split(values):
+    step = values.shape[1] // 8
+    cuts = [values[:, at * step : (at + 1) * step] for at in range(8)]
+    return jnp.concatenate(cuts[0::2] + cuts[1::2], axis=1)
+
+
+def from_split(values):
+    step = values.shape[1] // 8
+    cuts = [values[:, at * step : (at + 1) * step] for at in range(8)]
+    return jnp.concatenate([cut for pair in zip(cuts[:4], cuts[4:]) for cut in pair], axis=1)
+
+
+def column_sums(*arrays):
+    return jnp.concatenate([jnp.sum(v * v, axis=0, keepdims=True) for v in arrays], axis=0)
+
+
+def summed(parts):
+    total = wide(parts[0][...])
+    for part in parts[1:]:
+        total += wide(part[...])
+    return total
+
+
+def middle_body(stream_in, *refs):
+    parts, (middle_out, normed_out, squares_out) = refs[:-3], refs[-3:]
+    attn_out, rows = summed(parts), wide(stream_in[...])
+    middle = rows + attn_out
+    middle_out[...] = middle
+    normed_out[...] = to_split(low(middle * unit_scale(middle)))
+    squares_out[...] = column_sums(rows, attn_out, middle)
+
+
+def middle_pass(stream_in, parts):
+    rows, width = stream_in.shape
+    return pl.pallas_call(
+        middle_body,
+        out_shape=(wide_shape(rows, width), low_shape(rows, width), wide_shape(3, width)),
+        in_specs=[VMEM_SPEC] * (1 + len(parts)),
+        out_specs=(VMEM_SPEC,) * 3,
+        name="middle_pass",
+        **KERNEL,
+    )(stream_in, *parts)
+
+
+def final_body(middle, *refs):
+    parts, (layer_out, squares_out) = refs[:-2], refs[-2:]
+    mlp_out = from_split(summed(parts))
+    final = middle[...] + mlp_out
+    layer_out[...] = low(final)
+    squares_out[...] = column_sums(mlp_out, final)
+
+
+def final_pass(middle, parts):
+    rows, width = middle.shape
+    return pl.pallas_call(
+        final_body,
+        out_shape=(low_shape(rows, width), wide_shape(2, width)),
+        in_specs=[VMEM_SPEC] * (1 + len(parts)),
+        out_specs=(VMEM_SPEC,) * 2,
+        name="final_pass",
+        **KERNEL,
+    )(middle, *parts)
+
+
+def grad_middle_body(middle, cot, *refs):
+    parts, (grad_out, low_out) = refs[:-2], refs[-2:]
+    grad_normed = from_split(summed(parts))
+    grad = wide(cot[...]) + norm_pull(middle[...], grad_normed)
+    grad_out[...] = grad
+    low_out[...] = low(grad)
+
+
+def grad_middle_pass(middle, cot, parts):
+    rows, width = middle.shape
+    return pl.pallas_call(
+        grad_middle_body,
+        out_shape=(wide_shape(rows, width), low_shape(rows, width)),
+        in_specs=[VMEM_SPEC] * (2 + len(parts)),
+        out_specs=(VMEM_SPEC,) * 2,
+        name="grad_middle_pass",
+        **KERNEL,
+    )(middle, cot, *parts)
+
+
+def input_grad_body(stream_in, grad_middle, *refs):
+    parts, out = refs[:-1], refs[-1]
+    out[...] = grad_middle[...] + norm_pull(wide(stream_in[...]), summed(parts))
+
+
+def input_grad_pass(stream_in, grad_middle, parts):
+    return pl.pallas_call(
+        input_grad_body,
+        out_shape=wide_shape(*stream_in.shape),
+        in_specs=[VMEM_SPEC] * (2 + len(parts)),
+        out_specs=VMEM_SPEC,
+        name="input_grad_pass",
+        **KERNEL,
+    )(stream_in, grad_middle, *parts)
+
+
+def pack_body(gain, gate_up, down, gate_out, up_out, down_out):
+    gate_out[...] = low(wide(gate_up[:, 0, :]) * gain[...])
+    up_out[...] = low(wide(gate_up[:, 1, :]) * gain[...])
+    down_out[...] = down[...]
+
+
+def pack_pass(gain, gate_up, down, groups):
+    rows, chunk = down.shape[0], down.shape[1] // groups
+    out = pl.BlockSpec((rows, chunk), lambda g: (g, 0))
+    return pl.pallas_call(
+        pack_body,
+        grid=(groups,),
+        out_shape=(low_shape(groups * rows, chunk),) * 3,
+        in_specs=[
+            pl.BlockSpec((rows, 1), lambda g: (0, 0)),
+            pl.BlockSpec((rows, 2, chunk), lambda g: (0, 0, g)),
+            pl.BlockSpec((rows, chunk), lambda g: (0, g)),
+        ],
+        out_specs=(out,) * 3,
+        name="pack_pass",
+        **KERNEL,
+    )(gain, gate_up, down)
+
+
+def unpack_body(gain, weight, gate, up, out, gain_sum):
+    gate_term, up_term = wide(gate[...]), wide(up[...])
+    out[:, 0, :] = gate_term * gain[...]
+    out[:, 1, :] = up_term * gain[...]
+    products = gate_term * wide(weight[:, 0, :]) + up_term * wide(weight[:, 1, :])
+    total = jnp.sum(products, axis=1, keepdims=True)
+
+    @pl.when(pl.program_id(0) == 0)
+    def _():
+        gain_sum[...] = total
+
+    @pl.when(pl.program_id(0) > 0)
+    def _():
+        gain_sum[...] += total
+
+
+def unpack_pass(gain, weight, gate, up, groups):
+    rows, chunk = weight.shape[0], weight.shape[2] // groups
+    column = pl.BlockSpec((rows, 1), lambda g: (0, 0))
+    pair = pl.BlockSpec((rows, 2, chunk), lambda g: (0, 0, g))
+    by_group = pl.BlockSpec((rows, chunk), lambda g: (g, 0))
+    return pl.pallas_call(
+        unpack_body,
+        grid=(groups,),
+        out_shape=(jax.ShapeDtypeStruct(weight.shape, jnp.float32), wide_shape(rows, 1)),
+        in_specs=[column, pair, by_group, by_group],
+        out_specs=(pair, column),
+        name="unpack_pass",
+        **KERNEL,
+    )(gain, weight, gate, up)
+
+
+def exchange(values, axes):
+    return lax.all_to_all(values, axes, split_axis=0, concat_axis=0, tiled=True)
+
+
+def after(values, *earlier):
+    return lax.optimization_barrier((values, *earlier))[0]
+
+
+def together(*values):
+    return lax.optimization_barrier(values)
+
+
+def swap(values, *axes):
+    pairs = SWAP if len(axes) == 1 else DIAGONAL
+    return lax.ppermute(values, axes if len(axes) > 1 else axes[0], pairs)
+
+
+def plane_hop(rows):
+    return (rows, swap(rows, "uly"), swap(rows, "yy"), swap(rows, "yy", "uly"))
+
+
+def plane_back(parts):
+    return (parts[0], swap(parts[1], "uly"), swap(parts[2], "yy"), swap(parts[3], "yy", "uly"))
+
+
+def shift(values, by):
+    count = lax.axis_size("dp")
+    return lax.ppermute(values, "dp", [(i, (i + by) % count) for i in range(count)])
+
+
+def column_hop(rows):
+    return (rows, *(shift(rows, by) for by in range(1, lax.axis_size("dp"))))
+
+
+def column_back(parts):
+    return (parts[0], *(shift(v, -by) for by, v in enumerate(parts[1:], 1)))
+
+
+def core_hop(pieces):
+    return (*pieces, *(swap(v, "cc") for v in pieces))
+
+
+def chip_parts(first, arrived, count):
+    return tuple(jnp.split(low(wide(first) + wide(arrived)), count, axis=0))
+
+
+def plane_plan(
+    layer_input,
+    span_order,
+    qkv_weight,
+    out_weight,
+    gate_up_weight,
+    down_weight,
+    attn_gain,
+    mlp_gain,
+    output_cotangent,
+):
+    tok = layer_input.shape[0]
+    nz = lax.axis_size("dp")
+    ndev = lax.axis_size(ALL_AXES)
+    plane = ndev // nz
+    span_size = tok * plane // span_order.shape[1]
+    y_at, c_at, x_at = lax.axis_index("yy"), lax.axis_index("cc"), lax.axis_index("uly")
+    q_cols, kv_cols = H * HD // plane, KV * HD // plane
+    own_cols = q_cols + 2 * kv_cols
+    d_rows = qkv_weight.shape[0]
+    mlp_rows, ff_local = down_weight.shape
+    hgroups = lax.axis_size(GROUP_AXES)
+    hchunk = ff_local // hgroups
+
+    gain_a = wide(attn_gain)[:, None]
+    folded = low(wide(qkv_weight) * gain_a)
+    by_group = jnp.concatenate(
+        [
+            part.reshape(d_rows, plane, -1)
+            for part in jnp.split(folded, [H * HD, (H + KV) * HD], axis=1)
+        ],
+        axis=2,
+    ).transpose(1, 0, 2)
+
+    def to_planes(rows):
+        return jnp.broadcast_to(rows[None], (nz, *rows.shape)).reshape(-1, rows.shape[2])
+
+    qkv_rows = to_planes(by_group)
+    out_rows = out_weight.reshape(d_rows, plane, q_cols).transpose(1, 0, 2).reshape(-1, q_cols)
+    out_here = exchange(out_rows, PLANE_AXES)
+
+    gain_peer = swap(mlp_gain[None, :], "uly")
+    stream_in = wide(layer_input)
+    normed = low(stream_in * unit_scale(stream_in))
+    normed, gain_peer, out_here, qkv_rows = together(normed, gain_peer, out_here, qkv_rows)
+
+    gain_own, gain_peer = wide(mlp_gain)[None, :], wide(gain_peer)
+    gain_m = pick(
+        x_at,
+        jnp.concatenate([gain_own, gain_peer], axis=1),
+        jnp.concatenate([gain_peer, gain_own], axis=1),
+    ).reshape(mlp_rows, 1)
+    gate_rows, up_rows, down_rows = pack_pass(gain_m, gate_up_weight, down_weight, hgroups)
+
+    cot_split = to_split(output_cotangent)
+
+    block = jnp.arange(plane, dtype=jnp.int32)
+    core_of, y_of, x_of = (block // 4) ^ c_at, (block // 2) % 2 ^ y_at, block % 2 ^ x_at
+    stored = (y_of * 2 + core_of) * 2 + x_of
+    row_at = (stored[:, None] * tok + jnp.arange(tok, dtype=jnp.int32)[None, :]).reshape(-1)
+    positions = sequence_positions(row_at, span_size, span_order[0])
+    angles = rope_angles(positions)
+    cosine = jnp.concatenate([jnp.cos(angles)] * 2, axis=1)
+    sine = jnp.concatenate([-jnp.sin(angles), jnp.sin(angles)], axis=1)
+
+    wo = lax.all_gather(out_here, "dp", axis=0, tiled=True)
+    gate_here = exchange(gate_rows, GROUP_AXES)
+    normed_p = plane_hop(normed)
+    gate_here, normed_p, qkv_rows, up_rows, down_rows, cosine, sine, cot_split = together(
+        gate_here, normed_p, qkv_rows, up_rows, down_rows, cosine, sine, cot_split
+    )
+
+    def spread(here):
+        return lax.all_gather(here, SIDE_AXES, axis=0, tiled=True)
+
+    gate_w = spread(gate_here)
+    wq = exchange(qkv_rows, ALL_AXES)
+    normed_p = core_hop(normed_p)
+    cot_1 = shift(cot_split, 1)
+    wq, normed_p, cot_1, up_rows, cot_split = together(wq, normed_p, cot_1, up_rows, cot_split)
+
+    up_here = exchange(up_rows, GROUP_AXES)
+    query, key, value, heads = attention_forward(normed_p, wq, cosine, sine, positions)
+    up_here, heads, wo, down_rows = together(up_here, heads, wo, down_rows)
+
+    up_w = spread(up_here)
+    attn_first, attn_second = by_cols_pass(heads, wo, 1, "out_pass")
+    attn_arrived = swap(attn_second, "cc")
+    attn_parts = chip_parts(attn_first, attn_arrived, 4)
+    attn_parts, down_rows, cot_split = together(attn_parts, down_rows, cot_split)
+
+    down_here = exchange(down_rows, GROUP_AXES)
+    cot_3 = shift(cot_split, 3)
+    attn_parts = plane_back(attn_parts)
+    attn_parts, down_here, cot_3, cot_split = together(attn_parts, down_here, cot_3, cot_split)
+
+    down_w = spread(down_here)
+    middle, zhat, squares_a = middle_pass(layer_input, attn_parts)
+    zhat_p = column_hop(zhat)
+    zhat_p, gate_w, up_w, cot_split = together(zhat_p, gate_w, up_w, cot_split)
+    zhat_p, cot_split = together(core_hop(zhat_p), cot_split)
+
+    cot_p = (cot_split, cot_1, shift(cot_split, 2), cot_3)
+    hidden, gate_slope, up_slope = hidden_pass(zhat_p, gate_w, up_w)
+    hidden, cot_p, gate_slope, down_w = together(hidden, cot_p, gate_slope, down_w)
+    cot_p = core_hop(cot_p)
+    mlp_first, mlp_second = by_cols_pass(hidden, down_w, 2, "down_pass")
+    cot_p, mlp_first, mlp_second = together(cot_p, mlp_first, mlp_second)
+
+    mlp_arrived = swap(mlp_second, "cc")
+    grad_gate, grad_up, gz_first, gz_second = grad_hidden_pass(
+        cot_p, gate_slope, up_slope, gate_w, up_w, down_w
+    )
+    gz_second, grad_gate, mlp_arrived = together(gz_second, grad_gate, mlp_arrived)
+
+    def side_sum(term):
+        return lax.psum_scatter(term, SIDE_AXES, scatter_dimension=0, tiled=True)
+
+    gz_arrived = swap(gz_second, "cc")
+    gate_t = term_pass(zhat_p, grad_gate, 2, 2)
+    gz_parts = chip_parts(gz_first, gz_arrived, nz)
+    gz_parts, gate_t, mlp_arrived = together(gz_parts, gate_t, mlp_arrived)
+
+    gate_t = side_sum(gate_t)
+    gz_parts = column_back(gz_parts)
+    up_t = term_pass(zhat_p, grad_up, 2, 2)
+    down_t = term_pass(cot_p, hidden, 2, 2)
+    mlp_parts = chip_parts(mlp_first, mlp_arrived, nz)
+    gz_parts, up_t, down_t, mlp_parts = together(gz_parts, up_t, down_t, mlp_parts)
+
+    up_t = side_sum(up_t)
+    grad_middle, grad_out = grad_middle_pass(middle, output_cotangent, gz_parts)
+    mlp_1, mlp_3 = shift(mlp_parts[1], -1), shift(mlp_parts[3], -3)
+    grad_out_p = plane_hop(grad_out)
+    grad_out_p, mlp_1, mlp_3, down_t = together(grad_out_p, mlp_1, mlp_3, down_t)
+    grad_out_p, gate_t, down_t = together(core_hop(grad_out_p), gate_t, down_t)
+
+    down_t = side_sum(down_t)
+    gate_back = exchange(gate_t, GROUP_AXES)
+    mlp_2 = shift(mlp_parts[2], -2)
+    grad_qkv = attention_backward(grad_out_p, wo, query, key, value, cosine, sine, positions)
+    gx_first, gx_second = by_cols_pass(grad_qkv, wq, 1, "qkv_back_pass")
+    qkv_term = term_pass(normed_p, grad_qkv, 2, 1)
+    gx_second, qkv_term, gate_back, mlp_2, heads, up_t = together(
+        gx_second, qkv_term, gate_back, mlp_2, heads, up_t
+    )
+
+    gx_arrived = swap(gx_second, "cc")
+    out_term = term_pass(grad_out_p, heads, 2, 1)
+    gx_parts = chip_parts(gx_first, gx_arrived, 4)
+    gx_parts, out_term, qkv_term, up_t = together(gx_parts, out_term, qkv_term, up_t)
+
+    qkv_sum = exchange(qkv_term, ALL_AXES)
+    gx_parts = plane_back(gx_parts)
+    gx_parts, qkv_sum, up_t, down_t, out_term = together(
+        gx_parts, qkv_sum, up_t, down_t, out_term
+    )
+
+    out_term = lax.psum_scatter(out_term, "dp", scatter_dimension=0, tiled=True)
+    both_back = exchange(jnp.concatenate([up_t, down_t], axis=1), GROUP_AXES)
+    input_grad = input_grad_pass(layer_input, grad_middle, gx_parts)
+    layer_output, squares_b = final_pass(middle, (mlp_parts[0], mlp_1, mlp_2, mlp_3))
+    both_back, input_grad, out_term, squares_b = together(
+        both_back, input_grad, out_term, squares_b
+    )
+    up_back, down_back = jnp.split(both_back, 2, axis=1)
+
+    squares = jnp.sum(jnp.concatenate([squares_a, squares_b], axis=0), axis=1)
+    lanes = jnp.zeros((1, 128), jnp.float32).at[0, :5].set(squares)
+    gathered = exchange(jnp.broadcast_to(lanes, (ndev, 128)), ALL_AXES)
+    out_sum = exchange(out_term, PLANE_AXES)
+    def plane_sum(arrived, cols):
+        return jnp.sum(wide(arrived.reshape(nz, plane, d_rows, cols)), axis=0).transpose(1, 0, 2)
+
+    qkv_sum = plane_sum(qkv_sum, own_cols)
+    qkv_sum = jnp.concatenate(
+        [
+            qkv_sum[:, :, :q_cols].reshape(d_rows, -1),
+            qkv_sum[:, :, q_cols : q_cols + kv_cols].reshape(d_rows, -1),
+            qkv_sum[:, :, q_cols + kv_cols :].reshape(d_rows, -1),
+        ],
+        axis=1,
+    )
+    qkv_grad = qkv_sum * gain_a
+    attn_gain_grad = jnp.sum(qkv_sum * wide(qkv_weight), axis=1)
+    gate_up_grad, gain_sum = unpack_pass(gain_m, gate_up_weight, gate_back, up_back, hgroups)
+    down_back = down_back.reshape(hgroups, mlp_rows, hchunk)
+    down_grad = wide(down_back.transpose(1, 0, 2).reshape(mlp_rows, ff_local))
+    gain_halves = gain_sum.reshape(2, -1)
+    gain_keep = jnp.where(x_at == 0, gain_halves[0], gain_halves[1])
+    gain_send = jnp.where(x_at == 0, gain_halves[1], gain_halves[0])
+    mlp_gain_grad = gain_keep + swap(gain_send[None, :], "uly")[0]
+
+    out_sum = wide(out_sum).reshape(plane, d_rows, q_cols).transpose(1, 0, 2)
+    out_weight_grad = out_sum.reshape(d_rows, -1)
+    rms_values = jnp.sqrt(jnp.sum(gathered, axis=0)[:5] / (tok * ndev * D))
+    return (
+        layer_output,
+        input_grad,
+        qkv_grad,
+        out_weight_grad,
+        gate_up_grad,
+        down_grad,
+        attn_gain_grad,
+        mlp_gain_grad,
+        rms_values,
+    )
+
+
 def solution(mesh):
+    sizes = dict(mesh.shape)
+    if sizes["blk"] == 4 and sizes["uly"] == 2:
+        mesh = Mesh(mesh.devices.reshape(sizes["dp"], 2, 2, 2), ALL_AXES)
+        body, blk = plane_plan, ("yy", "cc")
+    else:
+        body, blk = general_plan, ("blk",)
+    every = ("dp", *blk, "uly")
+    rows = ("dp", *blk)
     return jax.shard_map(
-        per_device,
+        body,
         mesh=mesh,
         in_specs=(
-            P(("dp", "blk", "uly"), None),
+            P(every, None),
             P("dp", None),
-            P(("dp", "blk", "uly"), None),
-            P(("dp", "blk", "uly"), None),
-            P(("dp", "blk"), None, "uly"),
-            P(("dp", "blk"), "uly"),
-            P(("dp", "blk", "uly")),
-            P(("dp", "blk", "uly")),
-            P(("dp", "blk", "uly"), None),
+            P(every, None),
+            P(every, None),
+            P(rows, None, "uly"),
+            P(rows, "uly"),
+            P(every),
+            P(every),
+            P(every, None),
         ),
         out_specs=(
-            P(("dp", "blk", "uly"), None),
-            P(("dp", "blk", "uly"), None),
-            P(("dp", "blk", "uly"), None),
-            P(("dp", "blk", "uly"), None),
-            P(("dp", "blk"), None, "uly"),
-            P(("dp", "blk"), "uly"),
-            P(("dp", "blk", "uly")),
-            P(("dp", "blk", "uly")),
+            P(every, None),
+            P(every, None),
+            P(every, None),
+            P(every, None),
+            P(rows, None, "uly"),
+            P(rows, "uly"),
+            P(every),
+            P(every),
             P(),
         ),
         check_vma=False,

time: 2780 us -> 718 us (0.26)
  waiting for transfers between devices: 2280 us -> 381 us
  matrix products: 170 us -> 0 us
  Pallas kernels: 0 us -> 159 us
  blocking collectives: 110 us -> 0 us
  starting transfers between devices: 19.7 us -> 93 us
  local copies, waits for them, and re-layouts: 103 us -> 32.5 us
  other arithmetic: 66.1 us -> 28.1 us
    reduce_scatter x6 -> x4, waiting for transfers between devices: 1080 us -> 34.6 us  [the longest x1 34.6 us: plane_plan(): out_term = lax.psum_scatter(out_term, 'dp', scatter_dimension=0, tiled=True)]
    unnamed x16 -> x8, waiting for transfers between devices: 716 us -> 1.82 us
    all_gather x8 -> x4, waiting for transfers between devices: 454 us -> 0.02 us  [the longest x3 0.02 us: spread(): return lax.all_gather(here, SIDE_AXES, axis=0, tiled=True)]
    ppermute x0 -> x46, waiting for transfers between devices: none -> 292 us  [the longest x34 152 us: swap(): return lax.ppermute(values, axes if len(axes) > 1 else axes[0], pairs)]
    dot_general x40 -> x0, matrix products: 170 us -> none  [the longest x3 33.3 us: contract_rows(): lax.dot_general(left_side, right_side, (((0,), (0,)), ((), ())), preferre...]
    pallas_call x0 -> x18, Pallas kernels: none -> 159 us  [the longest x5 39.1 us: term_pass(): pl.pallas_call(term_body, grid=(row_parts, col_parts), out_shape=low_shap...]
    unnamed x2 -> x0, blocking collectives: 84.3 us -> none
    ppermute x0 -> x46, starting transfers between devices: none -> 52.8 us  [the longest x12 30.9 us: shift(): lax.ppermute(values, 'dp', [(i, (i + by) % count) for i in range(count)])]
  transfers between devices with their start and end apart: 20 -> 64, of which waited for: 17 -> 35; matrix products, arithmetic and copies ran while one was open for 9% -> 5% of each run, Pallas kernels for 0% -> 21%
where the time goes in v2:
time: 718 us; the launch traced here: 709 us
  waiting for transfers between devices  381 us (53%)
  Pallas kernels  159 us (22%)
  starting transfers between devices  93 us (13%)
  local copies, waits for them, and re-layouts  32.5 us (5%)
  other arithmetic  28.1 us (4%)
  between operations  15.3 us (2%)
    ppermute x34, waiting for transfers between devices, swap(): return lax.ppermute(values, axes if len(axes) > 1 else axes[0], pairs)  152 us
    ppermute x12, waiting for transfers between devices, shift(): lax.ppermute(values, 'dp', [(i, (i + by) % count) for i in range(count)])  140 us
    all_to_all x10, waiting for transfers between devices, exchange(): return lax.all_to_all(values, axes, split_axis=0, concat_axis=0, tiled=True)  52.4 us
    all_to_all x10, starting transfers between devices, exchange(): return lax.all_to_all(values, axes, split_axis=0, concat_axis=0, tiled=True)  39.6 us
    pallas_call x5, Pallas kernels, term_pass(): pl.pallas_call(term_body, grid=(row_parts, col_parts), out_shape=low_shap...  39.1 us
    reduce_scatter x1, waiting for transfers between devices, plane_plan(): out_term = lax.psum_scatter(out_term, 'dp', scatter_dimension=0, tiled=True)  34.6 us
    ppermute x12, starting transfers between devices, shift(): lax.ppermute(values, 'dp', [(i, (i + by) % count) for i in range(count)])  30.9 us
    pallas_call x1, Pallas kernels, grad_hidden_pass(): pl.pallas_call(grad_hidden_body, grid=(steps,), out_shape=(low_shape(rows...  22.6 us
  transfers between devices with their start and end apart: 64, of which 35 were waited for; matrix products, arithmetic and copies ran while one was open for 5% of the time, Pallas kernels for 21%

profile of v2, /device:TPU:0, one launch (start us, length us, event | category | flops | bytes accessed | tf_op | source)
XLA Modules:
  0.0 708.6 jit_solution(6486007240425937290)
XLA Ops:
  54.9 10.1 %collective-permute-done.2.refs_2_ = bf16[128,2048]{1,0:T(8,128)(2,1)S(1)} collective-permute-done((bf16[128,2048]{1,0:T(8,128)(2,1)S(1)}, bf16[128,2048]{1,0:T(8,128)(2,1)S(1)}, u32[]{:S(2)}, u32[]{:S(2)}) %collective-permute-start.2) | collective-permute-done | bytes 524320 | tf_op jit(solution)/shard_map/ppermute | solution.py:848
  66.7 9.6 %all-to-all-done.1 = bf16[8,128,512]{2,1,0:T(8,128)(2,1)S(1)} async-done(((bf16[8,128,512]{2,1,0:T(8,128)(2,1)}), bf16[8,128,512]{2,1,0:T(8,128)(2,1)S(1)}, u32[]{:S(2)}, u32[]{:S(2)}) %all-to-all-start.1) | async-done | bytes 1048608 | tf_op jit(solution)/shard_map/all_to_all | solution.py:835
  85.5 44.9 %collective-permute-done.8.refs_1_ = bf16[128,2048]{1,0:T(8,128)(2,1)} collective-permute-done((bf16[128,2048]{1,0:T(8,128)(2,1)}, bf16[128,2048]{1,0:T(8,128)(2,1)}, u32[]{:S(2)}, u32[]{:S(2)}) %collective-permute-start.8) | collective-permute-done | bytes 524320 | tf_op jit(solution)/shard_map/ppermute | solution.py:861
  130.3 9.9 %all-to-all-done.2 = bf16[32,64,512]{2,1,0:T(8,128)(2,1)S(1)} async-done(((bf16[32,64,512]{2,1,0:T(8,128)(2,1)}), bf16[32,64,512]{2,1,0:T(8,128)(2,1)S(1)}, u32[]{:S(2)}, u32[]{:S(2)}) %all-to-all-start.2) | async-done | bytes 2097184 | tf_op jit(solution)/shard_map/all_to_all | solution.py:835
  148.8 13.8 %attention_forward.1 = (bf16[1024,256]{1,0:T(8,128)(2,1)}, bf16[1024,128]{1,0:T(8,128)(2,1)}, bf16[1024,128]{1,0:T(8,128)(2,1)}, bf16[1024,256]{1,0:T(8,128)(2,1)}) custom-call(bf16[2048,512]{1,0:T(8,128)(2,1)} %bitcast.114, f32[1024,128]{1,0:T(8,128)} %get-tuple-element.203.cosine, f32[1024,128]{1,0:T(8,128)} %get-tuple-element.204.sine, ...), custom_call_target="tpu_custom_call" | custom-call | flops 1000 | bytes 1000 | tf_op jit(solution)/shard_map/attention_forward/pallas_call | solution.py:450
  195.8 11.0 %collective-permute-done.10.refs_1_ = bf16[128,2048]{1,0:T(8,128)(2,1)S(1)} collective-permute-done((bf16[128,2048]{1,0:T(8,128)(2,1)}, bf16[128,2048]{1,0:T(8,128)(2,1)S(1)}, u32[]{:S(2)}, u32[]{:S(2)}) %collective-permute-start.10) | collective-permute-done | bytes 524320 | tf_op jit(solution)/shard_map/ppermute | solution.py:848
  212.5 17.2 %collective-permute-done.12.refs_3_ = bf16[128,2048]{1,0:T(8,128)(2,1)S(1)} collective-permute-done((bf16[128,2048]{1,0:T(8,128)(2,1)}, bf16[128,2048]{1,0:T(8,128)(2,1)S(1)}, u32[]{:S(2)}, u32[]{:S(2)}) %collective-permute-start.12) | collective-permute-done | bytes 524320 | tf_op jit(solution)/shard_map/ppermute | solution.py:848
  239.9 11.1 %collective-permute-done.14.refs_1_ = bf16[128,2048]{1,0:T(8,128)(2,1)S(1)} collective-permute-done((bf16[128,2048]{1,0:T(8,128)(2,1)}, bf16[128,2048]{1,0:T(8,128)(2,1)S(1)}, u32[]{:S(2)}, u32[]{:S(2)}) %collective-permute-start.14) | collective-permute-done | bytes 524320 | tf_op jit(solution)/shard_map/ppermute | solution.py:861
  251.1 20.4 %collective-permute-done.15.refs_2_ = bf16[128,2048]{1,0:T(8,128)(2,1)S(1)} collective-permute-done((bf16[128,2048]{1,0:T(8,128)(2,1)}, bf16[128,2048]{1,0:T(8,128)(2,1)S(1)}, u32[]{:S(2)}, u32[]{:S(2)}) %collective-permute-start.15) | collective-permute-done | bytes 524320 | tf_op jit(solution)/shard_map/ppermute | solution.py:861
  275.8 10.2 %collective-permute-start.21 = (bf16[128,2048]{1,0:T(8,128)(2,1)}, bf16[128,2048]{1,0:T(8,128)(2,1)S(1)}, u32[]{:S(2)}, u32[]{:S(2)}) collective-permute-start(bf16[128,2048]{1,0:T(8,128)(2,1)} %slice_dynamic-update-slice_fusion.refs_0_), channel_id=1, source_target_pairs={{0,16},{8,24},{16,0},{24,8},{1,17},{9,25},{17,1},{25,9},{2,18},{10... | collective-permute-start | bytes 1572872 | tf_op jit(solution)/shard_map/ppermute | solution.py:861
  286.1 15.9 %hidden_pass.1 = (bf16[1024,1024]{1,0:T(8,128)(2,1)}, bf16[1024,1024]{1,0:T(8,128)(2,1)}, bf16[1024,1024]{1,0:T(8,128)(2,1)}) custom-call(bf16[4096,512]{1,0:T(8,128)(2,1)} %all-gather.7.cloned.1.call-done.gate_w, bf16[4096,512]{1,0:T(8,128)(2,1)} %all-gather.9.cloned.1.call-done.up_w, bf16[128,2048]{1,0:T(8,128)(2,1)} %get-tuple-element.244.refs_0_, ...), custom_call_target="tpu_custom_call" | custom-call | flops 1000 | bytes 1000 | tf_op jit(solution)/shard_map/hidden_pass/pallas_call | solution.py:590
  310.7 9.3 %down_pass.1 = (bf16[512,2048]{1,0:T(8,128)(2,1)}, bf16[512,2048]{1,0:T(8,128)(2,1)}) custom-call(bf16[1024,1024]{1,0:T(8,128)(2,1)} %get-tuple-element.265.rows.refs_8_, bf16[4096,512]{1,0:T(8,128)(2,1)} %all-gather.11.cloned.1.call-done.weight.down_w), custom_call_target="tpu_custom_call" | custom-call | flops 1000 | bytes 1000 | tf_op jit(solution)/shard_map/down_pass/pallas_call | solution.py:549
  321.4 22.6 %grad_hidden_pass.1 = (bf16[1024,1024]{1,0:T(8,128)(2,1)}, bf16[1024,1024]{1,0:T(8,128)(2,1)}, bf16[512,2048]{1,0:T(8,128)(2,1)}, bf16[512,2048]{1,0:T(8,128)(2,1)}) custom-call(bf16[4096,512]{1,0:T(8,128)(2,1)} %all-gather.7.cloned.1.call-done.gate_w, bf16[4096,512]{1,0:T(8,128)(2,1)} %all-gather.9.cloned.1.call-done.up_w, ...), custom_call_target="tpu_custom_call" | custom-call | flops 1000 | bytes 1000 | tf_op jit(solution)/shard_map/grad_hidden_pass/pallas_call | solution.py:629
  344.2 9.1 %term_pass.5 = bf16[4096,512]{1,0:T(8,128)(2,1)} custom-call(bf16[128,2048]{1,0:T(8,128)(2,1)} %get-tuple-element.244.refs_0_, bf16[128,2048]{1,0:T(8,128)(2,1)} %copy-done.5, bf16[128,2048]{1,0:T(8,128)(2,1)} %copy-done.6, bf16[128,2048]{1,0:T(8,128)(2,1)} %copy-done.7, bf16[128,2048]{1,0:T(8,128)(2,1)} %copy-done.8, bf16[128,2048]{1,0:T(8,128)(2,1)} %copy-done.9, ...), custom_call_target="tpu_custom_call" | custom-call | flops 1000 | bytes 1000 | tf_op jit(solution)/shard_map/term_pass/pallas_call | solution.py:652
  366.1 9.7 %term_pass.6 = bf16[4096,512]{1,0:T(8,128)(2,1)} custom-call(bf16[128,2048]{1,0:T(8,128)(2,1)} %get-tuple-element.244.refs_0_, bf16[128,2048]{1,0:T(8,128)(2,1)} %copy-done.5, bf16[128,2048]{1,0:T(8,128)(2,1)} %copy-done.6, bf16[128,2048]{1,0:T(8,128)(2,1)} %copy-done.7, bf16[128,2048]{1,0:T(8,128)(2,1)} %copy-done.8, bf16[128,2048]{1,0:T(8,128)(2,1)} %copy-done.9, ...), custom_call_target="tpu_custom_call" | custom-call | flops 1000 | bytes 1000 | tf_op jit(solution)/shard_map/term_pass/pallas_call | solution.py:652
  392.2 32.0 %collective-permute-done.29.refs_2_ = bf16[128,2048]{1,0:T(8,128)(2,1)S(1)} collective-permute-done((bf16[128,2048]{1,0:T(8,128)(2,1)}, bf16[128,2048]{1,0:T(8,128)(2,1)S(1)}, u32[]{:S(2)}, u32[]{:S(2)}) %collective-permute-start.29) | collective-permute-done | bytes 524320 | tf_op jit(solution)/shard_map/ppermute | solution.py:861
  434.5 20.2 %collective-permute-done.31.refs_1_ = bf16[128,2048]{1,0:T(8,128)(2,1)S(1)} collective-permute-done((bf16[128,2048]{1,0:T(8,128)(2,1)}, bf16[128,2048]{1,0:T(8,128)(2,1)S(1)}, u32[]{:S(2)}, u32[]{:S(2)}) %collective-permute-start.31) | collective-permute-done | bytes 524320 | tf_op jit(solution)/shard_map/ppermute | solution.py:848
  461.3 14.7 %collective-permute-done.33.refs_3_ = bf16[128,2048]{1,0:T(8,128)(2,1)S(1)} collective-permute-done((bf16[128,2048]{1,0:T(8,128)(2,1)}, bf16[128,2048]{1,0:T(8,128)(2,1)S(1)}, u32[]{:S(2)}, u32[]{:S(2)}) %collective-permute-start.33) | collective-permute-done | bytes 524320 | tf_op jit(solution)/shard_map/ppermute | solution.py:848
  489.3 17.0 %attention_backward.1.rows.refs_8_ = bf16[1024,512]{1,0:T(8,128)(2,1)} custom-call(bf16[2048,256]{1,0:T(8,128)(2,1)} %all-gather.5.cloned.1.call-done.weight, bf16[1024,256]{1,0:T(8,128)(2,1)} %get-tuple-element.300.query, bf16[1024,128]{1,0:T(8,128)(2,1)} %get-tuple-element.301.key, bf16[1024,128]{1,0:T(8,128)(2,1)} %get-tuple-element.302.value, ...), custom_call_target="tpu_custom_call" | custom-call | flops 1000 | bytes 1000 | tf_op jit(solution)/shard_map/attention_backward/pallas_call | solution.py:501
  519.5 15.2 %collective-permute-done.40.refs_2_ = bf16[128,2048]{1,0:T(8,128)(2,1)} collective-permute-done((bf16[128,2048]{1,0:T(8,128)(2,1)}, bf16[128,2048]{1,0:T(8,128)(2,1)}, u32[]{:S(2)}, u32[]{:S(2)}) %collective-permute-start.40) | collective-permute-done | bytes 524320 | tf_op jit(solution)/shard_map/ppermute | solution.py:861
  551.7 32.0 %collective-permute-done.42.refs_1_ = bf16[128,2048]{1,0:T(8,128)(2,1)S(1)} collective-permute-done((bf16[128,2048]{1,0:T(8,128)(2,1)}, bf16[128,2048]{1,0:T(8,128)(2,1)S(1)}, u32[]{:S(2)}, u32[]{:S(2)}) %collective-permute-start.42) | collective-permute-done | bytes 524320 | tf_op jit(solution)/shard_map/ppermute | solution.py:848
  585.3 13.4 %collective-permute-done.44.refs_3_ = bf16[128,2048]{1,0:T(8,128)(2,1)} collective-permute-done((bf16[128,2048]{1,0:T(8,128)(2,1)}, bf16[128,2048]{1,0:T(8,128)(2,1)}, u32[]{:S(2)}, u32[]{:S(2)}) %collective-permute-start.44) | collective-permute-done | bytes 524320 | tf_op jit(solution)/shard_map/ppermute | solution.py:848
  619.1 34.6 %reduce-scatter.11.cloned.1.call-done = bf16[512,256]{1,0:T(8,128)(2,1)} async-done(((bf16[2048,256]{1,0:T(8,128)(2,1)}), bf16[512,256]{1,0:T(8,128)(2,1)}) %reduce-scatter.11.cloned.1.call-update) | async-done | bytes 262160 | tf_op jit(solution)/shard_map/reduce_scatter | solution.py:1038
  653.6 19.8 %all-to-all-done.7 = bf16[8,128,1024]{2,1,0:T(8,128)(2,1)S(1)} async-done(((bf16[8,128,1024]{2,1,0:T(8,128)(2,1)}), bf16[8,128,1024]{2,1,0:T(8,128)(2,1)S(1)}, u32[]{:S(2)}, u32[]{:S(2)}) %all-to-all-start.7) | async-done | bytes 2097184 | tf_op jit(solution)/shard_map/all_to_all | solution.py:835
  (309 shorter events, 269.4 us)
Async XLA Ops:
  30.6 45.8 %all-to-all-start.1 = ((bf16[8,128,512]{2,1,0:T(8,128)(2,1)}), bf16[8,128,512]{2,1,0:T(8,128)(2,1)S(1)}, u32[]{:S(2)}, u32[]{:S(2)}) async-start(bf16[8,128,512]{2,1,0:T(8,128)(2,1)} %bitcast.131), calls=%async_computation.1 | async-start | bytes 2097152 | tf_op jit(solution)/shard_map/all_to_all | solution.py:835
  35.5 127.1 %all-gather.5.cloned.1.call-start = ((), (), s32[]{:S(2)}) async-start(), calls=%async_computation.14 | async-start | bytes 1310720 | tf_op jit(solution)/shard_map/all_gather | solution.py:945
  36.2 203.7 %all-gather.7.cloned.1.call-start = ((), (), s32[]{:S(2)}) async-start(), calls=%async_computation.15 | async-start | bytes 5242880 | tf_op jit(solution)/shard_map/all_gather | solution.py:953
  77.4 62.8 %all-to-all-start.2 = ((bf16[32,64,512]{2,1,0:T(8,128)(2,1)}), bf16[32,64,512]{2,1,0:T(8,128)(2,1)S(1)}, u32[]{:S(2)}, u32[]{:S(2)}) async-start(bf16[32,64,512]{2,1,0:T(8,128)(2,1)} %bitcast.116), calls=%async_computation.2 | async-start | bytes 4194304 | tf_op jit(solution)/shard_map/all_to_all | solution.py:835
  81.3 49.1 %collective-permute-start.8 = (bf16[128,2048]{1,0:T(8,128)(2,1)}, bf16[128,2048]{1,0:T(8,128)(2,1)}, u32[]{:S(2)}, u32[]{:S(2)}) collective-permute-start(bf16[128,2048]{1,0:T(8,128)(2,1)} %slice_dynamic-update-slice_fusion.refs_0_), channel_id=1, source_target_pairs={{0,8},{8,16},{16,24},{24,0},{1,9},{9,17},{17,25},{25,1},{2,10},{10... | collective-permute-start | bytes 1572872 | tf_op jit(solution)/shard_map/ppermute | solution.py:861
  143.8 127.8 %all-gather.9.cloned.1.call-start = ((), (), s32[]{:S(2)}) async-start(), calls=%async_computation.16 | async-start | bytes 5242880 | tf_op jit(solution)/shard_map/all_gather | solution.py:953
  185.0 44.6 %all-to-all-start.4 = ((bf16[8,128,512]{2,1,0:T(8,128)(2,1)}), bf16[8,128,512]{2,1,0:T(8,128)(2,1)S(1)}, u32[]{:S(2)}, u32[]{:S(2)}) async-start(bf16[8,128,512]{2,1,0:T(8,128)(2,1)} %bitcast.21), calls=%async_computation.4 | async-start | bytes 2097152 | tf_op jit(solution)/shard_map/all_to_all | solution.py:835
  188.6 121.1 %all-gather.11.cloned.1.call-start = ((), (), s32[]{:S(2)}) async-start(), calls=%async_computation.17 | async-start | bytes 5242880 | tf_op jit(solution)/shard_map/all_gather | solution.py:953
  191.7 38.0 %collective-permute-start.12 = (bf16[128,2048]{1,0:T(8,128)(2,1)}, bf16[128,2048]{1,0:T(8,128)(2,1)S(1)}, u32[]{:S(2)}, u32[]{:S(2)}) collective-permute-start(bf16[128,2048]{1,0:T(8,128)(2,1)} %get-tuple-element.225), channel_id=1, source_target_pairs={{0,5},{1,4},{4,1},{5,0},{2,7},{3,6},{6,3},{7,2},{8,13},{9,12},{12,... | collective-permute-start | bytes 1572872 | tf_op jit(solution)/shard_map/ppermute | solution.py:848
  192.2 37.5 %collective-permute-start.13 = (bf16[128,2048]{1,0:T(8,128)(2,1)}, bf16[128,2048]{1,0:T(8,128)(2,1)S(1)}, u32[]{:S(2)}, u32[]{:S(2)}) collective-permute-start(bf16[128,2048]{1,0:T(8,128)(2,1)} %slice_dynamic-update-slice_fusion.refs_0_), channel_id=1, source_target_pairs={{0,24},{8,0},{16,8},{24,16},{1,25},{9,1},{17,9},{25,17},{2,26},{10... | collective-permute-start | bytes 1572872 | tf_op jit(solution)/shard_map/ppermute | solution.py:861
  230.7 251.2 %reduce-scatter.5.cloned.1.call-start = ((), (), s32[]{:S(2)}) async-start(), calls=%async_computation.18 | async-start | bytes 5242880 | tf_op jit(solution)/shard_map/reduce_scatter | solution.py:996
  357.0 177.7 %reduce-scatter.7.cloned.1.call-start = ((), (), s32[]{:S(2)}) async-start(), calls=%async_computation.19 | async-start | bytes 5242880 | tf_op jit(solution)/shard_map/reduce_scatter | solution.py:996
  379.5 44.8 %collective-permute-start.29 = (bf16[128,2048]{1,0:T(8,128)(2,1)}, bf16[128,2048]{1,0:T(8,128)(2,1)S(1)}, u32[]{:S(2)}, u32[]{:S(2)}) collective-permute-start(bf16[128,2048]{1,0:T(8,128)(2,1)} %get-tuple-element.285), channel_id=1, source_target_pairs={{0,16},{8,24},{16,0},{24,8},{1,17},{9,25},{17,1},{25,9},{2,18},{10... | collective-permute-start | bytes 1572872 | tf_op jit(solution)/shard_map/ppermute | solution.py:861
  379.5 44.8 %collective-permute-start.30 = (bf16[128,2048]{1,0:T(8,128)(2,1)}, bf16[128,2048]{1,0:T(8,128)(2,1)}, u32[]{:S(2)}, u32[]{:S(2)}) collective-permute-start(bf16[128,2048]{1,0:T(8,128)(2,1)} %get-tuple-element.286), channel_id=1, source_target_pairs={{0,8},{8,16},{16,24},{24,0},{1,9},{9,17},{17,25},{25,1},{2,10},{10... | collective-permute-start | bytes 1572872 | tf_op jit(solution)/shard_map/ppermute | solution.py:861
  431.6 44.4 %collective-permute-start.33 = (bf16[128,2048]{1,0:T(8,128)(2,1)}, bf16[128,2048]{1,0:T(8,128)(2,1)S(1)}, u32[]{:S(2)}, u32[]{:S(2)}) collective-permute-start(bf16[128,2048]{1,0:T(8,128)(2,1)} %get-tuple-element.309.refs_0_), channel_id=1, source_target_pairs={{0,5},{1,4},{4,1},{5,0},{2,7},{3,6},{6,3},{7,2},{8,13},{9,12},{12,... | collective-permute-start | bytes 1572872 | tf_op jit(solution)/shard_map/ppermute | solution.py:848
  432.5 43.6 %collective-permute-start.34 = (bf16[128,2048]{1,0:T(8,128)(2,1)S(1)}, bf16[128,2048]{1,0:T(8,128)(2,1)S(1)}, u32[]{:S(2)}, u32[]{:S(2)}) collective-permute-start(bf16[128,2048]{1,0:T(8,128)(2,1)S(1)} %get-tuple-element.296), channel_id=1, source_target_pairs={{0,24},{8,0},{16,8},{24,16},{1,25},{9,1},{17,9},{25,17},{2,26},{10... | collective-permute-start | bytes 1572872 | tf_op jit(solution)/shard_map/ppermute | solution.py:861
  432.5 43.6 %collective-permute-start.35 = (bf16[128,2048]{1,0:T(8,128)(2,1)S(1)}, bf16[128,2048]{1,0:T(8,128)(2,1)S(1)}, u32[]{:S(2)}, u32[]{:S(2)}) collective-permute-start(bf16[128,2048]{1,0:T(8,128)(2,1)S(1)} %get-tuple-element.297), channel_id=1, source_target_pairs={{0,8},{8,16},{16,24},{24,0},{1,9},{9,17},{17,25},{25,1},{2,10},{10... | collective-permute-start | bytes 1572872 | tf_op jit(solution)/shard_map/ppermute | solution.py:861
  481.9 52.8 %all-to-all-start.5 = ((bf16[8,128,512]{2,1,0:T(8,128)(2,1)}), bf16[8,128,512]{2,1,0:T(8,128)(2,1)S(1)}, u32[]{:S(2)}, u32[]{:S(2)}) async-start(bf16[8,128,512]{2,1,0:T(8,128)(2,1)} %bitcast.129), calls=%async_computation.6 | async-start | bytes 2097152 | tf_op jit(solution)/shard_map/all_to_all | solution.py:835
  485.5 113.2 %reduce-scatter.9.cloned.1.call-start = ((), (), s32[]{:S(2)}) async-start(), calls=%async_computation.20 | async-start | bytes 5242880 | tf_op jit(solution)/shard_map/reduce_scatter | solution.py:996
  486.3 48.4 %collective-permute-start.40 = (bf16[128,2048]{1,0:T(8,128)(2,1)}, bf16[128,2048]{1,0:T(8,128)(2,1)}, u32[]{:S(2)}, u32[]{:S(2)}) collective-permute-start(bf16[128,2048]{1,0:T(8,128)(2,1)} %get-tuple-element.319), channel_id=1, source_target_pairs={{0,16},{8,24},{16,0},{24,8},{1,17},{9,25},{17,1},{25,9},{2,18},{10... | collective-permute-start | bytes 1572872 | tf_op jit(solution)/shard_map/ppermute | solution.py:861
  543.4 55.4 %all-to-all-start.6 = ((bf16[32,64,512]{2,1,0:T(8,128)(2,1)}), bf16[32,64,512]{2,1,0:T(8,128)(2,1)S(1)}, u32[]{:S(2)}, u32[]{:S(2)}) async-start(bf16[32,64,512]{2,1,0:T(8,128)(2,1)} %bitcast.25), calls=%async_computation.8 | async-start | bytes 4194304 | tf_op jit(solution)/shard_map/all_to_all | solution.py:835
  551.5 47.2 %collective-permute-start.44 = (bf16[128,2048]{1,0:T(8,128)(2,1)}, bf16[128,2048]{1,0:T(8,128)(2,1)}, u32[]{:S(2)}, u32[]{:S(2)}) collective-permute-start(bf16[128,2048]{1,0:T(8,128)(2,1)} %get-tuple-element.332), channel_id=1, source_target_pairs={{0,5},{1,4},{4,1},{5,0},{2,7},{3,6},{6,3},{7,2},{8,13},{9,12},{12,... | collective-permute-start | bytes 1572872 | tf_op jit(solution)/shard_map/ppermute | solution.py:848
  602.3 71.2 %all-to-all-start.7 = ((bf16[8,128,1024]{2,1,0:T(8,128)(2,1)}), bf16[8,128,1024]{2,1,0:T(8,128)(2,1)S(1)}, u32[]{:S(2)}, u32[]{:S(2)}) async-start(bf16[8,128,1024]{2,1,0:T(8,128)(2,1)} %bitcast.119), calls=%async_computation.10 | async-start | bytes 4194304 | tf_op jit(solution)/shard_map/all_to_all | solution.py:835
  607.6 46.1 %reduce-scatter.11.cloned.1.call-start = ((), (), s32[]{:S(2)}) async-start(), calls=%async_computation.21 | async-start | bytes 1310720 | tf_op jit(solution)/shard_map/reduce_scatter | solution.py:1038
  (94 other events, 1335.0 us)
Sparse Core Ops, SparseCore 0:
  37.9 41.3 all-gather.4
  81.2 66.2 all-gather.6
  171.4 66.7 all-gather.8
  239.9 52.9 all-gather.10
  357.2 53.5 reduce-scatter.4
  424.4 73.6 reduce-scatter.6
  501.0 56.9 reduce-scatter.8
  610.8 42.8 reduce-scatter.10

commit v3 on v2

--- a/solution.py
+++ b/solution.py
@@ -413,8 +413,8 @@
     allowed = key_pos <= query_pos
     scores = jnp.where(allowed, scores, MASKED)
     top = jnp.max(scores, axis=1, keepdims=True)
-    weights = jnp.where(allowed, jnp.exp(scores - top), 0.0)
-    return weights / jnp.sum(weights, axis=1, keepdims=True)
+    weights = jnp.exp(scores - top)
+    return weights * (1.0 / jnp.sum(weights, axis=1, keepdims=True))
 
 
 def attention_forward_body(group, weight, cosine, sine, pos_col, pos_row, *refs):
@@ -445,8 +445,8 @@
     lax.fori_loop(0, steps, attend, 0)
 
 
-def attention_forward(pieces, weight, cosine, sine, positions):
-    rows, group = positions.shape[0], weight.shape[1] // HD - 2
+def attention_forward(pieces, weight, cosine, sine, pos_col, pos_row):
+    rows, group = pos_col.shape[0], weight.shape[1] // HD - 2
     return pl.pallas_call(
         functools.partial(attention_forward_body, group),
         out_shape=(
@@ -460,7 +460,7 @@
         scratch_shapes=[pltpu.VMEM((rows, weight.shape[0]), jnp.bfloat16)],
         name="attention_forward",
         **KERNEL,
-    )(weight, cosine, sine, positions[:, None], positions[None, :], *pieces)
+    )(weight, cosine, sine, pos_col, pos_row, *pieces)
 
 
 def attention_backward_body(group, weight, query, key, value, cosine, sine, pos_col, pos_row, *refs):
@@ -496,7 +496,7 @@
     lax.fori_loop(0, steps, finish, 0)
 
 
-def attention_backward(pieces, weight, query, key, value, cosine, sine, positions):
+def attention_backward(pieces, weight, query, key, value, cosine, sine, pos_col, pos_row):
     rows, group = query.shape[0], query.shape[1] // HD
     return pl.pallas_call(
         functools.partial(attention_backward_body, group),
@@ -507,76 +507,76 @@
         + [pltpu.VMEM((rows, HD), jnp.float32)] * 2,
         name="attention_backward",
         **KERNEL,
-    )(weight, query, key, value, cosine, sine, positions[:, None], positions[None, :], *pieces)
-
-
-def halves_specs(steps, rows, cols):
-    half = steps // 2
-    return (
-        pl.BlockSpec((rows, cols), lambda i: (jnp.minimum(i, half - 1), 0)),
-        pl.BlockSpec((rows, cols), lambda i: (jnp.maximum(i - half, 0), 0)),
-    )
-
-
-def store_half(first, second, values):
-    step, half = pl.program_id(0), pl.num_programs(0) // 2
-
-    @pl.when(step < half)
-    def _():
-        first[...] = values
-
-    @pl.when(step >= half)
-    def _():
-        second[...] = values
-
-
-def by_cols_body(parts, rows, weight, first, second):
-    depth, chunk = weight.shape[0] // parts**2, weight.shape[1]
-    out = []
-    for y in range(parts):
-        total = 0.0
-        for x in range(parts):
-            at = (y * parts + x) * depth
-            cut = slice(x * chunk, (x + 1) * chunk)
-            total += dot32(rows[:, cut], weight[at : at + depth, :], BY_COLS)
-        out.append(low(total))
-    store_half(first, second, out[0] if parts == 1 else jnp.concatenate(out, axis=1))
-
-
-def by_cols_pass(rows, weight, parts, name):
-    count, width = rows.shape[0], weight.shape[0] // parts
-    steps = count // ROWS
+    )(weight, query, key, value, cosine, sine, pos_col, pos_row, *pieces)
+
+
+def stripes(weight, parts, number):
+    depth = weight.shape[0] // parts**2 // ROWS
+
+    def place(x, step):
+        at = jnp.clip(step - number, 0, parts * depth - 1)
+        return ((at // depth * parts + x) * depth + at % depth, 0)
+
+    shape = (ROWS, weight.shape[1])
+    return [pl.BlockSpec(shape, functools.partial(place, x)) for x in range(parts)]
+
+
+def stripe_dot(rows, refs):
+    chunk = refs[0].shape[1]
+    total = dot32(rows[:, :chunk], refs[0][...], BY_COLS)
+    for x, ref in enumerate(refs[1:], 1):
+        total += dot32(rows[:, x * chunk : (x + 1) * chunk], ref[...], BY_COLS)
+    return total
+
+
+def store_rows(outs, values):
+    rows = outs[0].shape[0]
+    for number, out in enumerate(outs):
+        out[...] = values[number * rows : (number + 1) * rows, :]
+
+
+def by_cols_body(parts, rows, *refs):
+    store_rows(refs[parts:], low(stripe_dot(rows, refs[:parts])))
+
+
+def by_cols_pass(rows, weight, parts, blocks, name):
+    width = weight.shape[0] // parts
+    block = rows.shape[0] // blocks
     return pl.pallas_call(
         functools.partial(by_cols_body, parts),
-        grid=(steps,),
-        out_shape=(low_shape(count // 2, width),) * 2,
-        in_specs=[pl.BlockSpec((ROWS, rows.shape[1]), lambda i: (i, 0)), once(weight.shape)],
-        out_specs=halves_specs(steps, ROWS, width),
+        grid=(width // ROWS,),
+        out_shape=(low_shape(block, width),) * blocks,
+        in_specs=[once(rows.shape), *stripes(weight, parts, 0)],
+        out_specs=(pl.BlockSpec((block, ROWS), lambda step: (0, step)),) * blocks,
         name=name,
         **KERNEL,
-    )(rows, weight)
-
-
-def square_dot(rows, weight):
-    depth = weight.shape[0] // 4
-    near, far = rows[:, :depth], rows[:, depth:]
-    out = [
-        dot32(near, weight[x * depth : (x + 1) * depth, :])
-        + dot32(far, weight[(2 + x) * depth : (3 + x) * depth, :])
-        for x in (0, 1)
-    ]
-    return jnp.concatenate(out, axis=1)
-
-
-def hidden_body(gate_w, up_w, *refs):
+    )(rows, *[weight] * parts)
+
+
+def columns_of(weight):
+    shape = (weight.shape[0] // 4, weight.shape[1] // 2)
+
+    def place(y, step):
+        at = jnp.minimum(step, 3)
+        return (2 * y + at // 2, at % 2)
+
+    return [pl.BlockSpec(shape, functools.partial(place, y)) for y in (0, 1)]
+
+
+def column_dot(rows, near, far):
+    depth = near.shape[0]
+    return dot32(rows[:, :depth], near[...]) + dot32(rows[:, depth:], far[...])
+
+
+def hidden_body(gate_near, gate_far, up_near, up_far, *refs):
     normed_p, (hidden_out, gate_slope, up_slope, normed) = refs[:-4], refs[-4:]
 
     @pl.when(pl.program_id(0) == 0)
     def _():
         join_rows(normed_p, normed)
 
-    rows = normed[row_block(pl.program_id(0)), :]
-    gate, up = square_dot(rows, gate_w), square_dot(rows, up_w)
+    gate = column_dot(normed, gate_near, gate_far)
+    up = column_dot(normed, up_near, up_far)
     sig = jax.nn.sigmoid(gate)
     hidden_out[...] = low(gate * sig * up)
     gate_slope[...] = low(up * sig * (1.0 + gate * (1.0 - sig)))
@@ -586,58 +586,67 @@
 def hidden_pass(normed_p, gate_w, up_w):
     rows, width = len(normed_p) * normed_p[0].shape[0], normed_p[0].shape[1]
     units = 2 * gate_w.shape[1]
-    by_rows = pl.BlockSpec((ROWS, units), lambda i: (i, 0))
     return pl.pallas_call(
         hidden_body,
-        grid=(rows // ROWS,),
+        grid=(4,),
         out_shape=(low_shape(rows, units),) * 3,
-        in_specs=[once(v.shape) for v in (gate_w, up_w, *normed_p)],
-        out_specs=(by_rows,) * 3,
+        in_specs=columns_of(gate_w) + columns_of(up_w) + [once(v.shape) for v in normed_p],
+        out_specs=(pl.BlockSpec((rows, units // 4), lambda step: (0, step)),) * 3,
         scratch_shapes=[pltpu.VMEM((rows, width), jnp.bfloat16)],
         name="hidden_pass",
         **KERNEL,
-    )(gate_w, up_w, *normed_p)
-
-
-def grad_hidden_body(gate_w, up_w, down_w, gate_slope, up_slope, *refs):
-    cot_p, (grad_gate, grad_up, first, second, cot) = refs[:-5], refs[-5:]
-
-    @pl.when(pl.program_id(0) == 0)
+    )(gate_w, gate_w, up_w, up_w, *normed_p)
+
+
+def grad_hidden_body(down_near, down_far, gate_slope, up_slope, *refs):
+    gate_s, up_s, refs = refs[:2], refs[2:4], refs[4:]
+    count = (len(refs) - 5) // 2
+    cot_p, (grad_gate_out, grad_up_out, *outs) = refs[:count], refs[count:-3]
+    cot, grad_gate, grad_up = refs[-3:]
+    step, chunk = pl.program_id(0), grad_gate_out.shape[1]
+
+    @pl.when(step == 0)
     def _():
         join_rows(cot_p, cot)
 
-    grad_hidden = square_dot(cot[row_block(pl.program_id(0)), :], down_w)
-    grad_gate[...] = low(grad_hidden * wide(gate_slope[...]))
-    grad_up[...] = low(grad_hidden * wide(up_slope[...]))
-    depth, chunk = gate_w.shape[0] // 4, gate_w.shape[1]
-    out = []
-    for y in (0, 1):
-        total = 0.0
-        for x in (0, 1):
-            at, cut = (2 * y + x) * depth, slice(x * chunk, (x + 1) * chunk)
-            total += dot32(grad_gate[:, cut], gate_w[at : at + depth, :], BY_COLS)
-            total += dot32(grad_up[:, cut], up_w[at : at + depth, :], BY_COLS)
-        out.append(low(total))
-    store_half(first, second, jnp.concatenate(out, axis=1))
+    @pl.when(step < 4)
+    def _():
+        grad_hidden = column_dot(cot, down_near, down_far)
+        grad_gate_out[...] = low(grad_hidden * wide(gate_slope[...]))
+        grad_up_out[...] = low(grad_hidden * wide(up_slope[...]))
+
+    for number in range(4):
+
+        @pl.when(step == number)
+        def _(cut=slice(number * chunk, (number + 1) * chunk)):
+            grad_gate[:, cut] = grad_gate_out[...]
+            grad_up[:, cut] = grad_up_out[...]
+
+    @pl.when(step >= 4)
+    def _():
+        store_rows(outs, low(stripe_dot(grad_gate, gate_s) + stripe_dot(grad_up, up_s)))
 
 
 def grad_hidden_pass(cot_p, gate_slope, up_slope, gate_w, up_w, down_w):
     rows, width = len(cot_p) * cot_p[0].shape[0], cot_p[0].shape[1]
     units = 2 * gate_w.shape[1]
-    by_rows = pl.BlockSpec((ROWS, units), lambda i: (i, 0))
-    steps = rows // ROWS
+    quarter = pl.BlockSpec((rows, units // 4), lambda step: (0, jnp.minimum(step, 3)))
+    stripe = pl.BlockSpec((cot_p[0].shape[0], ROWS), lambda step: (0, jnp.maximum(step - 4, 0)))
     return pl.pallas_call(
         grad_hidden_body,
-        grid=(steps,),
-        out_shape=(low_shape(rows, units),) * 2 + (low_shape(rows // 2, width),) * 2,
-        in_specs=[once(v.shape) for v in (gate_w, up_w, down_w)]
-        + [by_rows] * 2
+        grid=(4 + width // ROWS,),
+        out_shape=(low_shape(rows, units),) * 2 + tuple(low_shape(*v.shape) for v in cot_p),
+        in_specs=columns_of(down_w)
+        + [quarter] * 2
+        + stripes(gate_w, 2, 4)
+        + stripes(up_w, 2, 4)
         + [once(v.shape) for v in cot_p],
-        out_specs=(by_rows,) * 2 + halves_specs(steps, ROWS, width),
-        scratch_shapes=[pltpu.VMEM((rows, width), jnp.bfloat16)],
+        out_specs=(quarter,) * 2 + (stripe,) * len(cot_p),
+        scratch_shapes=[pltpu.VMEM((rows, width), jnp.bfloat16)]
+        + [pltpu.VMEM((rows, units), jnp.bfloat16)] * 2,
         name="grad_hidden_pass",
         **KERNEL,
-    )(gate_w, up_w, down_w, gate_slope, up_slope, *cot_p)
+    )(down_w, down_w, gate_slope, up_slope, gate_w, gate_w, up_w, up_w, *cot_p)
 
 
 def term_body(*refs):
@@ -698,6 +707,23 @@
     return total
 
 
+def prepare_body(stream_in, cot, normed_out, cot_out):
+    rows = wide(stream_in[...])
+    normed_out[...] = low(rows * unit_scale(rows))
+    cot_out[...] = to_split(cot[...])
+
+
+def prepare_pass(stream_in, cot):
+    return pl.pallas_call(
+        prepare_body,
+        out_shape=(low_shape(*stream_in.shape), low_shape(*cot.shape)),
+        in_specs=[VMEM_SPEC] * 2,
+        out_specs=(VMEM_SPEC,) * 2,
+        name="prepare_pass",
+        **KERNEL,
+    )(stream_in, cot)
+
+
 def middle_body(stream_in, *refs):
     parts, (middle_out, normed_out, squares_out) = refs[:-3], refs[-3:]
     attn_out, rows = summed(parts), wide(stream_in[...])
@@ -719,24 +745,30 @@
     )(stream_in, *parts)
 
 
-def final_body(middle, *refs):
-    parts, (layer_out, squares_out) = refs[:-2], refs[-2:]
+def final_body(middle, squares_a, *refs):
+    parts, (layer_out, sums_out) = refs[:-2], refs[-2:]
     mlp_out = from_split(summed(parts))
     final = middle[...] + mlp_out
     layer_out[...] = low(final)
-    squares_out[...] = column_sums(mlp_out, final)
-
-
-def final_pass(middle, parts):
+    squares = jnp.concatenate([squares_a[...], column_sums(mlp_out, final)], axis=0)
+    sums = jnp.sum(squares, axis=1, keepdims=True)
+    lane = lax.broadcasted_iota(jnp.int32, (1, sums_out.shape[1]), 1)
+    total = jnp.zeros((1, sums_out.shape[1]), jnp.float32)
+    for number in range(sums.shape[0]):
+        total += jnp.where(lane == number, sums[number : number + 1, :], 0.0)
+    sums_out[...] = jnp.broadcast_to(total, sums_out.shape)
+
+
+def final_pass(middle, squares_a, parts, copies):
     rows, width = middle.shape
     return pl.pallas_call(
         final_body,
-        out_shape=(low_shape(rows, width), wide_shape(2, width)),
-        in_specs=[VMEM_SPEC] * (1 + len(parts)),
+        out_shape=(low_shape(rows, width), wide_shape(copies, 128)),
+        in_specs=[VMEM_SPEC] * (2 + len(parts)),
         out_specs=(VMEM_SPEC,) * 2,
         name="final_pass",
         **KERNEL,
-    )(middle, *parts)
+    )(middle, squares_a, *parts)
 
 
 def grad_middle_body(middle, cot, *refs):
@@ -873,8 +905,23 @@
     return (*pieces, *(swap(v, "cc") for v in pieces))
 
 
-def chip_parts(first, arrived, count):
-    return tuple(jnp.split(low(wide(first) + wide(arrived)), count, axis=0))
+def add_body(*refs):
+    count = len(refs) // 3
+    for left, right, out in zip(refs[:count], refs[count : 2 * count], refs[2 * count :]):
+        out[...] = low(wide(left[...]) + wide(right[...]))
+
+
+def core_back(blocks):
+    half = len(blocks) // 2
+    arrived = [swap(v, "cc") for v in blocks[half:]]
+    return pl.pallas_call(
+        add_body,
+        out_shape=tuple(low_shape(*v.shape) for v in arrived),
+        in_specs=[VMEM_SPEC] * (2 * half),
+        out_specs=(VMEM_SPEC,) * half,
+        name="add_pass",
+        **KERNEL,
+    )(*blocks[:half], *arrived)
 
 
 def plane_plan(
@@ -901,6 +948,28 @@
     hgroups = lax.axis_size(GROUP_AXES)
     hchunk = ff_local // hgroups
 
+    gain_peer = swap(mlp_gain[None, :], "uly")
+    gain_own, gain_peer = wide(mlp_gain)[None, :], wide(gain_peer)
+    gain_m = pick(
+        x_at,
+        jnp.concatenate([gain_own, gain_peer], axis=1),
+        jnp.concatenate([gain_peer, gain_own], axis=1),
+    ).reshape(mlp_rows, 1)
+    gate_rows, up_rows, down_rows = pack_pass(gain_m, gate_up_weight, down_weight, hgroups)
+    out_rows = out_weight.reshape(d_rows, plane, q_cols).transpose(1, 0, 2).reshape(-1, q_cols)
+    out_here = exchange(out_rows, PLANE_AXES)
+    normed, cot_split = prepare_pass(layer_input, output_cotangent)
+    cot_1 = shift(cot_split, 1)
+    gate_rows, up_rows, down_rows, out_here, normed, cot_split, cot_1, qkv_weight = together(
+        gate_rows, up_rows, down_rows, out_here, normed, cot_split, cot_1, qkv_weight
+    )
+
+    def spread(here):
+        return lax.all_gather(here, SIDE_AXES, axis=0, tiled=True)
+
+    wo = lax.all_gather(out_here, "dp", axis=0, tiled=True)
+    gate_here = exchange(gate_rows, GROUP_AXES)
+    normed_p = plane_hop(normed)
     gain_a = wide(attn_gain)[:, None]
     folded = low(wide(qkv_weight) * gain_a)
     by_group = jnp.concatenate(
@@ -910,28 +979,10 @@
         ],
         axis=2,
     ).transpose(1, 0, 2)
-
-    def to_planes(rows):
-        return jnp.broadcast_to(rows[None], (nz, *rows.shape)).reshape(-1, rows.shape[2])
-
-    qkv_rows = to_planes(by_group)
-    out_rows = out_weight.reshape(d_rows, plane, q_cols).transpose(1, 0, 2).reshape(-1, q_cols)
-    out_here = exchange(out_rows, PLANE_AXES)
-
-    gain_peer = swap(mlp_gain[None, :], "uly")
-    stream_in = wide(layer_input)
-    normed = low(stream_in * unit_scale(stream_in))
-    normed, gain_peer, out_here, qkv_rows = together(normed, gain_peer, out_here, qkv_rows)
-
-    gain_own, gain_peer = wide(mlp_gain)[None, :], wide(gain_peer)
-    gain_m = pick(
-        x_at,
-        jnp.concatenate([gain_own, gain_peer], axis=1),
-        jnp.concatenate([gain_peer, gain_own], axis=1),
-    ).reshape(mlp_rows, 1)
-    gate_rows, up_rows, down_rows = pack_pass(gain_m, gate_up_weight, down_weight, hgroups)
-
-    cot_split = to_split(output_cotangent)
+    qkv_rows = jnp.broadcast_to(by_group[None], (nz, *by_group.shape)).reshape(-1, own_cols)
+    gate_here, normed_p, qkv_rows, up_rows, down_rows, cot_split = together(
+        gate_here, normed_p, qkv_rows, up_rows, down_rows, cot_split
+    )
 
     block = jnp.arange(plane, dtype=jnp.int32)
     core_of, y_of, x_of = (block // 4) ^ c_at, (block // 2) % 2 ^ y_at, block % 2 ^ x_at
@@ -941,36 +992,23 @@
     angles = rope_angles(positions)
     cosine = jnp.concatenate([jnp.cos(angles)] * 2, axis=1)
     sine = jnp.concatenate([-jnp.sin(angles), jnp.sin(angles)], axis=1)
-
-    wo = lax.all_gather(out_here, "dp", axis=0, tiled=True)
-    gate_here = exchange(gate_rows, GROUP_AXES)
-    normed_p = plane_hop(normed)
-    gate_here, normed_p, qkv_rows, up_rows, down_rows, cosine, sine, cot_split = together(
-        gate_here, normed_p, qkv_rows, up_rows, down_rows, cosine, sine, cot_split
-    )
-
-    def spread(here):
-        return lax.all_gather(here, SIDE_AXES, axis=0, tiled=True)
-
     gate_w = spread(gate_here)
     wq = exchange(qkv_rows, ALL_AXES)
     normed_p = core_hop(normed_p)
-    cot_1 = shift(cot_split, 1)
-    wq, normed_p, cot_1, up_rows, cot_split = together(wq, normed_p, cot_1, up_rows, cot_split)
+    rows_info = (cosine, sine, positions[:, None], positions[None, :])
+    wq, normed_p, up_rows, rows_info = together(wq, normed_p, up_rows, rows_info)
 
     up_here = exchange(up_rows, GROUP_AXES)
-    query, key, value, heads = attention_forward(normed_p, wq, cosine, sine, positions)
-    up_here, heads, wo, down_rows = together(up_here, heads, wo, down_rows)
+    query, key, value, heads = attention_forward(normed_p, wq, *rows_info)
+    attn_parts = core_back(by_cols_pass(heads, wo, 1, plane, "out_pass"))
+    up_here, attn_parts, down_rows, cot_split = together(
+        up_here, attn_parts, down_rows, cot_split
+    )
 
     up_w = spread(up_here)
-    attn_first, attn_second = by_cols_pass(heads, wo, 1, "out_pass")
-    attn_arrived = swap(attn_second, "cc")
-    attn_parts = chip_parts(attn_first, attn_arrived, 4)
-    attn_parts, down_rows, cot_split = together(attn_parts, down_rows, cot_split)
-
     down_here = exchange(down_rows, GROUP_AXES)
+    attn_parts = plane_back(attn_parts)
     cot_3 = shift(cot_split, 3)
-    attn_parts = plane_back(attn_parts)
     attn_parts, down_here, cot_3, cot_split = together(attn_parts, down_here, cot_3, cot_split)
 
     down_w = spread(down_here)
@@ -982,72 +1020,69 @@
     cot_p = (cot_split, cot_1, shift(cot_split, 2), cot_3)
     hidden, gate_slope, up_slope = hidden_pass(zhat_p, gate_w, up_w)
     hidden, cot_p, gate_slope, down_w = together(hidden, cot_p, gate_slope, down_w)
+
     cot_p = core_hop(cot_p)
-    mlp_first, mlp_second = by_cols_pass(hidden, down_w, 2, "down_pass")
-    cot_p, mlp_first, mlp_second = together(cot_p, mlp_first, mlp_second)
-
-    mlp_arrived = swap(mlp_second, "cc")
-    grad_gate, grad_up, gz_first, gz_second = grad_hidden_pass(
-        cot_p, gate_slope, up_slope, gate_w, up_w, down_w
-    )
-    gz_second, grad_gate, mlp_arrived = together(gz_second, grad_gate, mlp_arrived)
+    mlp_parts = core_back(by_cols_pass(hidden, down_w, 2, 2 * nz, "down_pass"))
+    down_t = term_pass(cot_p, hidden, 2, 2)
+    cot_p, mlp_parts, down_t = together(cot_p, mlp_parts, down_t)
 
     def side_sum(term):
         return lax.psum_scatter(term, SIDE_AXES, scatter_dimension=0, tiled=True)
 
-    gz_arrived = swap(gz_second, "cc")
+    down_t = side_sum(down_t)
+    mlp_2, mlp_3 = shift(mlp_parts[2], -2), shift(mlp_parts[3], -3)
+    grad_gate, grad_up, *gz_parts = grad_hidden_pass(
+        cot_p, gate_slope, up_slope, gate_w, up_w, down_w
+    )
+    gz_parts, grad_gate, mlp_2, mlp_3, mlp_parts = together(
+        gz_parts, grad_gate, mlp_2, mlp_3, mlp_parts
+    )
+
+    gz_parts = core_back(gz_parts)
+    mlp_1 = shift(mlp_parts[1], -1)
     gate_t = term_pass(zhat_p, grad_gate, 2, 2)
-    gz_parts = chip_parts(gz_first, gz_arrived, nz)
-    gz_parts, gate_t, mlp_arrived = together(gz_parts, gate_t, mlp_arrived)
+    gz_parts, gate_t, mlp_1, mlp_parts = together(gz_parts, gate_t, mlp_1, mlp_parts)
 
     gate_t = side_sum(gate_t)
     gz_parts = column_back(gz_parts)
     up_t = term_pass(zhat_p, grad_up, 2, 2)
-    down_t = term_pass(cot_p, hidden, 2, 2)
-    mlp_parts = chip_parts(mlp_first, mlp_arrived, nz)
-    gz_parts, up_t, down_t, mlp_parts = together(gz_parts, up_t, down_t, mlp_parts)
+    mlp_parts = (mlp_parts[0], mlp_1, mlp_2, mlp_3)
+    layer_output, lanes = final_pass(middle, squares_a, mlp_parts, ndev)
+    gathered = exchange(lanes, ALL_AXES)
+    gz_parts, up_t, down_t, gathered = together(gz_parts, up_t, down_t, gathered)
+
+    down_back = exchange(down_t, GROUP_AXES)
+    grad_middle, grad_out = grad_middle_pass(middle, output_cotangent, gz_parts)
+    grad_out_p = plane_hop(grad_out)
+    grad_out_p, gate_t, down_back, up_t = together(grad_out_p, gate_t, down_back, up_t)
+    grad_out_p, gate_t, up_t = together(core_hop(grad_out_p), gate_t, up_t)
 
     up_t = side_sum(up_t)
-    grad_middle, grad_out = grad_middle_pass(middle, output_cotangent, gz_parts)
-    mlp_1, mlp_3 = shift(mlp_parts[1], -1), shift(mlp_parts[3], -3)
-    grad_out_p = plane_hop(grad_out)
-    grad_out_p, mlp_1, mlp_3, down_t = together(grad_out_p, mlp_1, mlp_3, down_t)
-    grad_out_p, gate_t, down_t = together(core_hop(grad_out_p), gate_t, down_t)
-
-    down_t = side_sum(down_t)
     gate_back = exchange(gate_t, GROUP_AXES)
-    mlp_2 = shift(mlp_parts[2], -2)
-    grad_qkv = attention_backward(grad_out_p, wo, query, key, value, cosine, sine, positions)
-    gx_first, gx_second = by_cols_pass(grad_qkv, wq, 1, "qkv_back_pass")
+    grad_qkv = attention_backward(grad_out_p, wo, query, key, value, *rows_info)
+    gx_parts = core_back(by_cols_pass(grad_qkv, wq, 1, plane, "qkv_back_pass"))
     qkv_term = term_pass(normed_p, grad_qkv, 2, 1)
-    gx_second, qkv_term, gate_back, mlp_2, heads, up_t = together(
-        gx_second, qkv_term, gate_back, mlp_2, heads, up_t
-    )
-
-    gx_arrived = swap(gx_second, "cc")
+    gx_parts, qkv_term, gate_back, down_back, heads = together(
+        gx_parts, qkv_term, gate_back, down_back, heads
+    )
+
     out_term = term_pass(grad_out_p, heads, 2, 1)
-    gx_parts = chip_parts(gx_first, gx_arrived, 4)
-    gx_parts, out_term, qkv_term, up_t = together(gx_parts, out_term, qkv_term, up_t)
-
     qkv_sum = exchange(qkv_term, ALL_AXES)
     gx_parts = plane_back(gx_parts)
-    gx_parts, qkv_sum, up_t, down_t, out_term = together(
-        gx_parts, qkv_sum, up_t, down_t, out_term
+    down_back = down_back.reshape(hgroups, mlp_rows, hchunk)
+    down_grad = wide(down_back.transpose(1, 0, 2).reshape(mlp_rows, ff_local))
+    gx_parts, qkv_sum, up_t, out_term, down_grad = together(
+        gx_parts, qkv_sum, up_t, out_term, down_grad
     )
 
     out_term = lax.psum_scatter(out_term, "dp", scatter_dimension=0, tiled=True)
-    both_back = exchange(jnp.concatenate([up_t, down_t], axis=1), GROUP_AXES)
+    up_back = exchange(up_t, GROUP_AXES)
     input_grad = input_grad_pass(layer_input, grad_middle, gx_parts)
-    layer_output, squares_b = final_pass(middle, (mlp_parts[0], mlp_1, mlp_2, mlp_3))
-    both_back, input_grad, out_term, squares_b = together(
-        both_back, input_grad, out_term, squares_b
-    )
-    up_back, down_back = jnp.split(both_back, 2, axis=1)
-
-    squares = jnp.sum(jnp.concatenate([squares_a, squares_b], axis=0), axis=1)
-    lanes = jnp.zeros((1, 128), jnp.float32).at[0, :5].set(squares)
-    gathered = exchange(jnp.broadcast_to(lanes, (ndev, 128)), ALL_AXES)
+    up_back, input_grad, out_term = together(up_back, input_grad, out_term)
+
     out_sum = exchange(out_term, PLANE_AXES)
+    gate_up_grad, gain_sum = unpack_pass(gain_m, gate_up_weight, gate_back, up_back, hgroups)
+    out_sum, gate_up_grad, gain_sum = together(out_sum, gate_up_grad, gain_sum)
     def plane_sum(arrived, cols):
         return jnp.sum(wide(arrived.reshape(nz, plane, d_rows, cols)), axis=0).transpose(1, 0, 2)
 
@@ -1062,9 +1097,6 @@
     )
     qkv_grad = qkv_sum * gain_a
     attn_gain_grad = jnp.sum(qkv_sum * wide(qkv_weight), axis=1)
-    gate_up_grad, gain_sum = unpack_pass(gain_m, gate_up_weight, gate_back, up_back, hgroups)
-    down_back = down_back.reshape(hgroups, mlp_rows, hchunk)
-    down_grad = wide(down_back.transpose(1, 0, 2).reshape(mlp_rows, ff_local))
     gain_halves = gain_sum.reshape(2, -1)
     gain_keep = jnp.where(x_at == 0, gain_halves[0], gain_halves[1])
     gain_send = jnp.where(x_at == 0, gain_halves[1], gain_halves[0])

time: 718 us -> 640 us (0.89); the launches traced: 709 us -> 638 us
  waiting for transfers between devices: 381 us -> 308 us
  Pallas kernels: 159 us -> 178 us
  other arithmetic: 28.1 us -> 14.1 us
    ppermute x12, waiting for transfers between devices: 140 us -> 68.5 us  [shift(): lax.ppermute(values, 'dp', [(i, (i + by) % count) for i in range(count)])]
    all_to_all x10 -> x11, waiting for transfers between devices: 52.4 us -> 114 us  [exchange(): return lax.all_to_all(values, axes, split_axis=0, concat_axis=0, tiled=True)]
    reduce_scatter x1, waiting for transfers between devices: 34.6 us -> 0.01 us  [plane_plan(): out_term = lax.psum_scatter(out_term, 'dp', scatter_dimension=0, tiled=True)]
    ppermute x34 -> x46, waiting for transfers between devices: 152 us -> 123 us  [swap(): return lax.ppermute(values, axes if len(axes) > 1 else axes[0], pairs)]
    pallas_call x5 -> x10, Pallas kernels: 60.3 us -> 80.8 us  [the longest x1 24.1 us: grad_hidden_pass(): pl.pallas_call(grad_hidden_body, grid=(4 + width // ROWS,), out_shape=(lo...]
    ppermute x12, starting transfers between devices: 30.9 us -> 20.8 us  [shift(): lax.ppermute(values, 'dp', [(i, (i + by) % count) for i in range(count)])]
    convert_element_type x6 -> x1, other arithmetic: 10.8 us -> 1.19 us  [low(): return values.astype(jnp.bfloat16)]
    all_to_all x10 -> x11, starting transfers between devices: 39.6 us -> 46.4 us  [exchange(): return lax.all_to_all(values, axes, split_axis=0, concat_axis=0, tiled=True)]
  transfers between devices with their start and end apart: 64 -> 77, of which waited for: 35 -> 33; matrix products, arithmetic and copies ran while one was open for 5% -> 4% of each run, Pallas kernels for 21% -> 27%
where the time goes in v3:
time: 640 us; the launch traced here: 638 us
  waiting for transfers between devices  308 us (48%)
  Pallas kernels  178 us (28%)
  starting transfers between devices  95.2 us (15%)
  local copies, waits for them, and re-layouts  28.3 us (4%)
  between operations  15 us (2%)
  other arithmetic  14.1 us (2%)
    ppermute x46, waiting for transfers between devices, swap(): return lax.ppermute(values, axes if len(axes) > 1 else axes[0], pairs)  123 us
    all_to_all x11, waiting for transfers between devices, exchange(): return lax.all_to_all(values, axes, split_axis=0, concat_axis=0, tiled=True)  114 us
    ppermute x12, waiting for transfers between devices, shift(): lax.ppermute(values, 'dp', [(i, (i + by) % count) for i in range(count)])  68.5 us
    all_to_all x11, starting transfers between devices, exchange(): return lax.all_to_all(values, axes, split_axis=0, concat_axis=0, tiled=True)  46.4 us
    pallas_call x5, Pallas kernels, term_pass(): pl.pallas_call(term_body, grid=(row_parts, col_parts), out_shape=low_shap...  37.5 us
    ppermute x46, starting transfers between devices, swap(): return lax.ppermute(values, axes if len(axes) > 1 else axes[0], pairs)  27.7 us
    pallas_call x1, Pallas kernels, grad_hidden_pass(): pl.pallas_call(grad_hidden_body, grid=(4 + width // ROWS,), out_shape=(lo...  24.1 us
    pallas_call x3, Pallas kernels, by_cols_pass(): pl.pallas_call(functools.partial(by_cols_body, parts), grid=(width // ROW...  24 us
  transfers between devices with their start and end apart: 77, of which 33 were waited for; matrix products, arithmetic and copies ran while one was open for 4% of the time, Pallas kernels for 27%

profile of v3, /device:TPU:0, one launch (start us, length us, event | category | flops | bytes accessed | tf_op | source)
XLA Modules:
  0.0 637.9 jit_solution(13637116820204968439)
XLA Ops:
  44.3 9.8 %collective-permute-done.4.refs_3_ = bf16[128,2048]{1,0:T(8,128)(2,1)S(1)} collective-permute-done((bf16[128,2048]{1,0:T(8,128)(2,1)S(1)}, bf16[128,2048]{1,0:T(8,128)(2,1)S(1)}, u32[]{:S(2)}, u32[]{:S(2)}) %collective-permute-start.4) | collective-permute-done | bytes 524320 | tf_op jit(solution)/shard_map/ppermute | solution.py:880
  54.1 10.6 %collective-permute-done.3.refs_2_ = bf16[128,2048]{1,0:T(8,128)(2,1)S(1)} collective-permute-done((bf16[128,2048]{1,0:T(8,128)(2,1)S(1)}, bf16[128,2048]{1,0:T(8,128)(2,1)S(1)}, u32[]{:S(2)}, u32[]{:S(2)}) %collective-permute-start.3) | collective-permute-done | bytes 524320 | tf_op jit(solution)/shard_map/ppermute | solution.py:880
  65.1 12.6 %all-to-all-done.1 = bf16[8,128,512]{2,1,0:T(8,128)(2,1)S(1)} async-done(((bf16[8,128,512]{2,1,0:T(8,128)(2,1)}), bf16[8,128,512]{2,1,0:T(8,128)(2,1)S(1)}, u32[]{:S(2)}, u32[]{:S(2)}) %all-to-all-start.1) | async-done | bytes 1048608 | tf_op jit(solution)/shard_map/all_to_all | solution.py:867
  93.7 39.1 %all-to-all-done.2 = bf16[32,64,512]{2,1,0:T(8,128)(2,1)S(1)} async-done(((bf16[32,64,512]{2,1,0:T(8,128)(2,1)}), bf16[32,64,512]{2,1,0:T(8,128)(2,1)S(1)}, u32[]{:S(2)}, u32[]{:S(2)}) %all-to-all-start.2) | async-done | bytes 2097184 | tf_op jit(solution)/shard_map/all_to_all | solution.py:867
  136.5 13.4 %attention_forward.1 = (bf16[1024,256]{1,0:T(8,128)(2,1)}, bf16[1024,128]{1,0:T(8,128)(2,1)}, bf16[1024,128]{1,0:T(8,128)(2,1)}, bf16[1024,256]{1,0:T(8,128)(2,1)}) custom-call(bf16[2048,512]{1,0:T(8,128)(2,1)} %bitcast.117, f32[1024,128]{1,0:T(8,128)} %get-tuple-element.246.cosine, f32[1024,128]{1,0:T(8,128)} %get-tuple-element.247.sine, ...), custom_call_target="tpu_custom_call" | custom-call | flops 1000 | bytes 1000 | tf_op jit(solution)/shard_map/attention_forward/pallas_call | solution.py:450
  179.0 15.8 %collective-permute-done.13.refs_1_ = bf16[128,2048]{1,0:T(8,128)(2,1)S(1)} collective-permute-done((bf16[128,2048]{1,0:T(8,128)(2,1)}, bf16[128,2048]{1,0:T(8,128)(2,1)S(1)}, u32[]{:S(2)}, u32[]{:S(2)}) %collective-permute-start.13) | collective-permute-done | bytes 524320 | tf_op jit(solution)/shard_map/ppermute | solution.py:880
  199.8 9.8 %collective-permute-done.15.refs_3_ = bf16[128,2048]{1,0:T(8,128)(2,1)S(1)} collective-permute-done((bf16[128,2048]{1,0:T(8,128)(2,1)}, bf16[128,2048]{1,0:T(8,128)(2,1)S(1)}, u32[]{:S(2)}, u32[]{:S(2)}) %collective-permute-start.15) | collective-permute-done | bytes 524320 | tf_op jit(solution)/shard_map/ppermute | solution.py:880
  218.6 11.6 %collective-permute-done.19.refs_3_ = bf16[128,2048]{1,0:T(8,128)(2,1)S(1)} collective-permute-done((bf16[128,2048]{1,0:T(8,128)(2,1)}, bf16[128,2048]{1,0:T(8,128)(2,1)S(1)}, u32[]{:S(2)}, u32[]{:S(2)}) %collective-permute-start.19) | collective-permute-done | bytes 524320 | tf_op jit(solution)/shard_map/ppermute | solution.py:893
  230.3 31.9 %collective-permute-done.18.refs_2_ = bf16[128,2048]{1,0:T(8,128)(2,1)S(1)} collective-permute-done((bf16[128,2048]{1,0:T(8,128)(2,1)}, bf16[128,2048]{1,0:T(8,128)(2,1)S(1)}, u32[]{:S(2)}, u32[]{:S(2)}) %collective-permute-start.18) | collective-permute-done | bytes 524320 | tf_op jit(solution)/shard_map/ppermute | solution.py:893
  269.1 15.4 %hidden_pass.1 = (bf16[1024,1024]{1,0:T(8,128)(2,1)}, bf16[1024,1024]{1,0:T(8,128)(2,1)}, bf16[1024,1024]{1,0:T(8,128)(2,1)}) custom-call(bf16[4096,512]{1,0:T(8,128)(2,1)} %all-gather.7.cloned.1.call-done.gate_near.gate_far.refs_0_.refs_1_, bf16[4096,512]{1,0:T(8,128)(2,1)} %all-gather.7.cloned.1.call-done.gate_near.gate_far.refs_0_.refs_1_, ...), custom_call_target="tpu_custom_call" | custom-call | flops 1000 | bytes 1000 | tf_op jit(solution)/shard_map/hidden_pass/pallas_call | solution.py:589
  284.4 8.4 %collective-permute-done.24.refs_2_.refs_6_ = bf16[128,2048]{1,0:T(8,128)(2,1)} collective-permute-done((bf16[128,2048]{1,0:T(8,128)(2,1)}, bf16[128,2048]{1,0:T(8,128)(2,1)}, u32[]{:S(2)}, u32[]{:S(2)}) %collective-permute-start.24) | collective-permute-done | bytes 524320 | tf_op jit(solution)/shard_map/ppermute | solution.py:893
  295.9 9.5 %down_pass.1 = (bf16[128,2048]{1,0:T(8,128)(2,1)}, bf16[128,2048]{1,0:T(8,128)(2,1)}, bf16[128,2048]{1,0:T(8,128)(2,1)}, bf16[128,2048]{1,0:T(8,128)(2,1)}, bf16...) custom-call(bf16[1024,1024]{1,0:T(8,128)(2,1)} %get-tuple-element.318., ...), custom_call_target="tpu_custom_call" | custom-call | flops 1000 | bytes 1000 | tf_op jit(solution)/shard_map/down_pass/pallas_call | solution.py:545
  307.8 9.0 %term_pass.5 = bf16[4096,512]{1,0:T(8,128)(2,1)} custom-call(bf16[128,2048]{1,0:T(8,128)(2,1)} %get-tuple-element.331.refs_0_.refs_4_, bf16[128,2048]{1,0:T(8,128)(2,1)} %copy-done.14, bf16[128,2048]{1,0:T(8,128)(2,1)} %collective-permute-done.24.refs_2_.refs_6_, bf16[128,2048]{1,0:T(8,128)(2,1)} %collective-permute-done.16.refs_3_.refs_7_, ...), custom_call_target="tpu_custom_call" | custom-call | flops 1000 | bytes 1000 | tf_op jit(solution)/shard_map/term_pass/pallas_call | solution.py:661
  326.4 24.1 %grad_hidden_pass.1 = (bf16[1024,1024]{1,0:T(8,128)(2,1)}, bf16[1024,1024]{1,0:T(8,128)(2,1)}, bf16[128,2048]{1,0:T(8,128)(2,1)}, bf16[128,2048]{1,0:T(8,128)(2,...) custom-call(bf16[4096,512]{1,0:T(8,128)(2,1)} %all-gather.11.cloned., ...), custom_call_target="tpu_custom_call" | custom-call | flops 1000 | bytes 1000 | tf_op jit(solution)/shard_map/grad_hidden_pass/pallas_call | solution.py:635
  350.5 9.5 %collective-permute-done.33.refs_2_ = bf16[128,2048]{1,0:T(8,128)(2,1)S(1)} collective-permute-done((bf16[128,2048]{1,0:T(8,128)(2,1)S(1)}, bf16[128,2048]{1,0:T(8,128)(2,1)S(1)}, u32[]{:S(2)}, u32[]{:S(2)}) %collective-permute-start.33) | collective-permute-done | bytes 524320 | tf_op jit(solution)/shard_map/ppermute | solution.py:893
  361.1 9.2 %term_pass.6 = bf16[4096,512]{1,0:T(8,128)(2,1)} custom-call(bf16[128,2048]{1,0:T(8,128)(2,1)} %get-tuple-element.297.refs_0_, bf16[128,2048]{1,0:T(8,128)(2,1)} %copy-done.4, bf16[128,2048]{1,0:T(8,128)(2,1)} %copy-done.3, bf16[128,2048]{1,0:T(8,128)(2,1)} %copy-done.2, bf16[128,2048]{1,0:T(8,128)(2,1)} %copy-done.5, bf16[128,2048]{1,0:T(8,128)(2,1)} %copy-done.6, ...), custom_call_target="tpu_custom_call" | custom-call | flops 1000 | bytes 1000 | tf_op jit(solution)/shard_map/term_pass/pallas_call | solution.py:661
  388.8 9.3 %term_pass.7 = bf16[4096,512]{1,0:T(8,128)(2,1)} custom-call(bf16[128,2048]{1,0:T(8,128)(2,1)} %get-tuple-element.297.refs_0_, bf16[128,2048]{1,0:T(8,128)(2,1)} %copy-done.4, bf16[128,2048]{1,0:T(8,128)(2,1)} %copy-done.3, bf16[128,2048]{1,0:T(8,128)(2,1)} %copy-done.2, bf16[128,2048]{1,0:T(8,128)(2,1)} %copy-done.5, bf16[128,2048]{1,0:T(8,128)(2,1)} %copy-done.6, ...), custom_call_target="tpu_custom_call" | custom-call | flops 1000 | bytes 1000 | tf_op jit(solution)/shard_map/term_pass/pallas_call | solution.py:661
  398.1 28.1 %all-to-all-done.5 = f32[32,1,128]{2,1,0:T(1,128)S(1)} async-done(((f32[32,1,128]{2,1,0:T(1,128)}), f32[32,1,128]{2,1,0:T(1,128)S(1)}, u32[]{:S(2)}, u32[]{:S(2)}) %all-to-all-start.5) | async-done | bytes 16416 | tf_op jit(solution)/shard_map/all_to_all | solution.py:867
  438.5 12.4 %collective-permute-done.45.refs_3_ = bf16[128,2048]{1,0:T(8,128)(2,1)S(1)} collective-permute-done((bf16[128,2048]{1,0:T(8,128)(2,1)}, bf16[128,2048]{1,0:T(8,128)(2,1)S(1)}, u32[]{:S(2)}, u32[]{:S(2)}) %collective-permute-start.45) | collective-permute-done | bytes 524320 | tf_op jit(solution)/shard_map/ppermute | solution.py:880
  450.9 10.8 %collective-permute-done.44.refs_2_ = bf16[128,2048]{1,0:T(8,128)(2,1)S(1)} collective-permute-done((bf16[128,2048]{1,0:T(8,128)(2,1)}, bf16[128,2048]{1,0:T(8,128)(2,1)S(1)}, u32[]{:S(2)}, u32[]{:S(2)}) %collective-permute-start.44) | collective-permute-done | bytes 524320 | tf_op jit(solution)/shard_map/ppermute | solution.py:880
  471.7 17.1 %attention_backward.1.rows.refs_8_ = bf16[1024,512]{1,0:T(8,128)(2,1)} custom-call(bf16[2048,256]{1,0:T(8,128)(2,1)} %all-gather.5.cloned.1.call-done.refs_0_.weight, bf16[1024,256]{1,0:T(8,128)(2,1)} %get-tuple-element.372.query, bf16[1024,128]{1,0:T(8,128)(2,1)} %get-tuple-element.373.key, bf16[1024,128]{1,0:T(8,128)(2,1)} %get-tuple-element.374.value, ...), custom_call_target="tpu_custom_call" | custom-call | flops 1000 | bytes 1000 | tf_op jit(solution)/shard_map/attention_backward/pallas_call | solution.py:501
  527.2 23.0 %collective-permute-done.54.refs_1_ = bf16[128,2048]{1,0:T(8,128)(2,1)} collective-permute-done((bf16[128,2048]{1,0:T(8,128)(2,1)}, bf16[128,2048]{1,0:T(8,128)(2,1)}, u32[]{:S(2)}, u32[]{:S(2)}) %collective-permute-start.54) | collective-permute-done | bytes 524320 | tf_op jit(solution)/shard_map/ppermute | solution.py:880
  550.2 14.8 %collective-permute-done.56.refs_3_ = bf16[128,2048]{1,0:T(8,128)(2,1)} collective-permute-done((bf16[128,2048]{1,0:T(8,128)(2,1)}, bf16[128,2048]{1,0:T(8,128)(2,1)}, u32[]{:S(2)}, u32[]{:S(2)}) %collective-permute-start.56) | collective-permute-done | bytes 524320 | tf_op jit(solution)/shard_map/ppermute | solution.py:880
  579.5 33.6 %all-to-all-done.9 = bf16[8,128,512]{2,1,0:T(8,128)(2,1)} async-done(((bf16[8,128,512]{2,1,0:T(8,128)(2,1)}), bf16[8,128,512]{2,1,0:T(8,128)(2,1)}, u32[]{:S(2)}, u32[]{:S(2)}) %all-to-all-start.9) | async-done | bytes 1048608 | tf_op jit(solution)/shard_map/all_to_all | solution.py:867
  (331 shorter events, 234.1 us)
Async XLA Ops:
  34.0 43.8 %all-to-all-start.1 = ((bf16[8,128,512]{2,1,0:T(8,128)(2,1)}), bf16[8,128,512]{2,1,0:T(8,128)(2,1)S(1)}, u32[]{:S(2)}, u32[]{:S(2)}) async-start(bf16[8,128,512]{2,1,0:T(8,128)(2,1)} %bitcast.134), calls=%async_computation.1 | async-start | bytes 2097152 | tf_op jit(solution)/shard_map/all_to_all | solution.py:867
  37.5 112.3 %all-gather.5.cloned.1.call-start = ((), (), s32[]{:S(2)}) async-start(), calls=%async_computation.15 | async-start | bytes 1310720 | tf_op jit(solution)/shard_map/all_gather | solution.py:970
  38.3 180.4 %all-gather.7.cloned.1.call-start = ((), (), s32[]{:S(2)}) async-start(), calls=%async_computation.16 | async-start | bytes 5242880 | tf_op jit(solution)/shard_map/all_gather | solution.py:968
  80.8 52.1 %all-to-all-start.2 = ((bf16[32,64,512]{2,1,0:T(8,128)(2,1)}), bf16[32,64,512]{2,1,0:T(8,128)(2,1)S(1)}, u32[]{:S(2)}, u32[]{:S(2)}) async-start(bf16[32,64,512]{2,1,0:T(8,128)(2,1)} %bitcast.119), calls=%async_computation.2 | async-start | bytes 4194304 | tf_op jit(solution)/shard_map/all_to_all | solution.py:867
  136.4 125.8 %all-gather.9.cloned.1.call-start = ((), (), s32[]{:S(2)}) async-start(), calls=%async_computation.17 | async-start | bytes 5242880 | tf_op jit(solution)/shard_map/all_gather | solution.py:968
  166.6 43.0 %all-to-all-start.4 = ((bf16[8,128,512]{2,1,0:T(8,128)(2,1)}), bf16[8,128,512]{2,1,0:T(8,128)(2,1)S(1)}, u32[]{:S(2)}, u32[]{:S(2)}) async-start(bf16[8,128,512]{2,1,0:T(8,128)(2,1)} %bitcast.129), calls=%async_computation.4 | async-start | bytes 2097152 | tf_op jit(solution)/shard_map/all_to_all | solution.py:867
  171.6 123.2 %all-gather.11.cloned.1.call-start = ((), (), s32[]{:S(2)}) async-start(), calls=%async_computation.18 | async-start | bytes 5242880 | tf_op jit(solution)/shard_map/all_gather | solution.py:968
  210.6 215.7 %reduce-scatter.5.cloned.1.call-start = ((), (), s32[]{:S(2)}) async-start(), calls=%async_computation.19 | async-start | bytes 5242880 | tf_op jit(solution)/shard_map/reduce_scatter | solution.py:1030
  217.5 44.6 %collective-permute-start.18 = (bf16[128,2048]{1,0:T(8,128)(2,1)}, bf16[128,2048]{1,0:T(8,128)(2,1)S(1)}, u32[]{:S(2)}, u32[]{:S(2)}) collective-permute-start(bf16[128,2048]{1,0:T(8,128)(2,1)} %get-tuple-element.297.refs_0_), channel_id=1, source_target_pairs={{0,16},{8,24},{16,0},{24,8},{1,17},{9,25},{17,1},{25,9},{2,18},{10... | collective-permute-start | bytes 1572872 | tf_op jit(solution)/shard_map/ppermute | solution.py:893
  217.5 44.6 %collective-permute-start.17 = (bf16[128,2048]{1,0:T(8,128)(2,1)}, bf16[128,2048]{1,0:T(8,128)(2,1)S(1)}, u32[]{:S(2)}, u32[]{:S(2)}) collective-permute-start(bf16[128,2048]{1,0:T(8,128)(2,1)} %get-tuple-element.297.refs_0_), channel_id=1, source_target_pairs={{0,8},{8,16},{16,24},{24,0},{1,9},{9,17},{17,25},{25,1},{2,10},{10... | collective-permute-start | bytes 1572872 | tf_op jit(solution)/shard_map/ppermute | solution.py:893
  321.5 140.2 %reduce-scatter.7.cloned.1.call-start = ((), (), s32[]{:S(2)}) async-start(), calls=%async_computation.20 | async-start | bytes 5242880 | tf_op jit(solution)/shard_map/reduce_scatter | solution.py:1030
  322.5 37.5 %collective-permute-start.33 = (bf16[128,2048]{1,0:T(8,128)(2,1)S(1)}, bf16[128,2048]{1,0:T(8,128)(2,1)S(1)}, u32[]{:S(2)}, u32[]{:S(2)}) collective-permute-start(bf16[128,2048]{1,0:T(8,128)(2,1)S(1)} %copy-done.59), channel_id=1, source_target_pairs={{0,16},{8,24},{16,0},{24,8},{1,17},{9,25},{17,1},{25,9},{2,18},{10... | collective-permute-start | bytes 1572872 | tf_op jit(solution)/shard_map/ppermute | solution.py:893
  376.4 49.8 %collective-permute-start.40 = (bf16[128,2048]{1,0:T(8,128)(2,1)S(1)}, bf16[128,2048]{1,0:T(8,128)(2,1)S(1)}, u32[]{:S(2)}, u32[]{:S(2)}) collective-permute-start(bf16[128,2048]{1,0:T(8,128)(2,1)S(1)} %copy-done.57), channel_id=1, source_target_pairs={{0,24},{8,0},{16,8},{24,16},{1,25},{9,1},{17,9},{25,17},{2,26},{10... | collective-permute-start | bytes 1572872 | tf_op jit(solution)/shard_map/ppermute | solution.py:893
  380.1 46.1 %collective-permute-start.41 = (bf16[128,2048]{1,0:T(8,128)(2,1)S(1)}, bf16[128,2048]{1,0:T(8,128)(2,1)S(1)}, u32[]{:S(2)}, u32[]{:S(2)}) collective-permute-start(bf16[128,2048]{1,0:T(8,128)(2,1)S(1)} %copy-done.56), channel_id=1, source_target_pairs={{0,16},{8,24},{16,0},{24,8},{1,17},{9,25},{17,1},{25,9},{2,18},{10... | collective-permute-start | bytes 1572872 | tf_op jit(solution)/shard_map/ppermute | solution.py:893
  380.1 46.1 %collective-permute-start.42 = (bf16[128,2048]{1,0:T(8,128)(2,1)S(1)}, bf16[128,2048]{1,0:T(8,128)(2,1)S(1)}, u32[]{:S(2)}, u32[]{:S(2)}) collective-permute-start(bf16[128,2048]{1,0:T(8,128)(2,1)S(1)} %copy-done.55), channel_id=1, source_target_pairs={{0,8},{8,16},{16,24},{24,0},{1,9},{9,17},{17,25},{25,1},{2,10},{10... | collective-permute-start | bytes 1572872 | tf_op jit(solution)/shard_map/ppermute | solution.py:893
  384.2 42.1 %all-to-all-start.5 = ((f32[32,1,128]{2,1,0:T(1,128)}), f32[32,1,128]{2,1,0:T(1,128)S(1)}, u32[]{:S(2)}, u32[]{:S(2)}) async-start(f32[32,1,128]{2,1,0:T(1,128)} %bitcast.148), calls=%async_computation.6 | async-start | bytes 32768 | tf_op jit(solution)/shard_map/all_to_all | solution.py:867
  426.3 35.4 %all-to-all-start.6 = ((bf16[8,128,512]{2,1,0:T(8,128)(2,1)}), bf16[8,128,512]{2,1,0:T(8,128)(2,1)S(1)}, u32[]{:S(2)}, u32[]{:S(2)}) async-start(bf16[8,128,512]{2,1,0:T(8,128)(2,1)} %bitcast.132), calls=%async_computation.8 | async-start | bytes 2097152 | tf_op jit(solution)/shard_map/all_to_all | solution.py:867
  431.0 134.0 %reduce-scatter.9.cloned.1.call-start = ((), (), s32[]{:S(2)}) async-start(), calls=%async_computation.21 | async-start | bytes 5242880 | tf_op jit(solution)/shard_map/reduce_scatter | solution.py:1030
  466.9 41.7 %all-to-all-start.7 = ((bf16[8,128,512]{2,1,0:T(8,128)(2,1)}), bf16[8,128,512]{2,1,0:T(8,128)(2,1)S(1)}, u32[]{:S(2)}, u32[]{:S(2)}) async-start(bf16[8,128,512]{2,1,0:T(8,128)(2,1)} %bitcast.131), calls=%async_computation.9 | async-start | bytes 2097152 | tf_op jit(solution)/shard_map/all_to_all | solution.py:867
  509.6 55.3 %all-to-all-start.8 = ((bf16[32,64,512]{2,1,0:T(8,128)(2,1)}), bf16[32,64,512]{2,1,0:T(8,128)(2,1)S(1)}, u32[]{:S(2)}, u32[]{:S(2)}) async-start(bf16[32,64,512]{2,1,0:T(8,128)(2,1)} %bitcast.30), calls=%async_computation.10 | async-start | bytes 4194304 | tf_op jit(solution)/shard_map/all_to_all | solution.py:867
  514.6 98.6 %reduce-scatter.11.cloned.1.call-start = ((), (), s32[]{:S(2)}) async-start(), calls=%async_computation.22 | async-start | bytes 1310720 | tf_op jit(solution)/shard_map/reduce_scatter | solution.py:1078
  514.7 35.5 %collective-permute-start.54 = (bf16[128,2048]{1,0:T(8,128)(2,1)}, bf16[128,2048]{1,0:T(8,128)(2,1)}, u32[]{:S(2)}, u32[]{:S(2)}) collective-permute-start(bf16[128,2048]{1,0:T(8,128)(2,1)} %get-tuple-element.419), channel_id=1, source_target_pairs={{0,1},{1,0},{2,3},{3,2},{4,5},{5,4},{6,7},{7,6},{8,9},{9,8},{10,11... | collective-permute-start | bytes 1572872 | tf_op jit(solution)/shard_map/ppermute | solution.py:880
  518.0 47.0 %collective-permute-start.56 = (bf16[128,2048]{1,0:T(8,128)(2,1)}, bf16[128,2048]{1,0:T(8,128)(2,1)}, u32[]{:S(2)}, u32[]{:S(2)}) collective-permute-start(bf16[128,2048]{1,0:T(8,128)(2,1)} %get-tuple-element.421), channel_id=1, source_target_pairs={{0,5},{1,4},{4,1},{5,0},{2,7},{3,6},{6,3},{7,2},{8,13},{9,12},{12,... | collective-permute-start | bytes 1572872 | tf_op jit(solution)/shard_map/ppermute | solution.py:880
  565.0 48.2 %all-to-all-start.9 = ((bf16[8,128,512]{2,1,0:T(8,128)(2,1)}), bf16[8,128,512]{2,1,0:T(8,128)(2,1)}, u32[]{:S(2)}, u32[]{:S(2)}) async-start(bf16[8,128,512]{2,1,0:T(8,128)(2,1)} %bitcast.133), calls=%async_computation.12 | async-start | bytes 2097152 | tf_op jit(solution)/shard_map/all_to_all | solution.py:867
  (115 other events, 1133.4 us)
Sparse Core Ops, SparseCore 0:
  39.9 41.2 all-gather.4
  83.1 67.4 all-gather.6
  166.7 73.6 all-gather.8
  242.1 52.6 all-gather.10
  321.6 52.6 reduce-scatter.4
  378.0 52.8 reduce-scatter.6
  467.0 56.2 reduce-scatter.8
  565.1 42.9 reduce-scatter.10

commit v4 on v3

--- a/solution.py
+++ b/solution.py
@@ -356,6 +356,7 @@
 SWAP = [(0, 1), (1, 0)]
 DIAGONAL = [(0, 3), (1, 2), (2, 1), (3, 0)]
 VMEM_SPEC = pl.BlockSpec(memory_space=pltpu.VMEM)
+SMEM_SPEC = pl.BlockSpec(memory_space=pltpu.SMEM)
 KERNEL = dict(
     compiler_params=pltpu.CompilerParams(vmem_limit_bytes=58 * 1024 * 1024),
     cost_estimate=pl.CostEstimate(flops=1000, bytes_accessed=1000, transcendentals=0),
@@ -408,45 +409,54 @@
     return values * cosine + pltpu.roll(values, HD // 2, 1) * sine
 
 
-def softmax_rows(query, key, key_pos, query_pos):
+def softmax_rows(query, key, start):
     scores = dot32(query, key, BY_COLS) * HD ** (-0.5)
-    allowed = key_pos <= query_pos
-    scores = jnp.where(allowed, scores, MASKED)
-    top = jnp.max(scores, axis=1, keepdims=True)
-    weights = jnp.exp(scores - top)
+    row = lax.broadcasted_iota(jnp.int32, scores.shape, 0) + start
+    scores = jnp.where(lax.broadcasted_iota(jnp.int32, scores.shape, 1) <= row, scores, MASKED)
+    weights = jnp.exp(scores - jnp.max(scores, axis=1, keepdims=True))
     return weights * (1.0 / jnp.sum(weights, axis=1, keepdims=True))
 
 
-def attention_forward_body(group, weight, cosine, sine, pos_col, pos_row, *refs):
+def rows_at(block, size):
+    return pl.ds(pl.multiple_of(block * size, size), size)
+
+
+def attention_forward_body(group, place, weight, cosine, sine, *refs):
     pieces, (query_out, key_out, value_out, heads_out, normed) = refs[:-5], refs[-5:]
     join_rows(pieces, normed)
-    steps = normed.shape[0] // ROWS
+    size, rows = pieces[0].shape[0], normed.shape[0]
 
     def project(step, carry):
-        at = row_block(step)
+        at = rows_at(step, 2 * size)
         qkv = dot32(normed[at, :], weight[...])
+        turned = [
+            low(turn(qkv[:, head_cut(head)], cosine[at, :], sine[at, :]))
+            for head in range(group + 1)
+        ]
+        value = low(qkv[:, head_cut(group + 1)])
+        for part in (0, 1):
+            own, to = slice(part * size, (part + 1) * size), rows_at(place[2 * step + part], size)
+            for head in range(group):
+                query_out[to, head_cut(head)] = turned[head][own]
+            key_out[to, :] = turned[group][own]
+            value_out[to, :] = value[own]
+        return carry
+
+    lax.fori_loop(0, rows // (2 * size), project, 0)
+    blocks = rows // size
+    for start in range(0, rows, ROWS):
+        at, seen = slice(start, start + ROWS), slice(0, start + ROWS)
         for head in range(group):
-            turned = turn(qkv[:, head_cut(head)], cosine[at, :], sine[at, :])
-            query_out[at, head_cut(head)] = low(turned)
-        key_out[at, :] = low(turn(qkv[:, head_cut(group)], cosine[at, :], sine[at, :]))
-        value_out[at, :] = low(qkv[:, head_cut(group + 1)])
-        return carry
-
-    def attend(step, carry):
-        at = row_block(step)
-        for head in range(group):
-            probs = softmax_rows(
-                query_out[at, head_cut(head)], key_out[...], pos_row[...], pos_col[at, :]
-            )
-            heads_out[at, head_cut(head)] = low(dot32(low(probs), value_out[...]))
-        return carry
-
-    lax.fori_loop(0, steps, project, 0)
-    lax.fori_loop(0, steps, attend, 0)
-
-
-def attention_forward(pieces, weight, cosine, sine, pos_col, pos_row):
-    rows, group = pos_col.shape[0], weight.shape[1] // HD - 2
+            probs = softmax_rows(query_out[at, head_cut(head)], key_out[seen, :], start)
+            result = low(dot32(low(probs), value_out[seen, :]))
+            for part in range(ROWS // size):
+                to = rows_at(place[blocks + start // size + part], size)
+                own = slice(part * size, (part + 1) * size)
+                heads_out[to, head_cut(head)] = result[own]
+
+
+def attention_forward(pieces, weight, cosine, sine, place):
+    rows, group = cosine.shape[0], weight.shape[1] // HD - 2
     return pl.pallas_call(
         functools.partial(attention_forward_body, group),
         out_shape=(
@@ -455,59 +465,61 @@
             low_shape(rows, HD),
             low_shape(rows, group * HD),
         ),
-        in_specs=[VMEM_SPEC] * (5 + len(pieces)),
+        in_specs=[SMEM_SPEC] + [VMEM_SPEC] * (3 + len(pieces)),
         out_specs=(VMEM_SPEC,) * 4,
         scratch_shapes=[pltpu.VMEM((rows, weight.shape[0]), jnp.bfloat16)],
         name="attention_forward",
         **KERNEL,
-    )(weight, cosine, sine, pos_col, pos_row, *pieces)
-
-
-def attention_backward_body(group, weight, query, key, value, cosine, sine, pos_col, pos_row, *refs):
+    )(place, weight, cosine, sine, *pieces)
+
+
+def attention_backward_body(group, place, weight, query, key, value, cosine, sine, *refs):
     pieces, (grad_qkv, grad_out, key_sum, value_sum) = refs[:-4], refs[-4:]
-    join_rows(pieces, grad_out)
-    steps = query.shape[0] // ROWS
+    size, rows = pieces[0].shape[0], query.shape[0]
+    blocks = rows // size
+    for number, piece in enumerate(pieces):
+        grad_out[rows_at(place[number], size), :] = piece[...]
     key_sum[...] = jnp.zeros_like(key_sum)
     value_sum[...] = jnp.zeros_like(value_sum)
 
-    def block(step, carry):
-        at = row_block(step)
+    def store_turned(start, values, cut, back):
+        for part in range(values.shape[0] // size):
+            to = rows_at(place[blocks + start // size + part], size)
+            own = values[part * size : (part + 1) * size]
+            if back:
+                own = low(turn(wide(own), cosine[to, :], -sine[to, :]))
+            grad_qkv[to, cut] = own
+
+    for start in range(0, rows, ROWS):
+        at, seen = slice(start, start + ROWS), slice(0, start + ROWS)
         grad_heads = low(dot32(grad_out[at, :], weight[...]))
         for head in range(group):
             cut = head_cut(head)
-            probs = softmax_rows(query[at, cut], key[...], pos_row[...], pos_col[at, :])
-            grad_probs = dot32(grad_heads[:, cut], value[...], BY_COLS)
+            probs = softmax_rows(query[at, cut], key[seen, :], start)
+            grad_probs = dot32(grad_heads[:, cut], value[seen, :], BY_COLS)
             delta = jnp.sum(probs * grad_probs, axis=1, keepdims=True)
             grad_scores = low(probs * (grad_probs - delta))
-            grad_query = wide(low(dot32(grad_scores, key[...]) * HD ** (-0.5)))
-            grad_qkv[at, cut] = low(turn(grad_query, cosine[at, :], -sine[at, :]))
-            key_sum[...] += dot32(grad_scores, query[at, cut], BY_ROWS)
-            value_sum[...] += dot32(low(probs), grad_heads[:, cut], BY_ROWS)
-        return carry
-
-    def finish(step, carry):
-        at = row_block(step)
-        grad_key = wide(low(key_sum[at, :] * HD ** (-0.5)))
-        grad_qkv[at, head_cut(group)] = low(turn(grad_key, cosine[at, :], -sine[at, :]))
-        grad_qkv[at, head_cut(group + 1)] = low(value_sum[at, :])
-        return carry
-
-    lax.fori_loop(0, steps, block, 0)
-    lax.fori_loop(0, steps, finish, 0)
-
-
-def attention_backward(pieces, weight, query, key, value, cosine, sine, pos_col, pos_row):
+            store_turned(start, low(dot32(grad_scores, key[seen, :]) * HD ** (-0.5)), cut, True)
+            key_sum[seen, :] += dot32(grad_scores, query[at, cut], BY_ROWS)
+            value_sum[seen, :] += dot32(low(probs), grad_heads[:, cut], BY_ROWS)
+    for start in range(0, rows, ROWS):
+        at = slice(start, start + ROWS)
+        store_turned(start, low(key_sum[at, :] * HD ** (-0.5)), head_cut(group), True)
+        store_turned(start, low(value_sum[at, :]), head_cut(group + 1), False)
+
+
+def attention_backward(pieces, weight, query, key, value, cosine, sine, place):
     rows, group = query.shape[0], query.shape[1] // HD
     return pl.pallas_call(
         functools.partial(attention_backward_body, group),
         out_shape=low_shape(rows, (group + 2) * HD),
-        in_specs=[VMEM_SPEC] * (8 + len(pieces)),
+        in_specs=[SMEM_SPEC] + [VMEM_SPEC] * (6 + len(pieces)),
         out_specs=VMEM_SPEC,
         scratch_shapes=[pltpu.VMEM((rows, weight.shape[0]), jnp.bfloat16)]
         + [pltpu.VMEM((rows, HD), jnp.float32)] * 2,
         name="attention_backward",
         **KERNEL,
-    )(weight, query, key, value, cosine, sine, pos_col, pos_row, *pieces)
+    )(place, weight, query, key, value, cosine, sine, *pieces)
 
 
 def stripes(weight, parts, number):
@@ -522,11 +534,9 @@
 
 
 def stripe_dot(rows, refs):
-    chunk = refs[0].shape[1]
-    total = dot32(rows[:, :chunk], refs[0][...], BY_COLS)
-    for x, ref in enumerate(refs[1:], 1):
-        total += dot32(rows[:, x * chunk : (x + 1) * chunk], ref[...], BY_COLS)
-    return total
+    weight = [ref[...] for ref in refs]
+    weight = weight[0] if len(refs) == 1 else jnp.concatenate(weight, axis=1)
+    return dot32(rows[...], weight, BY_COLS)
 
 
 def store_rows(outs, values):
@@ -553,34 +563,35 @@
     )(rows, *[weight] * parts)
 
 
+def by_halves(weight):
+    return weight.reshape(2, 2, weight.shape[0] // 4, weight.shape[1])
+
+
 def columns_of(weight):
-    shape = (weight.shape[0] // 4, weight.shape[1] // 2)
-
-    def place(y, step):
+    def place(step):
         at = jnp.minimum(step, 3)
-        return (2 * y + at // 2, at % 2)
-
-    return [pl.BlockSpec(shape, functools.partial(place, y)) for y in (0, 1)]
-
-
-def column_dot(rows, near, far):
-    depth = near.shape[0]
-    return dot32(rows[:, :depth], near[...]) + dot32(rows[:, depth:], far[...])
-
-
-def hidden_body(gate_near, gate_far, up_near, up_far, *refs):
+        return (0, at // 2, 0, at % 2)
+
+    return pl.BlockSpec((2, 1, weight.shape[0] // 4, weight.shape[1] // 2), place)
+
+
+def column_dot(rows, ref):
+    return dot32(rows[...], ref[...].reshape(rows.shape[1], ref.shape[3]))
+
+
+def hidden_body(gate_w, up_w, *refs):
     normed_p, (hidden_out, gate_slope, up_slope, normed) = refs[:-4], refs[-4:]
 
     @pl.when(pl.program_id(0) == 0)
     def _():
         join_rows(normed_p, normed)
 
-    gate = column_dot(normed, gate_near, gate_far)
-    up = column_dot(normed, up_near, up_far)
+    gate, up = column_dot(normed, gate_w), column_dot(normed, up_w)
     sig = jax.nn.sigmoid(gate)
-    hidden_out[...] = low(gate * sig * up)
-    gate_slope[...] = low(up * sig * (1.0 + gate * (1.0 - sig)))
-    up_slope[...] = low(gate * sig)
+    act = gate * sig
+    hidden_out[...] = low(act * up)
+    gate_slope[...] = low(up * (sig + act * (1.0 - sig)))
+    up_slope[...] = low(act)
 
 
 def hidden_pass(normed_p, gate_w, up_w):
@@ -590,41 +601,41 @@
         hidden_body,
         grid=(4,),
         out_shape=(low_shape(rows, units),) * 3,
-        in_specs=columns_of(gate_w) + columns_of(up_w) + [once(v.shape) for v in normed_p],
+        in_specs=[columns_of(gate_w), columns_of(up_w)] + [once(v.shape) for v in normed_p],
         out_specs=(pl.BlockSpec((rows, units // 4), lambda step: (0, step)),) * 3,
         scratch_shapes=[pltpu.VMEM((rows, width), jnp.bfloat16)],
         name="hidden_pass",
         **KERNEL,
-    )(gate_w, gate_w, up_w, up_w, *normed_p)
-
-
-def grad_hidden_body(down_near, down_far, gate_slope, up_slope, *refs):
-    gate_s, up_s, refs = refs[:2], refs[2:4], refs[4:]
-    count = (len(refs) - 5) // 2
-    cot_p, (grad_gate_out, grad_up_out, *outs) = refs[:count], refs[count:-3]
-    cot, grad_gate, grad_up = refs[-3:]
+    )(by_halves(gate_w), by_halves(up_w), *normed_p)
+
+
+def grad_hidden_body(down_w, gate_slope, up_slope, *refs):
+    stripe_refs, refs = refs[:4], refs[4:]
+    count = (len(refs) - 4) // 2
+    cot_p, (grad_gate_out, grad_up_out, *outs) = refs[:count], refs[count:-2]
+    cot, grads = refs[-2:]
     step, chunk = pl.program_id(0), grad_gate_out.shape[1]
 
     @pl.when(step == 0)
     def _():
         join_rows(cot_p, cot)
 
-    @pl.when(step < 4)
-    def _():
-        grad_hidden = column_dot(cot, down_near, down_far)
-        grad_gate_out[...] = low(grad_hidden * wide(gate_slope[...]))
-        grad_up_out[...] = low(grad_hidden * wide(up_slope[...]))
-
     for number in range(4):
 
         @pl.when(step == number)
-        def _(cut=slice(number * chunk, (number + 1) * chunk)):
-            grad_gate[:, cut] = grad_gate_out[...]
-            grad_up[:, cut] = grad_up_out[...]
+        def _(number=number):
+            grad_hidden = column_dot(cot, down_w)
+            slopes = (gate_slope, up_slope), (grad_gate_out, grad_up_out)
+            for part, (slope, out) in enumerate(zip(*slopes)):
+                grad = low(grad_hidden * wide(slope[...]))
+                out[...] = grad
+                start = (4 * part + number) * chunk
+                grads[:, start : start + chunk] = grad
 
     @pl.when(step >= 4)
     def _():
-        store_rows(outs, low(stripe_dot(grad_gate, gate_s) + stripe_dot(grad_up, up_s)))
+        weight = jnp.concatenate([ref[...] for ref in stripe_refs], axis=1)
+        store_rows(outs, low(dot32(grads[...], weight, BY_COLS)))
 
 
 def grad_hidden_pass(cot_p, gate_slope, up_slope, gate_w, up_w, down_w):
@@ -636,17 +647,17 @@
         grad_hidden_body,
         grid=(4 + width // ROWS,),
         out_shape=(low_shape(rows, units),) * 2 + tuple(low_shape(*v.shape) for v in cot_p),
-        in_specs=columns_of(down_w)
+        in_specs=[columns_of(down_w)]
         + [quarter] * 2
         + stripes(gate_w, 2, 4)
         + stripes(up_w, 2, 4)
         + [once(v.shape) for v in cot_p],
         out_specs=(quarter,) * 2 + (stripe,) * len(cot_p),
         scratch_shapes=[pltpu.VMEM((rows, width), jnp.bfloat16)]
-        + [pltpu.VMEM((rows, units), jnp.bfloat16)] * 2,
+        + [pltpu.VMEM((rows, 2 * units), jnp.bfloat16)],
         name="grad_hidden_pass",
         **KERNEL,
-    )(down_w, down_w, gate_slope, up_slope, gate_w, gate_w, up_w, up_w, *cot_p)
+    )(by_halves(down_w), gate_slope, up_slope, gate_w, gate_w, up_w, up_w, *cot_p)
 
 
 def term_body(*refs):
@@ -807,28 +818,62 @@
     )(stream_in, grad_middle, *parts)
 
 
-def pack_body(gain, gate_up, down, gate_out, up_out, down_out):
-    gate_out[...] = low(wide(gate_up[:, 0, :]) * gain[...])
+def pack_body(gain, gate_up, out):
+    out[...] = low(wide(gate_up[:, 0, :]) * gain[...])
+
+
+def pack_more_body(gain, gate_up, down, up_out, down_out):
     up_out[...] = low(wide(gate_up[:, 1, :]) * gain[...])
     down_out[...] = down[...]
 
 
-def pack_pass(gain, gate_up, down, groups):
-    rows, chunk = down.shape[0], down.shape[1] // groups
-    out = pl.BlockSpec((rows, chunk), lambda g: (g, 0))
-    return pl.pallas_call(
-        pack_body,
+def pack_pass(body, outs, groups, gain, gate_up, *down):
+    rows, chunk = gate_up.shape[0], gate_up.shape[2] // groups
+    return pl.pallas_call(
+        body,
         grid=(groups,),
-        out_shape=(low_shape(groups * rows, chunk),) * 3,
+        out_shape=(low_shape(groups * rows, chunk),) * outs,
         in_specs=[
             pl.BlockSpec((rows, 1), lambda g: (0, 0)),
             pl.BlockSpec((rows, 2, chunk), lambda g: (0, 0, g)),
-            pl.BlockSpec((rows, chunk), lambda g: (0, g)),
+        ]
+        + [pl.BlockSpec((rows, chunk), lambda g: (0, g))] * len(down),
+        out_specs=(pl.BlockSpec((rows, chunk), lambda g: (g, 0)),) * outs,
+        name="pack_pass",
+        **KERNEL,
+    )(gain, gate_up, *down)
+
+
+def qkv_pack_body(gain, query, key, value, out):
+    start = 0
+    for part in (query, key, value):
+        cut = slice(start, start + part.shape[1])
+        rows = low(wide(part[...]) * gain[...])
+        for plane in range(out.shape[0]):
+            out[plane, 0, :, cut] = rows
+        start += part.shape[1]
+
+
+def qkv_pack_pass(gain, weight, planes, groups):
+    rows = weight.shape[0]
+    query, rest = H * HD // groups, KV * HD // groups
+    first = H * HD // rest
+    block = (planes, 1, rows, query + 2 * rest)
+    out = pl.pallas_call(
+        qkv_pack_body,
+        grid=(groups,),
+        out_shape=jax.ShapeDtypeStruct((planes, groups, *block[2:]), jnp.bfloat16),
+        in_specs=[
+            pl.BlockSpec((rows, 1), lambda g: (0, 0)),
+            pl.BlockSpec((rows, query), lambda g: (0, g)),
+            pl.BlockSpec((rows, rest), lambda g: (0, first + g)),
+            pl.BlockSpec((rows, rest), lambda g: (0, first + groups + g)),
         ],
-        out_specs=(out,) * 3,
-        name="pack_pass",
-        **KERNEL,
-    )(gain, gate_up, down)
+        out_specs=pl.BlockSpec(block, lambda g: (0, g, 0, 0)),
+        name="qkv_pack_pass",
+        **KERNEL,
+    )(gain, weight, weight, weight)
+    return out.reshape(-1, block[3])
 
 
 def unpack_body(gain, weight, gate, up, out, gain_sum):
@@ -861,6 +906,23 @@
         name="unpack_pass",
         **KERNEL,
     )(gain, weight, gate, up)
+
+
+def side_by_side_body(part, out):
+    out[...] = wide(part[...])
+
+
+def side_by_side(values, groups):
+    rows, cols = values.shape[0] // groups, values.shape[1]
+    return pl.pallas_call(
+        side_by_side_body,
+        grid=(groups,),
+        out_shape=wide_shape(rows, groups * cols),
+        in_specs=[pl.BlockSpec((rows, cols), lambda g: (g, 0))],
+        out_specs=pl.BlockSpec((rows, cols), lambda g: (0, g)),
+        name="side_by_side",
+        **KERNEL,
+    )(values)
 
 
 def exchange(values, axes):
@@ -955,13 +1017,12 @@
         jnp.concatenate([gain_own, gain_peer], axis=1),
         jnp.concatenate([gain_peer, gain_own], axis=1),
     ).reshape(mlp_rows, 1)
-    gate_rows, up_rows, down_rows = pack_pass(gain_m, gate_up_weight, down_weight, hgroups)
+    (gate_rows,) = pack_pass(pack_body, 1, hgroups, gain_m, gate_up_weight)
     out_rows = out_weight.reshape(d_rows, plane, q_cols).transpose(1, 0, 2).reshape(-1, q_cols)
     out_here = exchange(out_rows, PLANE_AXES)
     normed, cot_split = prepare_pass(layer_input, output_cotangent)
-    cot_1 = shift(cot_split, 1)
-    gate_rows, up_rows, down_rows, out_here, normed, cot_split, cot_1, qkv_weight = together(
-        gate_rows, up_rows, down_rows, out_here, normed, cot_split, cot_1, qkv_weight
+    gate_rows, gain_m, out_here, normed, cot_split, qkv_weight, down_weight = together(
+        gate_rows, gain_m, out_here, normed, cot_split, qkv_weight, down_weight
     )
 
     def spread(here):
@@ -971,15 +1032,10 @@
     gate_here = exchange(gate_rows, GROUP_AXES)
     normed_p = plane_hop(normed)
     gain_a = wide(attn_gain)[:, None]
-    folded = low(wide(qkv_weight) * gain_a)
-    by_group = jnp.concatenate(
-        [
-            part.reshape(d_rows, plane, -1)
-            for part in jnp.split(folded, [H * HD, (H + KV) * HD], axis=1)
-        ],
-        axis=2,
-    ).transpose(1, 0, 2)
-    qkv_rows = jnp.broadcast_to(by_group[None], (nz, *by_group.shape)).reshape(-1, own_cols)
+    qkv_rows = qkv_pack_pass(gain_a, qkv_weight, nz, plane)
+    up_rows, down_rows = pack_pass(
+        pack_more_body, 2, hgroups, gain_m, gate_up_weight, down_weight
+    )
     gate_here, normed_p, qkv_rows, up_rows, down_rows, cot_split = together(
         gate_here, normed_p, qkv_rows, up_rows, down_rows, cot_split
     )
@@ -995,7 +1051,10 @@
     gate_w = spread(gate_here)
     wq = exchange(qkv_rows, ALL_AXES)
     normed_p = core_hop(normed_p)
-    rows_info = (cosine, sine, positions[:, None], positions[None, :])
+    place = positions[::tok] // span_size
+    ordered = place[None, :] == block[:, None]
+    place = jnp.concatenate([place, jnp.sum(jnp.where(ordered, block[None, :], 0), axis=1)])
+    rows_info = (cosine, sine, place)
     wq, normed_p, up_rows, rows_info = together(wq, normed_p, up_rows, rows_info)
 
     up_here = exchange(up_rows, GROUP_AXES)
@@ -1011,37 +1070,39 @@
     cot_3 = shift(cot_split, 3)
     attn_parts, down_here, cot_3, cot_split = together(attn_parts, down_here, cot_3, cot_split)
 
+    middle, zhat, squares_a = middle_pass(layer_input, attn_parts)
+    zhat, down_here = together(zhat, down_here)
     down_w = spread(down_here)
-    middle, zhat, squares_a = middle_pass(layer_input, attn_parts)
-    zhat_p = column_hop(zhat)
+    zhat_p = core_hop(column_hop(zhat))
     zhat_p, gate_w, up_w, cot_split = together(zhat_p, gate_w, up_w, cot_split)
-    zhat_p, cot_split = together(core_hop(zhat_p), cot_split)
-
-    cot_p = (cot_split, cot_1, shift(cot_split, 2), cot_3)
+
+    cot_2 = shift(cot_split, 2)
     hidden, gate_slope, up_slope = hidden_pass(zhat_p, gate_w, up_w)
-    hidden, cot_p, gate_slope, down_w = together(hidden, cot_p, gate_slope, down_w)
-
-    cot_p = core_hop(cot_p)
+    hidden, cot_2, cot_split, gate_slope, down_w = together(
+        hidden, cot_2, cot_split, gate_slope, down_w
+    )
+
+    cot_p = core_hop((cot_split, shift(cot_split, 1), cot_2, cot_3))
     mlp_parts = core_back(by_cols_pass(hidden, down_w, 2, 2 * nz, "down_pass"))
+    cot_p, mlp_parts = together(cot_p, mlp_parts)
+    mlp_1 = shift(mlp_parts[1], -1)
     down_t = term_pass(cot_p, hidden, 2, 2)
-    cot_p, mlp_parts, down_t = together(cot_p, mlp_parts, down_t)
+    mlp_1, mlp_parts, down_t = together(mlp_1, mlp_parts, down_t)
 
     def side_sum(term):
         return lax.psum_scatter(term, SIDE_AXES, scatter_dimension=0, tiled=True)
 
     down_t = side_sum(down_t)
-    mlp_2, mlp_3 = shift(mlp_parts[2], -2), shift(mlp_parts[3], -3)
+    mlp_2 = shift(mlp_parts[2], -2)
     grad_gate, grad_up, *gz_parts = grad_hidden_pass(
         cot_p, gate_slope, up_slope, gate_w, up_w, down_w
     )
-    gz_parts, grad_gate, mlp_2, mlp_3, mlp_parts = together(
-        gz_parts, grad_gate, mlp_2, mlp_3, mlp_parts
-    )
+    gz_parts, grad_gate, mlp_2, mlp_parts = together(gz_parts, grad_gate, mlp_2, mlp_parts)
 
     gz_parts = core_back(gz_parts)
-    mlp_1 = shift(mlp_parts[1], -1)
+    mlp_3 = shift(mlp_parts[3], -3)
     gate_t = term_pass(zhat_p, grad_gate, 2, 2)
-    gz_parts, gate_t, mlp_1, mlp_parts = together(gz_parts, gate_t, mlp_1, mlp_parts)
+    gz_parts, gate_t, mlp_3, mlp_parts = together(gz_parts, gate_t, mlp_3, mlp_parts)
 
     gate_t = side_sum(gate_t)
     gz_parts = column_back(gz_parts)
@@ -1069,8 +1130,7 @@
     out_term = term_pass(grad_out_p, heads, 2, 1)
     qkv_sum = exchange(qkv_term, ALL_AXES)
     gx_parts = plane_back(gx_parts)
-    down_back = down_back.reshape(hgroups, mlp_rows, hchunk)
-    down_grad = wide(down_back.transpose(1, 0, 2).reshape(mlp_rows, ff_local))
+    down_grad = side_by_side(down_back, hgroups)
     gx_parts, qkv_sum, up_t, out_term, down_grad = together(
         gx_parts, qkv_sum, up_t, out_term, down_grad
     )
@@ -1078,11 +1138,7 @@
     out_term = lax.psum_scatter(out_term, "dp", scatter_dimension=0, tiled=True)
     up_back = exchange(up_t, GROUP_AXES)
     input_grad = input_grad_pass(layer_input, grad_middle, gx_parts)
-    up_back, input_grad, out_term = together(up_back, input_grad, out_term)
-
-    out_sum = exchange(out_term, PLANE_AXES)
-    gate_up_grad, gain_sum = unpack_pass(gain_m, gate_up_weight, gate_back, up_back, hgroups)
-    out_sum, gate_up_grad, gain_sum = together(out_sum, gate_up_grad, gain_sum)
+
     def plane_sum(arrived, cols):
         return jnp.sum(wide(arrived.reshape(nz, plane, d_rows, cols)), axis=0).transpose(1, 0, 2)
 
@@ -1097,6 +1153,13 @@
     )
     qkv_grad = qkv_sum * gain_a
     attn_gain_grad = jnp.sum(qkv_sum * wide(qkv_weight), axis=1)
+    up_back, input_grad, out_term, qkv_grad, attn_gain_grad = together(
+        up_back, input_grad, out_term, qkv_grad, attn_gain_grad
+    )
+
+    out_sum = exchange(out_term, PLANE_AXES)
+    gate_up_grad, gain_sum = unpack_pass(gain_m, gate_up_weight, gate_back, up_back, hgroups)
+    out_sum, gate_up_grad, gain_sum = together(out_sum, gate_up_grad, gain_sum)
     gain_halves = gain_sum.reshape(2, -1)
     gain_keep = jnp.where(x_at == 0, gain_halves[0], gain_halves[1])
     gain_send = jnp.where(x_at == 0, gain_halves[1], gain_halves[0])

time: 640 us -> 636 us (level); the launches traced: 638 us -> 624 us
  local copies, waits for them, and re-layouts: 28.3 us -> 17.5 us
  waiting for transfers between devices: 308 us -> 300 us
  Pallas kernels: 178 us -> 185 us
    pallas_call x1 -> x4, Pallas kernels: 6.84 us -> 22.4 us  [the longest x2 11.8 us: pack_pass(): pl.pallas_call(body, grid=(groups,), out_shape=(low_shape(groups * rows,...]
    ppermute x46, waiting for transfers between devices: 123 us -> 116 us  [swap(): return lax.ppermute(values, axes if len(axes) > 1 else axes[0], pairs)]
    ppermute x12, waiting for transfers between devices: 68.5 us -> 61.8 us  [shift(): lax.ppermute(values, 'dp', [(i, (i + by) % count) for i in range(count)])]
    unnamed x133 -> x138, local copies, waits for them, and re-layouts: 15.7 us -> 13.9 us
  transfers between devices with their start and end apart: 77 -> 77, of which waited for: 33 -> 32; matrix products, arithmetic and copies ran while one was open for 4% -> 2% of each run, Pallas kernels for 27% -> 30%
where the time goes in v4:
time: 636 us; the launch traced here: 624 us
  waiting for transfers between devices  300 us (47%)
  Pallas kernels  185 us (29%)
  starting transfers between devices  96.5 us (15%)
  local copies, waits for them, and re-layouts  17.5 us (3%)
  between operations  15.2 us (2%)
  other arithmetic  9.63 us (2%)
    all_to_all x11, waiting for transfers between devices, exchange(): return lax.all_to_all(values, axes, split_axis=0, concat_axis=0, tiled=True)  118 us
    ppermute x46, waiting for transfers between devices, swap(): return lax.ppermute(values, axes if len(axes) > 1 else axes[0], pairs)  116 us
    ppermute x12, waiting for transfers between devices, shift(): lax.ppermute(values, 'dp', [(i, (i + by) % count) for i in range(count)])  61.8 us
    all_to_all x11, starting transfers between devices, exchange(): return lax.all_to_all(values, axes, split_axis=0, concat_axis=0, tiled=True)  49.7 us
    pallas_call x5, Pallas kernels, term_pass(): pl.pallas_call(term_body, grid=(row_parts, col_parts), out_shape=low_shap...  37.4 us
    ppermute x46, starting transfers between devices, swap(): return lax.ppermute(values, axes if len(axes) > 1 else axes[0], pairs)  27.1 us
    pallas_call x3, Pallas kernels, by_cols_pass(): pl.pallas_call(functools.partial(by_cols_body, parts), grid=(width // ROW...  24.1 us
    pallas_call x1, Pallas kernels, grad_hidden_pass(): pl.pallas_call(grad_hidden_body, grid=(4 + width // ROWS,), out_shape=(lo...  22.4 us
  transfers between devices with their start and end apart: 77, of which 32 were waited for; matrix products, arithmetic and copies ran while one was open for 2% of the time, Pallas kernels for 30%

profile of v4, /device:TPU:0, one launch (start us, length us, event | category | flops | bytes accessed | tf_op | source)
XLA Modules:
  0.0 624.4 jit_solution(16623979334703880438)
XLA Ops:
  46.5 10.9 %collective-permute-done.2.refs_2_ = bf16[128,2048]{1,0:T(8,128)(2,1)S(1)} collective-permute-done((bf16[128,2048]{1,0:T(8,128)(2,1)S(1)}, bf16[128,2048]{1,0:T(8,128)(2,1)S(1)}, u32[]{:S(2)}, u32[]{:S(2)}) %collective-permute-start.2) | collective-permute-done | bytes 524320 | tf_op jit(solution)/shard_map/ppermute | solution.py:942
  57.7 12.4 %all-to-all-done.1 = bf16[8,128,512]{2,1,0:T(8,128)(2,1)S(1)} async-done(((bf16[8,128,512]{2,1,0:T(8,128)(2,1)}), bf16[8,128,512]{2,1,0:T(8,128)(2,1)S(1)}, u32[]{:S(2)}, u32[]{:S(2)}) %all-to-all-start.1) | async-done | bytes 1048608 | tf_op jit(solution)/shard_map/all_to_all | solution.py:929
  82.0 41.6 %all-to-all-done.2 = bf16[32,64,512]{2,1,0:T(8,128)(2,1)S(1)} async-done(((bf16[32,64,512]{2,1,0:T(8,128)(2,1)}), bf16[32,64,512]{2,1,0:T(8,128)(2,1)S(1)}, u32[]{:S(2)}, u32[]{:S(2)}) %all-to-all-start.2) | async-done | bytes 2097184 | tf_op jit(solution)/shard_map/all_to_all | solution.py:929
  127.2 11.7 %attention_forward.1 = (bf16[1024,256]{1,0:T(8,128)(2,1)}, bf16[1024,128]{1,0:T(8,128)(2,1)}, bf16[1024,128]{1,0:T(8,128)(2,1)}, bf16[1024,256]{1,0:T(8,128)(2,1)}) custom-call(s32[16]{0:T(128)} %pad_add_fusion.place, bf16[2048,512]{1,0:T(8,128)(2,1)} %bitcast.107, f32[1024,128]{1,0:T(8,128)} %get-tuple-element.243.cosine, ...), custom_call_target="tpu_custom_call" | custom-call | flops 1000 | bytes 1000 | tf_op jit(solution)/shard_map/attention_forward/pallas_call | solution.py:460
  168.0 15.8 %collective-permute-done.12.refs_1_ = bf16[128,2048]{1,0:T(8,128)(2,1)S(1)} collective-permute-done((bf16[128,2048]{1,0:T(8,128)(2,1)}, bf16[128,2048]{1,0:T(8,128)(2,1)S(1)}, u32[]{:S(2)}, u32[]{:S(2)}) %collective-permute-start.12) | collective-permute-done | bytes 524320 | tf_op jit(solution)/shard_map/ppermute | solution.py:942
  188.8 9.8 %collective-permute-done.14.refs_3_ = bf16[128,2048]{1,0:T(8,128)(2,1)S(1)} collective-permute-done((bf16[128,2048]{1,0:T(8,128)(2,1)}, bf16[128,2048]{1,0:T(8,128)(2,1)S(1)}, u32[]{:S(2)}, u32[]{:S(2)}) %collective-permute-start.14) | collective-permute-done | bytes 524320 | tf_op jit(solution)/shard_map/ppermute | solution.py:942
  207.7 11.3 %collective-permute-done.18.refs_3_ = bf16[128,2048]{1,0:T(8,128)(2,1)S(1)} collective-permute-done((bf16[128,2048]{1,0:T(8,128)(2,1)}, bf16[128,2048]{1,0:T(8,128)(2,1)S(1)}, u32[]{:S(2)}, u32[]{:S(2)}) %collective-permute-start.18) | collective-permute-done | bytes 524320 | tf_op jit(solution)/shard_map/ppermute | solution.py:955
  219.0 31.9 %collective-permute-done.17.refs_2_ = bf16[128,2048]{1,0:T(8,128)(2,1)S(1)} collective-permute-done((bf16[128,2048]{1,0:T(8,128)(2,1)}, bf16[128,2048]{1,0:T(8,128)(2,1)S(1)}, u32[]{:S(2)}, u32[]{:S(2)}) %collective-permute-start.17) | collective-permute-done | bytes 524320 | tf_op jit(solution)/shard_map/ppermute | solution.py:955
  255.7 14.4 %hidden_pass.1 = (bf16[1024,1024]{1,0:T(8,128)(2,1)}, bf16[1024,1024]{1,0:T(8,128)(2,1)}, bf16[1024,1024]{1,0:T(8,128)(2,1)}) custom-call(bf16[2,2,1024,512]{3,2,1,0:T(8,128)(2,1)} %bitcast.104, bf16[2,2,1024,512]{3,2,1,0:T(8,128)(2,1)} %bitcast.105, bf16[128,2048]{1,0:T(8,128)(2,1)} %get-tuple-element.289.refs_0_, bf16[128,2048]{1,0:T(8,128)(2,1)} %copy-done.4, ...), custom_call_target="tpu_custom_call" | custom-call | flops 1000 | bytes 1000 | tf_op jit(solution)/shard_map/hidden_pass/pallas_call | solution.py:600
  270.1 9.6 %collective-permute-done.23.refs_6_.refs_2_ = bf16[128,2048]{1,0:T(8,128)(2,1)} collective-permute-done((bf16[128,2048]{1,0:T(8,128)(2,1)}, bf16[128,2048]{1,0:T(8,128)(2,1)}, u32[]{:S(2)}, u32[]{:S(2)}) %collective-permute-start.23) | collective-permute-done | bytes 524320 | tf_op jit(solution)/shard_map/ppermute | solution.py:955
  285.3 9.6 %down_pass.1 = (bf16[128,2048]{1,0:T(8,128)(2,1)}, bf16[128,2048]{1,0:T(8,128)(2,1)}, bf16[128,2048]{1,0:T(8,128)(2,1)}, bf16[128,2048]{1,0:T(8,128)(2,1)}, bf16...) custom-call(bf16[1024,1024]{1,0:T(8,128)(2,1)} %get-tuple-element.307., ...), custom_call_target="tpu_custom_call" | custom-call | flops 1000 | bytes 1000 | tf_op jit(solution)/shard_map/down_pass/pallas_call | solution.py:555
  306.8 9.0 %term_pass.5 = bf16[4096,512]{1,0:T(8,128)(2,1)} custom-call(bf16[128,2048]{1,0:T(8,128)(2,1)} %get-tuple-element.320.refs_4_.refs_0_, bf16[128,2048]{1,0:T(8,128)(2,1)} %copy-done.16, bf16[128,2048]{1,0:T(8,128)(2,1)} %collective-permute-done.23.refs_6_.refs_2_, bf16[128,2048]{1,0:T(8,128)(2,1)} %collective-permute-done.15.refs_7_.refs_3_, ...), custom_call_target="tpu_custom_call" | custom-call | flops 1000 | bytes 1000 | tf_op jit(solution)/shard_map/term_pass/pallas_call | solution.py:672
  321.4 22.4 %grad_hidden_pass.1 = (bf16[1024,1024]{1,0:T(8,128)(2,1)}, bf16[1024,1024]{1,0:T(8,128)(2,1)}, bf16[128,2048]{1,0:T(8,128)(2,1)}, bf16[128,2048]{1,0:T(8,128)(2,...) custom-call(bf16[2,2,1024,512]{3,2,1,0:T(8,128)(2,1)} %bitcast.106, ...), custom_call_target="tpu_custom_call" | custom-call | flops 1000 | bytes 1000 | tf_op jit(solution)/shard_map/grad_hidden_pass/pallas_call | solution.py:646
  347.6 9.3 %term_pass.6 = bf16[4096,512]{1,0:T(8,128)(2,1)} custom-call(bf16[128,2048]{1,0:T(8,128)(2,1)} %get-tuple-element.289.refs_0_, bf16[128,2048]{1,0:T(8,128)(2,1)} %copy-done.4, bf16[128,2048]{1,0:T(8,128)(2,1)} %copy-done.3, bf16[128,2048]{1,0:T(8,128)(2,1)} %copy-done.2, bf16[128,2048]{1,0:T(8,128)(2,1)} %copy-done.5, ...), custom_call_target="tpu_custom_call" | custom-call | flops 1000 | bytes 1000 | tf_op jit(solution)/shard_map/term_pass/pallas_call | solution.py:672
  375.0 9.0 %term_pass.7 = bf16[4096,512]{1,0:T(8,128)(2,1)} custom-call(bf16[128,2048]{1,0:T(8,128)(2,1)} %get-tuple-element.289.refs_0_, bf16[128,2048]{1,0:T(8,128)(2,1)} %copy-done.4, bf16[128,2048]{1,0:T(8,128)(2,1)} %copy-done.3, bf16[128,2048]{1,0:T(8,128)(2,1)} %copy-done.2, bf16[128,2048]{1,0:T(8,128)(2,1)} %copy-done.5, ...), custom_call_target="tpu_custom_call" | custom-call | flops 1000 | bytes 1000 | tf_op jit(solution)/shard_map/term_pass/pallas_call | solution.py:672
  384.1 28.1 %all-to-all-done.5 = f32[32,1,128]{2,1,0:T(1,128)S(1)} async-done(((f32[32,1,128]{2,1,0:T(1,128)}), f32[32,1,128]{2,1,0:T(1,128)S(1)}, u32[]{:S(2)}, u32[]{:S(2)}) %all-to-all-start.5) | async-done | bytes 16416 | tf_op jit(solution)/shard_map/all_to_all | solution.py:929
  425.4 14.2 %collective-permute-done.45.refs_3_ = bf16[128,2048]{1,0:T(8,128)(2,1)S(1)} collective-permute-done((bf16[128,2048]{1,0:T(8,128)(2,1)}, bf16[128,2048]{1,0:T(8,128)(2,1)S(1)}, u32[]{:S(2)}, u32[]{:S(2)}) %collective-permute-start.45) | collective-permute-done | bytes 524320 | tf_op jit(solution)/shard_map/ppermute | solution.py:942
  439.6 10.2 %collective-permute-done.44.refs_2_ = bf16[128,2048]{1,0:T(8,128)(2,1)S(1)} collective-permute-done((bf16[128,2048]{1,0:T(8,128)(2,1)}, bf16[128,2048]{1,0:T(8,128)(2,1)S(1)}, u32[]{:S(2)}, u32[]{:S(2)}) %collective-permute-start.44) | collective-permute-done | bytes 524320 | tf_op jit(solution)/shard_map/ppermute | solution.py:942
  459.8 13.9 %attention_backward.1.rows.refs_8_ = bf16[1024,512]{1,0:T(8,128)(2,1)} custom-call(s32[16]{0:T(128)} %pad_add_fusion.place, bf16[2048,256]{1,0:T(8,128)(2,1)} %all-gather.5.cloned.1.call-done.refs_0_.weight, bf16[1024,256]{1,0:T(8,128)(2,1)} %get-tuple-element.364.query, bf16[1024,128]{1,0:T(8,128)(2,1)} %get-tuple-element.365.key, ...), custom_call_target="tpu_custom_call" | custom-call | flops 1000 | bytes 1000 | tf_op jit(solution)/shard_map/attention_backward/pallas_call | solution.py:513
  473.7 7.6 %qkv_back_pass.1 = (bf16[128,2048]{1,0:T(8,128)(2,1)}, bf16[128,2048]{1,0:T(8,128)(2,1)}, bf16[128,2048]{1,0:T(8,128)(2,1)}, bf16[128,2048]{1,0:T(8,128)(2,1)}, ...) custom-call(bf16[1024,512]{1,0:T(8,128)(2,1)} %attention_backward.1., ...), custom_call_target="tpu_custom_call" | custom-call | flops 1000 | bytes 1000 | tf_op jit(solution)/shard_map/qkv_back_pass/pallas_call | solution.py:555
  512.5 26.2 %collective-permute-done.54.refs_1_ = bf16[128,2048]{1,0:T(8,128)(2,1)S(1)} collective-permute-done((bf16[128,2048]{1,0:T(8,128)(2,1)}, bf16[128,2048]{1,0:T(8,128)(2,1)S(1)}, u32[]{:S(2)}, u32[]{:S(2)}) %collective-permute-start.54) | collective-permute-done | bytes 524320 | tf_op jit(solution)/shard_map/ppermute | solution.py:942
  541.3 10.9 %collective-permute-done.56.refs_3_ = bf16[128,2048]{1,0:T(8,128)(2,1)} collective-permute-done((bf16[128,2048]{1,0:T(8,128)(2,1)}, bf16[128,2048]{1,0:T(8,128)(2,1)}, u32[]{:S(2)}, u32[]{:S(2)}) %collective-permute-start.56) | collective-permute-done | bytes 524320 | tf_op jit(solution)/shard_map/ppermute | solution.py:942
  565.0 35.7 %all-to-all-done.9 = bf16[8,128,512]{2,1,0:T(8,128)(2,1)S(1)} async-done(((bf16[8,128,512]{2,1,0:T(8,128)(2,1)}), bf16[8,128,512]{2,1,0:T(8,128)(2,1)S(1)}, u32[]{:S(2)}, u32[]{:S(2)}) %all-to-all-start.9) | async-done | bytes 1048608 | tf_op jit(solution)/shard_map/all_to_all | solution.py:929
  604.7 7.7 %unpack_pass.1 = (f32[128,2,4096]{2,1,0:T(2,128)}, f32[128,1]{1,0:T(8,128)}) custom-call(f32[128,1]{1,0:T(8,128)} %broadcast_select_fusion.gain, bf16[128,2,4096]{2,1,0:T(2,128)(2,1)} %weight.1, bf16[1024,512]{1,0:T(8,128)(2,1)} %bitcast.118, bf16[1024,512]{1,0:T(8,128)(2,1)} %bitcast.119), custom_call_target="tpu_custom_call" | custom-call | flops 1000 | bytes 1000 | tf_op jit(solution)/shard_map/unpack_pass/pallas_call | solution.py:900
  (332 shorter events, 226.2 us)
Async XLA Ops:
  25.0 45.1 %all-to-all-start.1 = ((bf16[8,128,512]{2,1,0:T(8,128)(2,1)}), bf16[8,128,512]{2,1,0:T(8,128)(2,1)S(1)}, u32[]{:S(2)}, u32[]{:S(2)}) async-start(bf16[8,128,512]{2,1,0:T(8,128)(2,1)} %bitcast.112), calls=%async_computation.1 | async-start | bytes 2097152 | tf_op jit(solution)/shard_map/all_to_all | solution.py:929
  29.9 109.0 %all-gather.5.cloned.1.call-start = ((), (), s32[]{:S(2)}) async-start(), calls=%async_computation.15 | async-start | bytes 1310720 | tf_op jit(solution)/shard_map/all_gather | solution.py:1031
  30.6 220.8 %all-gather.7.cloned.1.call-start = ((), (), s32[]{:S(2)}) async-start(), calls=%async_computation.16 | async-start | bytes 5242880 | tf_op jit(solution)/shard_map/all_gather | solution.py:1029
  71.1 52.4 %all-to-all-start.2 = ((bf16[32,64,512]{2,1,0:T(8,128)(2,1)}), bf16[32,64,512]{2,1,0:T(8,128)(2,1)S(1)}, u32[]{:S(2)}, u32[]{:S(2)}) async-start(bf16[32,64,512]{2,1,0:T(8,128)(2,1)} %bitcast.109), calls=%async_computation.2 | async-start | bytes 4194304 | tf_op jit(solution)/shard_map/all_to_all | solution.py:929
  127.1 126.5 %all-gather.9.cloned.1.call-start = ((), (), s32[]{:S(2)}) async-start(), calls=%async_computation.17 | async-start | bytes 5242880 | tf_op jit(solution)/shard_map/all_gather | solution.py:1029
  155.6 43.0 %all-to-all-start.4 = ((bf16[8,128,512]{2,1,0:T(8,128)(2,1)}), bf16[8,128,512]{2,1,0:T(8,128)(2,1)S(1)}, u32[]{:S(2)}, u32[]{:S(2)}) async-start(bf16[8,128,512]{2,1,0:T(8,128)(2,1)} %bitcast.17), calls=%async_computation.4 | async-start | bytes 2097152 | tf_op jit(solution)/shard_map/all_to_all | solution.py:929
  160.6 123.2 %all-gather.11.cloned.1.call-start = ((), (), s32[]{:S(2)}) async-start(), calls=%async_computation.18 | async-start | bytes 5242880 | tf_op jit(solution)/shard_map/all_gather | solution.py:1029
  202.7 209.6 %reduce-scatter.5.cloned.1.call-start = ((), (), s32[]{:S(2)}) async-start(), calls=%async_computation.19 | async-start | bytes 5242880 | tf_op jit(solution)/shard_map/reduce_scatter | solution.py:1093
  206.2 44.6 %collective-permute-start.17 = (bf16[128,2048]{1,0:T(8,128)(2,1)}, bf16[128,2048]{1,0:T(8,128)(2,1)S(1)}, u32[]{:S(2)}, u32[]{:S(2)}) collective-permute-start(bf16[128,2048]{1,0:T(8,128)(2,1)} %get-tuple-element.289.refs_0_), channel_id=1, source_target_pairs={{0,16},{8,24},{16,0},{24,8},{1,17},{9,25},{17,1},{25,9},{2,18},{10... | collective-permute-start | bytes 1572872 | tf_op jit(solution)/shard_map/ppermute | solution.py:955
  206.3 44.6 %collective-permute-start.16 = (bf16[128,2048]{1,0:T(8,128)(2,1)}, bf16[128,2048]{1,0:T(8,128)(2,1)S(1)}, u32[]{:S(2)}, u32[]{:S(2)}) collective-permute-start(bf16[128,2048]{1,0:T(8,128)(2,1)} %get-tuple-element.289.refs_0_), channel_id=1, source_target_pairs={{0,8},{8,16},{16,24},{24,0},{1,9},{9,17},{17,25},{25,1},{2,10},{10... | collective-permute-start | bytes 1572872 | tf_op jit(solution)/shard_map/ppermute | solution.py:955
  207.7 43.7 %collective-permute-start.19 = (bf16[128,2048]{1,0:T(8,128)(2,1)}, bf16[128,2048]{1,0:T(8,128)(2,1)S(1)}, u32[]{:S(2)}, u32[]{:S(2)}) collective-permute-start(bf16[128,2048]{1,0:T(8,128)(2,1)} %get-tuple-element.289.refs_0_), channel_id=1, source_target_pairs={{0,2},{2,0},{1,3},{3,1},{4,6},{6,4},{5,7},{7,5},{8,10},{10,8},{9,1... | collective-permute-start | bytes 1572872 | tf_op jit(solution)/shard_map/ppermute | solution.py:942
  320.3 129.5 %reduce-scatter.7.cloned.1.call-start = ((), (), s32[]{:S(2)}) async-start(), calls=%async_computation.20 | async-start | bytes 5242880 | tf_op jit(solution)/shard_map/reduce_scatter | solution.py:1093
  363.4 48.9 %collective-permute-start.40 = (bf16[128,2048]{1,0:T(8,128)(2,1)}, bf16[128,2048]{1,0:T(8,128)(2,1)S(1)}, u32[]{:S(2)}, u32[]{:S(2)}) collective-permute-start(bf16[128,2048]{1,0:T(8,128)(2,1)} %get-tuple-element.368), channel_id=1, source_target_pairs={{0,24},{8,0},{16,8},{24,16},{1,25},{9,1},{17,9},{25,17},{2,26},{10... | collective-permute-start | bytes 1572872 | tf_op jit(solution)/shard_map/ppermute | solution.py:955
  366.1 46.2 %collective-permute-start.41 = (bf16[128,2048]{1,0:T(8,128)(2,1)S(1)}, bf16[128,2048]{1,0:T(8,128)(2,1)S(1)}, u32[]{:S(2)}, u32[]{:S(2)}) collective-permute-start(bf16[128,2048]{1,0:T(8,128)(2,1)S(1)} %copy-done.65), channel_id=1, source_target_pairs={{0,16},{8,24},{16,0},{24,8},{1,17},{9,25},{17,1},{25,9},{2,18},{10... | collective-permute-start | bytes 1572872 | tf_op jit(solution)/shard_map/ppermute | solution.py:955
  366.1 46.2 %collective-permute-start.42 = (bf16[128,2048]{1,0:T(8,128)(2,1)S(1)}, bf16[128,2048]{1,0:T(8,128)(2,1)S(1)}, u32[]{:S(2)}, u32[]{:S(2)}) collective-permute-start(bf16[128,2048]{1,0:T(8,128)(2,1)S(1)} %copy-done.64), channel_id=1, source_target_pairs={{0,8},{8,16},{16,24},{24,0},{1,9},{9,17},{17,25},{25,1},{2,10},{10... | collective-permute-start | bytes 1572872 | tf_op jit(solution)/shard_map/ppermute | solution.py:955
  370.4 41.8 %all-to-all-start.5 = ((f32[32,1,128]{2,1,0:T(1,128)}), f32[32,1,128]{2,1,0:T(1,128)S(1)}, u32[]{:S(2)}, u32[]{:S(2)}) async-start(f32[32,1,128]{2,1,0:T(1,128)} %bitcast.130), calls=%async_computation.6 | async-start | bytes 32768 | tf_op jit(solution)/shard_map/all_to_all | solution.py:929
  417.8 134.4 %reduce-scatter.9.cloned.1.call-start = ((), (), s32[]{:S(2)}) async-start(), calls=%async_computation.21 | async-start | bytes 5242880 | tf_op jit(solution)/shard_map/reduce_scatter | solution.py:1093
  455.0 38.0 %all-to-all-start.7 = ((bf16[8,128,512]{2,1,0:T(8,128)(2,1)}), bf16[8,128,512]{2,1,0:T(8,128)(2,1)S(1)}, u32[]{:S(2)}, u32[]{:S(2)}) async-start(bf16[8,128,512]{2,1,0:T(8,128)(2,1)} %bitcast.121), calls=%async_computation.9 | async-start | bytes 2097152 | tf_op jit(solution)/shard_map/all_to_all | solution.py:929
  494.0 58.2 %all-to-all-start.8 = ((bf16[32,64,512]{2,1,0:T(8,128)(2,1)}), bf16[32,64,512]{2,1,0:T(8,128)(2,1)S(1)}, u32[]{:S(2)}, u32[]{:S(2)}) async-start(bf16[32,64,512]{2,1,0:T(8,128)(2,1)} %bitcast.29), calls=%async_computation.10 | async-start | bytes 4194304 | tf_op jit(solution)/shard_map/all_to_all | solution.py:929
  499.1 101.6 %reduce-scatter.11.cloned.1.call-start = ((), (), s32[]{:S(2)}) async-start(), calls=%async_computation.22 | async-start | bytes 1310720 | tf_op jit(solution)/shard_map/reduce_scatter | solution.py:1138
  499.1 39.5 %collective-permute-start.54 = (bf16[128,2048]{1,0:T(8,128)(2,1)}, bf16[128,2048]{1,0:T(8,128)(2,1)S(1)}, u32[]{:S(2)}, u32[]{:S(2)}) collective-permute-start(bf16[128,2048]{1,0:T(8,128)(2,1)} %get-tuple-element.411), channel_id=1, source_target_pairs={{0,1},{1,0},{2,3},{3,2},{4,5},{5,4},{6,7},{7,6},{8,9},{9,8},{10,11... | collective-permute-start | bytes 1572872 | tf_op jit(solution)/shard_map/ppermute | solution.py:942
  501.0 40.4 %collective-permute-start.55 = (bf16[128,2048]{1,0:T(8,128)(2,1)}, bf16[128,2048]{1,0:T(8,128)(2,1)S(1)}, u32[]{:S(2)}, u32[]{:S(2)}) collective-permute-start(bf16[128,2048]{1,0:T(8,128)(2,1)} %get-tuple-element.412), channel_id=1, source_target_pairs={{0,4},{4,0},{1,5},{5,1},{2,6},{6,2},{3,7},{7,3},{8,12},{12,8},{9,1... | collective-permute-start | bytes 1572872 | tf_op jit(solution)/shard_map/ppermute | solution.py:942
  502.4 49.8 %collective-permute-start.56 = (bf16[128,2048]{1,0:T(8,128)(2,1)}, bf16[128,2048]{1,0:T(8,128)(2,1)}, u32[]{:S(2)}, u32[]{:S(2)}) collective-permute-start(bf16[128,2048]{1,0:T(8,128)(2,1)} %get-tuple-element.413), channel_id=1, source_target_pairs={{0,5},{1,4},{4,1},{5,0},{2,7},{3,6},{6,3},{7,2},{8,13},{9,12},{12,... | collective-permute-start | bytes 1572872 | tf_op jit(solution)/shard_map/ppermute | solution.py:942
  552.3 48.4 %all-to-all-start.9 = ((bf16[8,128,512]{2,1,0:T(8,128)(2,1)}), bf16[8,128,512]{2,1,0:T(8,128)(2,1)S(1)}, u32[]{:S(2)}, u32[]{:S(2)}) async-start(bf16[8,128,512]{2,1,0:T(8,128)(2,1)} %bitcast.123), calls=%async_computation.12 | async-start | bytes 2097152 | tf_op jit(solution)/shard_map/all_to_all | solution.py:929
  (120 other events, 1061.8 us)
Sparse Core Ops, SparseCore 0:
  32.3 41.3 all-gather.4
  76.2 65.1 all-gather.6
  155.7 73.6 all-gather.8
  231.1 52.6 all-gather.10
  319.6 52.6 reduce-scatter.4
  376.0 65.3 reduce-scatter.6
  455.1 71.7 reduce-scatter.8
  552.4 43.0 reduce-scatter.10

commit v5 on v4

--- a/solution.py
+++ b/solution.py
@@ -666,6 +666,32 @@
     out[...] = low(dot32(rows, columns[...], BY_ROWS))
 
 
+def term_halves_body(*refs):
+    pieces, columns, outs = refs[:-3], refs[-3], refs[-2:]
+    rows = jnp.concatenate([piece[...] for piece in pieces], axis=0)
+    term = low(dot32(rows, columns[...], BY_ROWS))
+    for number, out in enumerate(outs):
+
+        @pl.when(pl.program_id(1) == number)
+        def _(out=out):
+            out[...] = term
+
+
+def term_halves(pieces, columns):
+    tokens, width = pieces[0].shape
+    depth, chunk = width // 2, columns.shape[1] // 2
+    return pl.pallas_call(
+        term_halves_body,
+        grid=(2, 2),
+        out_shape=(low_shape(width, chunk),) * 2,
+        in_specs=[pl.BlockSpec((tokens, depth), lambda y, x: (0, y))] * len(pieces)
+        + [pl.BlockSpec((columns.shape[0], chunk), lambda y, x: (0, x))],
+        out_specs=(pl.BlockSpec((depth, chunk), lambda y, x: (y, 0)),) * 2,
+        name="term_halves",
+        **KERNEL,
+    )(*pieces, columns)
+
+
 def term_pass(pieces, columns, row_parts, col_parts):
     tokens, width = pieces[0].shape
     depth, chunk = width // row_parts, columns.shape[1] // col_parts
@@ -1122,44 +1148,48 @@
     gate_back = exchange(gate_t, GROUP_AXES)
     grad_qkv = attention_backward(grad_out_p, wo, query, key, value, *rows_info)
     gx_parts = core_back(by_cols_pass(grad_qkv, wq, 1, plane, "qkv_back_pass"))
-    qkv_term = term_pass(normed_p, grad_qkv, 2, 1)
-    gx_parts, qkv_term, gate_back, down_back, heads = together(
-        gx_parts, qkv_term, gate_back, down_back, heads
-    )
-
+    query_term, rest_term = term_halves(normed_p, grad_qkv)
+    gx_parts, query_term, rest_term, gate_back, down_back, heads = together(
+        gx_parts, query_term, rest_term, gate_back, down_back, heads
+    )
+
+    query_sum = exchange(query_term, ALL_AXES)
     out_term = term_pass(grad_out_p, heads, 2, 1)
-    qkv_sum = exchange(qkv_term, ALL_AXES)
-    gx_parts = plane_back(gx_parts)
     down_grad = side_by_side(down_back, hgroups)
-    gx_parts, qkv_sum, up_t, out_term, down_grad = together(
-        gx_parts, qkv_sum, up_t, out_term, down_grad
+    query_sum, up_t, out_term, down_grad, rest_term, gx_parts = together(
+        query_sum, up_t, out_term, down_grad, rest_term, gx_parts
     )
 
     out_term = lax.psum_scatter(out_term, "dp", scatter_dimension=0, tiled=True)
     up_back = exchange(up_t, GROUP_AXES)
+    gx_parts = plane_back(gx_parts)
+
+    def plane_sum(arrived):
+        parts = wide(arrived.reshape(nz, plane, d_rows, arrived.shape[1]))
+        return jnp.sum(parts, axis=0).transpose(1, 0, 2)
+
+    query_sum = plane_sum(query_sum).reshape(d_rows, -1)
+    up_back, gx_parts, rest_term, query_sum = together(up_back, gx_parts, rest_term, query_sum)
+
+    rest_sum = exchange(rest_term, ALL_AXES)
     input_grad = input_grad_pass(layer_input, grad_middle, gx_parts)
-
-    def plane_sum(arrived, cols):
-        return jnp.sum(wide(arrived.reshape(nz, plane, d_rows, cols)), axis=0).transpose(1, 0, 2)
-
-    qkv_sum = plane_sum(qkv_sum, own_cols)
+    gate_up_grad, gain_sum = unpack_pass(gain_m, gate_up_weight, gate_back, up_back, hgroups)
+    rest_sum, input_grad, gate_up_grad, gain_sum, out_term = together(
+        rest_sum, input_grad, gate_up_grad, gain_sum, out_term
+    )
+    out_sum = exchange(out_term, PLANE_AXES)
+
+    rest_sum = plane_sum(rest_sum)
     qkv_sum = jnp.concatenate(
         [
-            qkv_sum[:, :, :q_cols].reshape(d_rows, -1),
-            qkv_sum[:, :, q_cols : q_cols + kv_cols].reshape(d_rows, -1),
-            qkv_sum[:, :, q_cols + kv_cols :].reshape(d_rows, -1),
+            query_sum,
+            rest_sum[:, :, :kv_cols].reshape(d_rows, -1),
+            rest_sum[:, :, kv_cols:].reshape(d_rows, -1),
         ],
         axis=1,
     )
     qkv_grad = qkv_sum * gain_a
     attn_gain_grad = jnp.sum(qkv_sum * wide(qkv_weight), axis=1)
-    up_back, input_grad, out_term, qkv_grad, attn_gain_grad = together(
-        up_back, input_grad, out_term, qkv_grad, attn_gain_grad
-    )
-
-    out_sum = exchange(out_term, PLANE_AXES)
-    gate_up_grad, gain_sum = unpack_pass(gain_m, gate_up_weight, gate_back, up_back, hgroups)
-    out_sum, gate_up_grad, gain_sum = together(out_sum, gate_up_grad, gain_sum)
     gain_halves = gain_sum.reshape(2, -1)
     gain_keep = jnp.where(x_at == 0, gain_halves[0], gain_halves[1])
     gain_send = jnp.where(x_at == 0, gain_halves[1], gain_halves[0])

time: 636 us -> 634 us (level)
  starting transfers between devices: 96.5 us -> 108 us
    ppermute x46, waiting for transfers between devices: 116 us -> 101 us  [swap(): return lax.ppermute(values, axes if len(axes) > 1 else axes[0], pairs)]
    all_to_all x11 -> x12, starting transfers between devices: 49.7 us -> 60.8 us  [exchange(): return lax.all_to_all(values, axes, split_axis=0, concat_axis=0, tiled=True)]
    all_to_all x11 -> x12, waiting for transfers between devices: 118 us -> 127 us  [exchange(): return lax.all_to_all(values, axes, split_axis=0, concat_axis=0, tiled=True)]
    pallas_call x0 -> x1, Pallas kernels: none -> 7.4 us  [term_halves(): pl.pallas_call(term_halves_body, grid=(2, 2), out_shape=(low_shape(width,...]
    pallas_call x5 -> x4, Pallas kernels: 37.4 us -> 31.7 us  [term_pass(): pl.pallas_call(term_body, grid=(row_parts, col_parts), out_shape=low_shap...]
    unnamed x138 -> x139, local copies, waits for them, and re-layouts: 13.9 us -> 11.9 us
  transfers between devices with their start and end apart: 77 -> 78, of which waited for: 32 -> 33; matrix products, arithmetic and copies ran while one was open for 2% -> 2% of each run, Pallas kernels for 30% -> 30%
where the time goes in v5:
time: 634 us; the launch traced here: 628 us
  waiting for transfers between devices  294 us (46%)
  Pallas kernels  186 us (29%)
  starting transfers between devices  108 us (17%)
  local copies, waits for them, and re-layouts  15.5 us (2%)
  between operations  15.2 us (2%)
  other arithmetic  8.84 us (1%)
    all_to_all x12, waiting for transfers between devices, exchange(): return lax.all_to_all(values, axes, split_axis=0, concat_axis=0, tiled=True)  127 us
    ppermute x46, waiting for transfers between devices, swap(): return lax.ppermute(values, axes if len(axes) > 1 else axes[0], pairs)  101 us
    ppermute x12, waiting for transfers between devices, shift(): lax.ppermute(values, 'dp', [(i, (i + by) % count) for i in range(count)])  61.9 us
    all_to_all x12, starting transfers between devices, exchange(): return lax.all_to_all(values, axes, split_axis=0, concat_axis=0, tiled=True)  60.8 us
    pallas_call x4, Pallas kernels, term_pass(): pl.pallas_call(term_body, grid=(row_parts, col_parts), out_shape=low_shap...  31.7 us
    ppermute x46, starting transfers between devices, swap(): return lax.ppermute(values, axes if len(axes) > 1 else axes[0], pairs)  27.3 us
    pallas_call x3, Pallas kernels, by_cols_pass(): pl.pallas_call(functools.partial(by_cols_body, parts), grid=(width // ROW...  24.1 us
    pallas_call x1, Pallas kernels, grad_hidden_pass(): pl.pallas_call(grad_hidden_body, grid=(4 + width // ROWS,), out_shape=(lo...  22.4 us
  transfers between devices with their start and end apart: 78, of which 33 were waited for; matrix products, arithmetic and copies ran while one was open for 2% of the time, Pallas kernels for 30%

profile of v5, /device:TPU:0, one launch (start us, length us, event | category | flops | bytes accessed | tf_op | source)
XLA Modules:
  0.0 627.6 jit_solution(18086519831164761579)
XLA Ops:
  46.5 10.9 %collective-permute-done.2.refs_2_ = bf16[128,2048]{1,0:T(8,128)(2,1)S(1)} collective-permute-done((bf16[128,2048]{1,0:T(8,128)(2,1)S(1)}, bf16[128,2048]{1,0:T(8,128)(2,1)S(1)}, u32[]{:S(2)}, u32[]{:S(2)}) %collective-permute-start.2) | collective-permute-done | bytes 524320 | tf_op jit(solution)/shard_map/ppermute | solution.py:968
  57.7 12.4 %all-to-all-done.1 = bf16[8,128,512]{2,1,0:T(8,128)(2,1)S(1)} async-done(((bf16[8,128,512]{2,1,0:T(8,128)(2,1)}), bf16[8,128,512]{2,1,0:T(8,128)(2,1)S(1)}, u32[]{:S(2)}, u32[]{:S(2)}) %all-to-all-start.1) | async-done | bytes 1048608 | tf_op jit(solution)/shard_map/all_to_all | solution.py:955
  82.0 41.6 %all-to-all-done.2 = bf16[32,64,512]{2,1,0:T(8,128)(2,1)S(1)} async-done(((bf16[32,64,512]{2,1,0:T(8,128)(2,1)}), bf16[32,64,512]{2,1,0:T(8,128)(2,1)S(1)}, u32[]{:S(2)}, u32[]{:S(2)}) %all-to-all-start.2) | async-done | bytes 2097184 | tf_op jit(solution)/shard_map/all_to_all | solution.py:955
  127.2 11.7 %attention_forward.1 = (bf16[1024,256]{1,0:T(8,128)(2,1)}, bf16[1024,128]{1,0:T(8,128)(2,1)}, bf16[1024,128]{1,0:T(8,128)(2,1)}, bf16[1024,256]{1,0:T(8,128)(2,1)}) custom-call(s32[16]{0:T(128)} %pad_add_fusion.place, bf16[2048,512]{1,0:T(8,128)(2,1)} %bitcast.108, f32[1024,128]{1,0:T(8,128)} %get-tuple-element.251.cosine, ...), custom_call_target="tpu_custom_call" | custom-call | flops 1000 | bytes 1000 | tf_op jit(solution)/shard_map/attention_forward/pallas_call | solution.py:460
  167.9 15.8 %collective-permute-done.12.refs_1_ = bf16[128,2048]{1,0:T(8,128)(2,1)S(1)} collective-permute-done((bf16[128,2048]{1,0:T(8,128)(2,1)}, bf16[128,2048]{1,0:T(8,128)(2,1)S(1)}, u32[]{:S(2)}, u32[]{:S(2)}) %collective-permute-start.12) | collective-permute-done | bytes 524320 | tf_op jit(solution)/shard_map/ppermute | solution.py:968
  188.7 9.8 %collective-permute-done.14.refs_3_ = bf16[128,2048]{1,0:T(8,128)(2,1)S(1)} collective-permute-done((bf16[128,2048]{1,0:T(8,128)(2,1)}, bf16[128,2048]{1,0:T(8,128)(2,1)S(1)}, u32[]{:S(2)}, u32[]{:S(2)}) %collective-permute-start.14) | collective-permute-done | bytes 524320 | tf_op jit(solution)/shard_map/ppermute | solution.py:968
  207.6 11.4 %collective-permute-done.18.refs_3_ = bf16[128,2048]{1,0:T(8,128)(2,1)S(1)} collective-permute-done((bf16[128,2048]{1,0:T(8,128)(2,1)}, bf16[128,2048]{1,0:T(8,128)(2,1)S(1)}, u32[]{:S(2)}, u32[]{:S(2)}) %collective-permute-start.18) | collective-permute-done | bytes 524320 | tf_op jit(solution)/shard_map/ppermute | solution.py:981
  219.0 31.9 %collective-permute-done.17.refs_2_ = bf16[128,2048]{1,0:T(8,128)(2,1)S(1)} collective-permute-done((bf16[128,2048]{1,0:T(8,128)(2,1)}, bf16[128,2048]{1,0:T(8,128)(2,1)S(1)}, u32[]{:S(2)}, u32[]{:S(2)}) %collective-permute-start.17) | collective-permute-done | bytes 524320 | tf_op jit(solution)/shard_map/ppermute | solution.py:981
  255.6 14.4 %hidden_pass.1 = (bf16[1024,1024]{1,0:T(8,128)(2,1)}, bf16[1024,1024]{1,0:T(8,128)(2,1)}, bf16[1024,1024]{1,0:T(8,128)(2,1)}) custom-call(bf16[2,2,1024,512]{3,2,1,0:T(8,128)(2,1)} %bitcast.105, bf16[2,2,1024,512]{3,2,1,0:T(8,128)(2,1)} %bitcast.106, bf16[128,2048]{1,0:T(8,128)(2,1)} %get-tuple-element.297.refs_0_, bf16[128,2048]{1,0:T(8,128)(2,1)} %copy-done.4, ...), custom_call_target="tpu_custom_call" | custom-call | flops 1000 | bytes 1000 | tf_op jit(solution)/shard_map/hidden_pass/pallas_call | solution.py:600
  270.0 9.6 %collective-permute-done.23.refs_6_.refs_2_ = bf16[128,2048]{1,0:T(8,128)(2,1)} collective-permute-done((bf16[128,2048]{1,0:T(8,128)(2,1)}, bf16[128,2048]{1,0:T(8,128)(2,1)}, u32[]{:S(2)}, u32[]{:S(2)}) %collective-permute-start.23) | collective-permute-done | bytes 524320 | tf_op jit(solution)/shard_map/ppermute | solution.py:981
  285.3 9.6 %down_pass.1 = (bf16[128,2048]{1,0:T(8,128)(2,1)}, bf16[128,2048]{1,0:T(8,128)(2,1)}, bf16[128,2048]{1,0:T(8,128)(2,1)}, bf16[128,2048]{1,0:T(8,128)(2,1)}, bf16...) custom-call(bf16[1024,1024]{1,0:T(8,128)(2,1)} %get-tuple-element.315., ...), custom_call_target="tpu_custom_call" | custom-call | flops 1000 | bytes 1000 | tf_op jit(solution)/shard_map/down_pass/pallas_call | solution.py:555
  321.3 22.4 %grad_hidden_pass.1 = (bf16[1024,1024]{1,0:T(8,128)(2,1)}, bf16[1024,1024]{1,0:T(8,128)(2,1)}, bf16[128,2048]{1,0:T(8,128)(2,1)}, bf16[128,2048]{1,0:T(8,128)(2,...) custom-call(bf16[2,2,1024,512]{3,2,1,0:T(8,128)(2,1)} %bitcast.107, ...), custom_call_target="tpu_custom_call" | custom-call | flops 1000 | bytes 1000 | tf_op jit(solution)/shard_map/grad_hidden_pass/pallas_call | solution.py:646
  347.7 9.2 %term_pass.5 = bf16[4096,512]{1,0:T(8,128)(2,1)} custom-call(bf16[128,2048]{1,0:T(8,128)(2,1)} %get-tuple-element.297.refs_0_, bf16[128,2048]{1,0:T(8,128)(2,1)} %copy-done.4, bf16[128,2048]{1,0:T(8,128)(2,1)} %copy-done.3, bf16[128,2048]{1,0:T(8,128)(2,1)} %copy-done.2, bf16[128,2048]{1,0:T(8,128)(2,1)} %copy-done.5, ...), custom_call_target="tpu_custom_call" | custom-call | flops 1000 | bytes 1000 | tf_op jit(solution)/shard_map/term_pass/pallas_call | solution.py:698
  375.0 9.0 %term_pass.6 = bf16[4096,512]{1,0:T(8,128)(2,1)} custom-call(bf16[128,2048]{1,0:T(8,128)(2,1)} %get-tuple-element.297.refs_0_, bf16[128,2048]{1,0:T(8,128)(2,1)} %copy-done.4, bf16[128,2048]{1,0:T(8,128)(2,1)} %copy-done.3, bf16[128,2048]{1,0:T(8,128)(2,1)} %copy-done.2, bf16[128,2048]{1,0:T(8,128)(2,1)} %copy-done.5, ...), custom_call_target="tpu_custom_call" | custom-call | flops 1000 | bytes 1000 | tf_op jit(solution)/shard_map/term_pass/pallas_call | solution.py:698
  384.0 28.2 %all-to-all-done.5 = f32[32,1,128]{2,1,0:T(1,128)S(1)} async-done(((f32[32,1,128]{2,1,0:T(1,128)}), f32[32,1,128]{2,1,0:T(1,128)S(1)}, u32[]{:S(2)}, u32[]{:S(2)}) %all-to-all-start.5) | async-done | bytes 16416 | tf_op jit(solution)/shard_map/all_to_all | solution.py:955
  425.3 14.3 %collective-permute-done.45.refs_3_ = bf16[128,2048]{1,0:T(8,128)(2,1)S(1)} collective-permute-done((bf16[128,2048]{1,0:T(8,128)(2,1)}, bf16[128,2048]{1,0:T(8,128)(2,1)S(1)}, u32[]{:S(2)}, u32[]{:S(2)}) %collective-permute-start.45) | collective-permute-done | bytes 524320 | tf_op jit(solution)/shard_map/ppermute | solution.py:968
  439.6 10.2 %collective-permute-done.44.refs_2_ = bf16[128,2048]{1,0:T(8,128)(2,1)S(1)} collective-permute-done((bf16[128,2048]{1,0:T(8,128)(2,1)}, bf16[128,2048]{1,0:T(8,128)(2,1)S(1)}, u32[]{:S(2)}, u32[]{:S(2)}) %collective-permute-start.44) | collective-permute-done | bytes 524320 | tf_op jit(solution)/shard_map/ppermute | solution.py:968
  454.9 13.1 %all-to-all-start.7 = ((bf16[8,128,512]{2,1,0:T(8,128)(2,1)}), bf16[8,128,512]{2,1,0:T(8,128)(2,1)S(1)}, u32[]{:S(2)}, u32[]{:S(2)}) async-start(bf16[8,128,512]{2,1,0:T(8,128)(2,1)} %bitcast.123), calls=%async_computation.9 | async-start | bytes 2097152 | tf_op jit(solution)/shard_map/all_to_all | solution.py:955
  468.1 13.2 %attention_backward.1.rows.refs_8_ = bf16[1024,512]{1,0:T(8,128)(2,1)} custom-call(s32[16]{0:T(128)} %pad_add_fusion.place, bf16[2048,256]{1,0:T(8,128)(2,1)} %all-gather.5.cloned.1.call-done.refs_0_.weight, bf16[1024,256]{1,0:T(8,128)(2,1)} %get-tuple-element.372.query, bf16[1024,128]{1,0:T(8,128)(2,1)} %get-tuple-element.373.key, ...), custom_call_target="tpu_custom_call" | custom-call | flops 1000 | bytes 1000 | tf_op jit(solution)/shard_map/attention_backward/pallas_call | solution.py:513
  517.7 16.4 %all-to-all-done.8 = bf16[32,64,256]{2,1,0:T(8,128)(2,1)S(1)} async-done(((bf16[32,64,256]{2,1,0:T(8,128)(2,1)}), bf16[32,64,256]{2,1,0:T(8,128)(2,1)S(1)}, u32[]{:S(2)}, u32[]{:S(2)}) %all-to-all-start.8) | async-done | bytes 1048608 | tf_op jit(solution)/shard_map/all_to_all | solution.py:955
  541.6 11.2 %collective-permute-done.54.refs_1_ = bf16[128,2048]{1,0:T(8,128)(2,1)S(1)} collective-permute-done((bf16[128,2048]{1,0:T(8,128)(2,1)}, bf16[128,2048]{1,0:T(8,128)(2,1)S(1)}, u32[]{:S(2)}, u32[]{:S(2)}) %collective-permute-start.54) | collective-permute-done | bytes 524320 | tf_op jit(solution)/shard_map/ppermute | solution.py:968
  552.8 11.8 %collective-permute-done.55.refs_2_ = bf16[128,2048]{1,0:T(8,128)(2,1)S(1)} collective-permute-done((bf16[128,2048]{1,0:T(8,128)(2,1)}, bf16[128,2048]{1,0:T(8,128)(2,1)S(1)}, u32[]{:S(2)}, u32[]{:S(2)}) %collective-permute-start.55) | collective-permute-done | bytes 524320 | tf_op jit(solution)/shard_map/ppermute | solution.py:968
  564.6 13.9 %all-to-all-done.9 = bf16[8,128,512]{2,1,0:T(8,128)(2,1)S(1)} async-done(((bf16[8,128,512]{2,1,0:T(8,128)(2,1)}), bf16[8,128,512]{2,1,0:T(8,128)(2,1)S(1)}, u32[]{:S(2)}, u32[]{:S(2)}) %all-to-all-start.9) | async-done | bytes 1048608 | tf_op jit(solution)/shard_map/all_to_all | solution.py:955
  594.9 14.2 %all-to-all-done.10 = bf16[32,64,256]{2,1,0:T(8,128)(2,1)S(1)} async-done(((bf16[32,64,256]{2,1,0:T(8,128)(2,1)}), bf16[32,64,256]{2,1,0:T(8,128)(2,1)S(1)}, u32[]{:S(2)}, u32[]{:S(2)}) %all-to-all-start.10) | async-done | bytes 1048608 | tf_op jit(solution)/shard_map/all_to_all | solution.py:955
  (336 shorter events, 246.2 us)
Async XLA Ops:
  25.0 45.1 %all-to-all-start.1 = ((bf16[8,128,512]{2,1,0:T(8,128)(2,1)}), bf16[8,128,512]{2,1,0:T(8,128)(2,1)S(1)}, u32[]{:S(2)}, u32[]{:S(2)}) async-start(bf16[8,128,512]{2,1,0:T(8,128)(2,1)} %bitcast.112), calls=%async_computation.1 | async-start | bytes 2097152 | tf_op jit(solution)/shard_map/all_to_all | solution.py:955
  29.9 109.0 %all-gather.5.cloned.1.call-start = ((), (), s32[]{:S(2)}) async-start(), calls=%async_computation.16 | async-start | bytes 1310720 | tf_op jit(solution)/shard_map/all_gather | solution.py:1057
  30.6 220.7 %all-gather.7.cloned.1.call-start = ((), (), s32[]{:S(2)}) async-start(), calls=%async_computation.17 | async-start | bytes 5242880 | tf_op jit(solution)/shard_map/all_gather | solution.py:1055
  71.1 52.4 %all-to-all-start.2 = ((bf16[32,64,512]{2,1,0:T(8,128)(2,1)}), bf16[32,64,512]{2,1,0:T(8,128)(2,1)S(1)}, u32[]{:S(2)}, u32[]{:S(2)}) async-start(bf16[32,64,512]{2,1,0:T(8,128)(2,1)} %bitcast.110), calls=%async_computation.2 | async-start | bytes 4194304 | tf_op jit(solution)/shard_map/all_to_all | solution.py:955
  127.1 126.5 %all-gather.9.cloned.1.call-start = ((), (), s32[]{:S(2)}) async-start(), calls=%async_computation.18 | async-start | bytes 5242880 | tf_op jit(solution)/shard_map/all_gather | solution.py:1055
  155.6 43.0 %all-to-all-start.4 = ((bf16[8,128,512]{2,1,0:T(8,128)(2,1)}), bf16[8,128,512]{2,1,0:T(8,128)(2,1)S(1)}, u32[]{:S(2)}, u32[]{:S(2)}) async-start(bf16[8,128,512]{2,1,0:T(8,128)(2,1)} %bitcast.17), calls=%async_computation.4 | async-start | bytes 2097152 | tf_op jit(solution)/shard_map/all_to_all | solution.py:955
  160.6 123.2 %all-gather.11.cloned.1.call-start = ((), (), s32[]{:S(2)}) async-start(), calls=%async_computation.19 | async-start | bytes 5242880 | tf_op jit(solution)/shard_map/all_gather | solution.py:1055
  163.6 34.9 %collective-permute-start.14 = (bf16[128,2048]{1,0:T(8,128)(2,1)}, bf16[128,2048]{1,0:T(8,128)(2,1)S(1)}, u32[]{:S(2)}, u32[]{:S(2)}) collective-permute-start(bf16[128,2048]{1,0:T(8,128)(2,1)} %get-tuple-element.280), channel_id=1, source_target_pairs={{0,5},{1,4},{4,1},{5,0},{2,7},{3,6},{6,3},{7,2},{8,13},{9,12},{12,... | collective-permute-start | bytes 1572872 | tf_op jit(solution)/shard_map/ppermute | solution.py:968
  164.2 34.3 %collective-permute-start.15 = (bf16[128,2048]{1,0:T(8,128)(2,1)S(1)}, bf16[128,2048]{1,0:T(8,128)(2,1)}, u32[]{:S(2)}, u32[]{:S(2)}) collective-permute-start(bf16[128,2048]{1,0:T(8,128)(2,1)S(1)} %copy-done.14), channel_id=1, source_target_pairs={{0,24},{8,0},{16,8},{24,16},{1,25},{9,1},{17,9},{25,17},{2,26},{10... | collective-permute-start | bytes 1572872 | tf_op jit(solution)/shard_map/ppermute | solution.py:981
  202.7 209.6 %reduce-scatter.5.cloned.1.call-start = ((), (), s32[]{:S(2)}) async-start(), calls=%async_computation.20 | async-start | bytes 5242880 | tf_op jit(solution)/shard_map/reduce_scatter | solution.py:1119
  206.2 44.6 %collective-permute-start.17 = (bf16[128,2048]{1,0:T(8,128)(2,1)}, bf16[128,2048]{1,0:T(8,128)(2,1)S(1)}, u32[]{:S(2)}, u32[]{:S(2)}) collective-permute-start(bf16[128,2048]{1,0:T(8,128)(2,1)} %get-tuple-element.297.refs_0_), channel_id=1, source_target_pairs={{0,16},{8,24},{16,0},{24,8},{1,17},{9,25},{17,1},{25,9},{2,18},{10... | collective-permute-start | bytes 1572872 | tf_op jit(solution)/shard_map/ppermute | solution.py:981
  206.2 44.6 %collective-permute-start.16 = (bf16[128,2048]{1,0:T(8,128)(2,1)}, bf16[128,2048]{1,0:T(8,128)(2,1)S(1)}, u32[]{:S(2)}, u32[]{:S(2)}) collective-permute-start(bf16[128,2048]{1,0:T(8,128)(2,1)} %get-tuple-element.297.refs_0_), channel_id=1, source_target_pairs={{0,8},{8,16},{16,24},{24,0},{1,9},{9,17},{17,25},{25,1},{2,10},{10... | collective-permute-start | bytes 1572872 | tf_op jit(solution)/shard_map/ppermute | solution.py:981
  207.6 43.8 %collective-permute-start.19 = (bf16[128,2048]{1,0:T(8,128)(2,1)}, bf16[128,2048]{1,0:T(8,128)(2,1)S(1)}, u32[]{:S(2)}, u32[]{:S(2)}) collective-permute-start(bf16[128,2048]{1,0:T(8,128)(2,1)} %get-tuple-element.297.refs_0_), channel_id=1, source_target_pairs={{0,2},{2,0},{1,3},{3,1},{4,6},{6,4},{5,7},{7,5},{8,10},{10,8},{9,1... | collective-permute-start | bytes 1572872 | tf_op jit(solution)/shard_map/ppermute | solution.py:968
  219.0 32.4 %collective-permute-start.22 = (bf16[128,2048]{1,0:T(8,128)(2,1)S(1)}, bf16[128,2048]{1,0:T(8,128)(2,1)S(1)}, u32[]{:S(2)}, u32[]{:S(2)}) collective-permute-start(bf16[128,2048]{1,0:T(8,128)(2,1)S(1)} %collective-permute-done.18.refs_3_), channel_id=1, source_target_pairs={{0,2},{2,0},{1,3},{3,1},{4,6},{6,4},{5,7},{7,5},{8,10},{10,8},{9,1... | collective-permute-start | bytes 1572872 | tf_op jit(solution)/shard_map/ppermute | solution.py:968
  320.2 129.5 %reduce-scatter.7.cloned.1.call-start = ((), (), s32[]{:S(2)}) async-start(), calls=%async_computation.21 | async-start | bytes 5242880 | tf_op jit(solution)/shard_map/reduce_scatter | solution.py:1119
  363.3 48.9 %collective-permute-start.40 = (bf16[128,2048]{1,0:T(8,128)(2,1)}, bf16[128,2048]{1,0:T(8,128)(2,1)S(1)}, u32[]{:S(2)}, u32[]{:S(2)}) collective-permute-start(bf16[128,2048]{1,0:T(8,128)(2,1)} %get-tuple-element.376), channel_id=1, source_target_pairs={{0,24},{8,0},{16,8},{24,16},{1,25},{9,1},{17,9},{25,17},{2,26},{10... | collective-permute-start | bytes 1572872 | tf_op jit(solution)/shard_map/ppermute | solution.py:981
  366.0 46.2 %collective-permute-start.41 = (bf16[128,2048]{1,0:T(8,128)(2,1)S(1)}, bf16[128,2048]{1,0:T(8,128)(2,1)S(1)}, u32[]{:S(2)}, u32[]{:S(2)}) collective-permute-start(bf16[128,2048]{1,0:T(8,128)(2,1)S(1)} %copy-done.66), channel_id=1, source_target_pairs={{0,16},{8,24},{16,0},{24,8},{1,17},{9,25},{17,1},{25,9},{2,18},{10... | collective-permute-start | bytes 1572872 | tf_op jit(solution)/shard_map/ppermute | solution.py:981
  366.0 46.2 %collective-permute-start.42 = (bf16[128,2048]{1,0:T(8,128)(2,1)S(1)}, bf16[128,2048]{1,0:T(8,128)(2,1)S(1)}, u32[]{:S(2)}, u32[]{:S(2)}) collective-permute-start(bf16[128,2048]{1,0:T(8,128)(2,1)S(1)} %copy-done.65), channel_id=1, source_target_pairs={{0,8},{8,16},{16,24},{24,0},{1,9},{9,17},{17,25},{25,1},{2,10},{10... | collective-permute-start | bytes 1572872 | tf_op jit(solution)/shard_map/ppermute | solution.py:981
  370.3 41.9 %all-to-all-start.5 = ((f32[32,1,128]{2,1,0:T(1,128)}), f32[32,1,128]{2,1,0:T(1,128)S(1)}, u32[]{:S(2)}, u32[]{:S(2)}) async-start(f32[32,1,128]{2,1,0:T(1,128)} %bitcast.132), calls=%async_computation.6 | async-start | bytes 32768 | tf_op jit(solution)/shard_map/all_to_all | solution.py:955
  412.3 37.5 %all-to-all-start.6 = ((bf16[8,128,512]{2,1,0:T(8,128)(2,1)}), bf16[8,128,512]{2,1,0:T(8,128)(2,1)S(1)}, u32[]{:S(2)}, u32[]{:S(2)}) async-start(bf16[8,128,512]{2,1,0:T(8,128)(2,1)} %bitcast.124), calls=%async_computation.8 | async-start | bytes 2097152 | tf_op jit(solution)/shard_map/all_to_all | solution.py:955
  417.8 116.4 %reduce-scatter.9.cloned.1.call-start = ((), (), s32[]{:S(2)}) async-start(), calls=%async_computation.22 | async-start | bytes 5242880 | tf_op jit(solution)/shard_map/reduce_scatter | solution.py:1119
  454.9 47.6 %all-to-all-start.7 = ((bf16[8,128,512]{2,1,0:T(8,128)(2,1)}), bf16[8,128,512]{2,1,0:T(8,128)(2,1)S(1)}, u32[]{:S(2)}, u32[]{:S(2)}) async-start(bf16[8,128,512]{2,1,0:T(8,128)(2,1)} %bitcast.123), calls=%async_computation.9 | async-start | bytes 2097152 | tf_op jit(solution)/shard_map/all_to_all | solution.py:955
  534.2 44.4 %all-to-all-start.9 = ((bf16[8,128,512]{2,1,0:T(8,128)(2,1)}), bf16[8,128,512]{2,1,0:T(8,128)(2,1)S(1)}, u32[]{:S(2)}, u32[]{:S(2)}) async-start(bf16[8,128,512]{2,1,0:T(8,128)(2,1)} %bitcast.126), calls=%async_computation.12 | async-start | bytes 2097152 | tf_op jit(solution)/shard_map/all_to_all | solution.py:955
  537.8 57.2 %reduce-scatter.11.cloned.1.call-start = ((), (), s32[]{:S(2)}) async-start(), calls=%async_computation.23 | async-start | bytes 1310720 | tf_op jit(solution)/shard_map/reduce_scatter | solution.py:1163
  (122 other events, 1113.8 us)
Sparse Core Ops, SparseCore 0:
  32.3 41.3 all-gather.4
  76.2 65.1 all-gather.6
  155.7 73.6 all-gather.8
  231.1 52.6 all-gather.10
  319.6 52.6 reduce-scatter.4
  376.0 65.4 reduce-scatter.6
  455.0 52.6 reduce-scatter.8
  541.6 40.1 reduce-scatter.10

commit v6 on v5

--- a/solution.py
+++ b/solution.py
@@ -362,6 +362,7 @@
     cost_estimate=pl.CostEstimate(flops=1000, bytes_accessed=1000, transcendentals=0),
 )
 ROWS = 256
+STRIPE = 1024
 BY_ROWS = (((0,), (0,)), ((), ()))
 BY_COLS = (((1,), (1,)), ((), ()))
 PLAIN = (((1,), (0,)), ((), ()))
@@ -523,13 +524,13 @@
 
 
 def stripes(weight, parts, number):
-    depth = weight.shape[0] // parts**2 // ROWS
+    depth = weight.shape[0] // parts**2 // STRIPE
 
     def place(x, step):
         at = jnp.clip(step - number, 0, parts * depth - 1)
         return ((at // depth * parts + x) * depth + at % depth, 0)
 
-    shape = (ROWS, weight.shape[1])
+    shape = (STRIPE, weight.shape[1])
     return [pl.BlockSpec(shape, functools.partial(place, x)) for x in range(parts)]
 
 
@@ -554,10 +555,10 @@
     block = rows.shape[0] // blocks
     return pl.pallas_call(
         functools.partial(by_cols_body, parts),
-        grid=(width // ROWS,),
+        grid=(width // STRIPE,),
         out_shape=(low_shape(block, width),) * blocks,
         in_specs=[once(rows.shape), *stripes(weight, parts, 0)],
-        out_specs=(pl.BlockSpec((block, ROWS), lambda step: (0, step)),) * blocks,
+        out_specs=(pl.BlockSpec((block, STRIPE), lambda step: (0, step)),) * blocks,
         name=name,
         **KERNEL,
     )(rows, *[weight] * parts)
@@ -642,10 +643,10 @@
     rows, width = len(cot_p) * cot_p[0].shape[0], cot_p[0].shape[1]
     units = 2 * gate_w.shape[1]
     quarter = pl.BlockSpec((rows, units // 4), lambda step: (0, jnp.minimum(step, 3)))
-    stripe = pl.BlockSpec((cot_p[0].shape[0], ROWS), lambda step: (0, jnp.maximum(step - 4, 0)))
+    stripe = pl.BlockSpec((cot_p[0].shape[0], STRIPE), lambda step: (0, jnp.maximum(step - 4, 0)))
     return pl.pallas_call(
         grad_hidden_body,
-        grid=(4 + width // ROWS,),
+        grid=(4 + width // STRIPE,),
         out_shape=(low_shape(rows, units),) * 2 + tuple(low_shape(*v.shape) for v in cot_p),
         in_specs=[columns_of(down_w)]
         + [quarter] * 2
@@ -844,27 +845,35 @@
     )(stream_in, grad_middle, *parts)
 
 
+def stack_groups(out, values):
+    rows, chunk = values.shape[0], out.shape[1]
+    for number in range(out.shape[0] // rows):
+        out[number * rows : (number + 1) * rows, :] = values[:, number * chunk : (number + 1) * chunk]
+
+
 def pack_body(gain, gate_up, out):
-    out[...] = low(wide(gate_up[:, 0, :]) * gain[...])
+    stack_groups(out, low(wide(gate_up[:, 0, :]) * gain[...]))
 
 
 def pack_more_body(gain, gate_up, down, up_out, down_out):
-    up_out[...] = low(wide(gate_up[:, 1, :]) * gain[...])
-    down_out[...] = down[...]
+    stack_groups(up_out, low(wide(gate_up[:, 1, :]) * gain[...]))
+    stack_groups(down_out, down[...])
 
 
 def pack_pass(body, outs, groups, gain, gate_up, *down):
     rows, chunk = gate_up.shape[0], gate_up.shape[2] // groups
+    steps = 2
+    per_step = groups // steps
     return pl.pallas_call(
         body,
-        grid=(groups,),
+        grid=(steps,),
         out_shape=(low_shape(groups * rows, chunk),) * outs,
         in_specs=[
             pl.BlockSpec((rows, 1), lambda g: (0, 0)),
-            pl.BlockSpec((rows, 2, chunk), lambda g: (0, 0, g)),
+            pl.BlockSpec((rows, 2, per_step * chunk), lambda g: (0, 0, g)),
         ]
-        + [pl.BlockSpec((rows, chunk), lambda g: (0, g))] * len(down),
-        out_specs=(pl.BlockSpec((rows, chunk), lambda g: (g, 0)),) * outs,
+        + [pl.BlockSpec((rows, per_step * chunk), lambda g: (0, g))] * len(down),
+        out_specs=(pl.BlockSpec((per_step * rows, chunk), lambda g: (g, 0)),) * outs,
         name="pack_pass",
         **KERNEL,
     )(gain, gate_up, *down)

time: 634 us -> 623 us (0.983)
  Pallas kernels: 186 us -> 173 us
  starting transfers between devices: 108 us -> 97.3 us
  waiting for transfers between devices: 294 us -> 302 us
    pallas_call x6, Pallas kernels: 58.3 us -> 45.4 us  [the longest x1 21.3 us: grad_hidden_pass(): pl.pallas_call(grad_hidden_body, grid=(4 + width // STRIPE,), out_shape=(...]
    all_to_all x12, starting transfers between devices: 60.8 us -> 50.8 us  [exchange(): return lax.all_to_all(values, axes, split_axis=0, concat_axis=0, tiled=True)]
  transfers between devices with their start and end apart: 78 -> 78, of which waited for: 33 -> 35; matrix products, arithmetic and copies ran while one was open for 2% -> 2% of each run, Pallas kernels for 30% -> 28%
where the time goes in v6:
time: 623 us; the launch traced here: 612 us
  waiting for transfers between devices  302 us (48%)
  Pallas kernels  173 us (28%)
  starting transfers between devices  97.3 us (16%)
  local copies, waits for them, and re-layouts  15.6 us (3%)
  between operations  15.2 us (2%)
  other arithmetic  8.84 us (1%)
    all_to_all x12, waiting for transfers between devices, exchange(): return lax.all_to_all(values, axes, split_axis=0, concat_axis=0, tiled=True)  129 us
    ppermute x46, waiting for transfers between devices, swap(): return lax.ppermute(values, axes if len(axes) > 1 else axes[0], pairs)  103 us
    ppermute x12, waiting for transfers between devices, shift(): lax.ppermute(values, 'dp', [(i, (i + by) % count) for i in range(count)])  65.4 us
    all_to_all x12, starting transfers between devices, exchange(): return lax.all_to_all(values, axes, split_axis=0, concat_axis=0, tiled=True)  50.8 us
    pallas_call x4, Pallas kernels, term_pass(): pl.pallas_call(term_body, grid=(row_parts, col_parts), out_shape=low_shap...  31.7 us
    ppermute x46, starting transfers between devices, swap(): return lax.ppermute(values, axes if len(axes) > 1 else axes[0], pairs)  27.1 us
    pallas_call x1, Pallas kernels, grad_hidden_pass(): pl.pallas_call(grad_hidden_body, grid=(4 + width // STRIPE,), out_shape=(...  21.3 us
    ppermute x12, starting transfers between devices, shift(): lax.ppermute(values, 'dp', [(i, (i + by) % count) for i in range(count)])  18.6 us
  transfers between devices with their start and end apart: 78, of which 35 were waited for; matrix products, arithmetic and copies ran while one was open for 2% of the time, Pallas kernels for 28%

profile of v6, /device:TPU:0, one launch (start us, length us, event | category | flops | bytes accessed | tf_op | source)
XLA Modules:
  0.0 612.2 jit_solution(6911956692252173065)
XLA Ops:
  43.9 10.9 %collective-permute-done.2.refs_2_ = bf16[128,2048]{1,0:T(8,128)(2,1)S(1)} collective-permute-done((bf16[128,2048]{1,0:T(8,128)(2,1)S(1)}, bf16[128,2048]{1,0:T(8,128)(2,1)S(1)}, u32[]{:S(2)}, u32[]{:S(2)}) %collective-permute-start.2) | collective-permute-done | bytes 524320 | tf_op jit(solution)/shard_map/ppermute | solution.py:977
  55.1 12.4 %all-to-all-done.1 = bf16[8,128,512]{2,1,0:T(8,128)(2,1)S(1)} async-done(((bf16[8,128,512]{2,1,0:T(8,128)(2,1)}), bf16[8,128,512]{2,1,0:T(8,128)(2,1)S(1)}, u32[]{:S(2)}, u32[]{:S(2)}) %all-to-all-start.1) | async-done | bytes 1048608 | tf_op jit(solution)/shard_map/all_to_all | solution.py:964
  79.4 41.6 %all-to-all-done.2 = bf16[32,64,512]{2,1,0:T(8,128)(2,1)S(1)} async-done(((bf16[32,64,512]{2,1,0:T(8,128)(2,1)}), bf16[32,64,512]{2,1,0:T(8,128)(2,1)S(1)}, u32[]{:S(2)}, u32[]{:S(2)}) %all-to-all-start.2) | async-done | bytes 2097184 | tf_op jit(solution)/shard_map/all_to_all | solution.py:964
  124.6 11.7 %attention_forward.1 = (bf16[1024,256]{1,0:T(8,128)(2,1)}, bf16[1024,128]{1,0:T(8,128)(2,1)}, bf16[1024,128]{1,0:T(8,128)(2,1)}, bf16[1024,256]{1,0:T(8,128)(2,1)}) custom-call(s32[16]{0:T(128)} %pad_add_fusion.place, bf16[2048,512]{1,0:T(8,128)(2,1)} %bitcast.108, f32[1024,128]{1,0:T(8,128)} %get-tuple-element.251.cosine, ...), custom_call_target="tpu_custom_call" | custom-call | flops 1000 | bytes 1000 | tf_op jit(solution)/shard_map/attention_forward/pallas_call | solution.py:461
  163.1 17.0 %collective-permute-done.12.refs_1_ = bf16[128,2048]{1,0:T(8,128)(2,1)S(1)} collective-permute-done((bf16[128,2048]{1,0:T(8,128)(2,1)}, bf16[128,2048]{1,0:T(8,128)(2,1)S(1)}, u32[]{:S(2)}, u32[]{:S(2)}) %collective-permute-start.12) | collective-permute-done | bytes 524320 | tf_op jit(solution)/shard_map/ppermute | solution.py:977
  180.1 13.0 %collective-permute-done.13.refs_2_ = bf16[128,2048]{1,0:T(8,128)(2,1)S(1)} collective-permute-done((bf16[128,2048]{1,0:T(8,128)(2,1)}, bf16[128,2048]{1,0:T(8,128)(2,1)S(1)}, u32[]{:S(2)}, u32[]{:S(2)}) %collective-permute-start.13) | collective-permute-done | bytes 524320 | tf_op jit(solution)/shard_map/ppermute | solution.py:977
  202.6 11.6 %collective-permute-done.18.refs_3_ = bf16[128,2048]{1,0:T(8,128)(2,1)S(1)} collective-permute-done((bf16[128,2048]{1,0:T(8,128)(2,1)}, bf16[128,2048]{1,0:T(8,128)(2,1)S(1)}, u32[]{:S(2)}, u32[]{:S(2)}) %collective-permute-start.18) | collective-permute-done | bytes 524320 | tf_op jit(solution)/shard_map/ppermute | solution.py:990
  214.2 31.9 %collective-permute-done.17.refs_2_ = bf16[128,2048]{1,0:T(8,128)(2,1)S(1)} collective-permute-done((bf16[128,2048]{1,0:T(8,128)(2,1)}, bf16[128,2048]{1,0:T(8,128)(2,1)S(1)}, u32[]{:S(2)}, u32[]{:S(2)}) %collective-permute-start.17) | collective-permute-done | bytes 524320 | tf_op jit(solution)/shard_map/ppermute | solution.py:990
  250.9 14.4 %hidden_pass.1 = (bf16[1024,1024]{1,0:T(8,128)(2,1)}, bf16[1024,1024]{1,0:T(8,128)(2,1)}, bf16[1024,1024]{1,0:T(8,128)(2,1)}) custom-call(bf16[2,2,1024,512]{3,2,1,0:T(8,128)(2,1)} %bitcast.105, bf16[2,2,1024,512]{3,2,1,0:T(8,128)(2,1)} %bitcast.106, bf16[128,2048]{1,0:T(8,128)(2,1)} %get-tuple-element.297.refs_0_, bf16[128,2048]{1,0:T(8,128)(2,1)} %copy-done.4, ...), custom_call_target="tpu_custom_call" | custom-call | flops 1000 | bytes 1000 | tf_op jit(solution)/shard_map/hidden_pass/pallas_call | solution.py:601
  265.3 9.6 %collective-permute-done.23.refs_6_.refs_2_ = bf16[128,2048]{1,0:T(8,128)(2,1)} collective-permute-done((bf16[128,2048]{1,0:T(8,128)(2,1)}, bf16[128,2048]{1,0:T(8,128)(2,1)}, u32[]{:S(2)}, u32[]{:S(2)}) %collective-permute-start.23) | collective-permute-done | bytes 524320 | tf_op jit(solution)/shard_map/ppermute | solution.py:990
  280.5 8.3 %down_pass.1 = (bf16[128,2048]{1,0:T(8,128)(2,1)}, bf16[128,2048]{1,0:T(8,128)(2,1)}, bf16[128,2048]{1,0:T(8,128)(2,1)}, bf16[128,2048]{1,0:T(8,128)(2,1)}, bf16...) custom-call(bf16[1024,1024]{1,0:T(8,128)(2,1)} %get-tuple-element.315., ...), custom_call_target="tpu_custom_call" | custom-call | flops 1000 | bytes 1000 | tf_op jit(solution)/shard_map/down_pass/pallas_call | solution.py:556
  302.0 9.0 %term_pass.4 = bf16[4096,512]{1,0:T(8,128)(2,1)} custom-call(bf16[128,2048]{1,0:T(8,128)(2,1)} %get-tuple-element.328.refs_4_.refs_0_, bf16[128,2048]{1,0:T(8,128)(2,1)} %copy-done.16, bf16[128,2048]{1,0:T(8,128)(2,1)} %collective-permute-done.23.refs_6_.refs_2_, bf16[128,2048]{1,0:T(8,128)(2,1)} %collective-permute-done.15.refs_7_.refs_3_, ...), custom_call_target="tpu_custom_call" | custom-call | flops 1000 | bytes 1000 | tf_op jit(solution)/shard_map/term_pass/pallas_call | solution.py:699
  316.6 21.3 %grad_hidden_pass.1 = (bf16[1024,1024]{1,0:T(8,128)(2,1)}, bf16[1024,1024]{1,0:T(8,128)(2,1)}, bf16[128,2048]{1,0:T(8,128)(2,1)}, bf16[128,2048]{1,0:T(8,128)(2,...) custom-call(bf16[2,2,1024,512]{3,2,1,0:T(8,128)(2,1)} %bitcast.107, ...), custom_call_target="tpu_custom_call" | custom-call | flops 1000 | bytes 1000 | tf_op jit(solution)/shard_map/grad_hidden_pass/pallas_call | solution.py:647
  343.0 9.2 %term_pass.5 = bf16[4096,512]{1,0:T(8,128)(2,1)} custom-call(bf16[128,2048]{1,0:T(8,128)(2,1)} %get-tuple-element.297.refs_0_, bf16[128,2048]{1,0:T(8,128)(2,1)} %copy-done.4, bf16[128,2048]{1,0:T(8,128)(2,1)} %copy-done.3, bf16[128,2048]{1,0:T(8,128)(2,1)} %copy-done.2, bf16[128,2048]{1,0:T(8,128)(2,1)} %copy-done.5, ...), custom_call_target="tpu_custom_call" | custom-call | flops 1000 | bytes 1000 | tf_op jit(solution)/shard_map/term_pass/pallas_call | solution.py:699
  370.4 9.0 %term_pass.6 = bf16[4096,512]{1,0:T(8,128)(2,1)} custom-call(bf16[128,2048]{1,0:T(8,128)(2,1)} %get-tuple-element.297.refs_0_, bf16[128,2048]{1,0:T(8,128)(2,1)} %copy-done.4, bf16[128,2048]{1,0:T(8,128)(2,1)} %copy-done.3, bf16[128,2048]{1,0:T(8,128)(2,1)} %copy-done.2, bf16[128,2048]{1,0:T(8,128)(2,1)} %copy-done.5, ...), custom_call_target="tpu_custom_call" | custom-call | flops 1000 | bytes 1000 | tf_op jit(solution)/shard_map/term_pass/pallas_call | solution.py:699
  379.5 28.0 %all-to-all-done.5 = f32[32,1,128]{2,1,0:T(1,128)S(1)} async-done(((f32[32,1,128]{2,1,0:T(1,128)}), f32[32,1,128]{2,1,0:T(1,128)S(1)}, u32[]{:S(2)}, u32[]{:S(2)}) %all-to-all-start.5) | async-done | bytes 16416 | tf_op jit(solution)/shard_map/all_to_all | solution.py:964
  420.9 13.9 %collective-permute-done.45.refs_3_ = bf16[128,2048]{1,0:T(8,128)(2,1)S(1)} collective-permute-done((bf16[128,2048]{1,0:T(8,128)(2,1)}, bf16[128,2048]{1,0:T(8,128)(2,1)S(1)}, u32[]{:S(2)}, u32[]{:S(2)}) %collective-permute-start.45) | collective-permute-done | bytes 524320 | tf_op jit(solution)/shard_map/ppermute | solution.py:977
  434.8 10.2 %collective-permute-done.44.refs_2_ = bf16[128,2048]{1,0:T(8,128)(2,1)S(1)} collective-permute-done((bf16[128,2048]{1,0:T(8,128)(2,1)}, bf16[128,2048]{1,0:T(8,128)(2,1)S(1)}, u32[]{:S(2)}, u32[]{:S(2)}) %collective-permute-start.44) | collective-permute-done | bytes 524320 | tf_op jit(solution)/shard_map/ppermute | solution.py:977
  455.0 13.8 %attention_backward.1.rows.refs_8_ = bf16[1024,512]{1,0:T(8,128)(2,1)} custom-call(s32[16]{0:T(128)} %pad_add_fusion.place, bf16[2048,256]{1,0:T(8,128)(2,1)} %all-gather.5.cloned.1.call-done.refs_0_.weight, bf16[1024,256]{1,0:T(8,128)(2,1)} %get-tuple-element.372.query, bf16[1024,128]{1,0:T(8,128)(2,1)} %get-tuple-element.373.key, ...), custom_call_target="tpu_custom_call" | custom-call | flops 1000 | bytes 1000 | tf_op jit(solution)/shard_map/attention_backward/pallas_call | solution.py:514
  502.1 16.4 %all-to-all-done.8 = bf16[32,64,256]{2,1,0:T(8,128)(2,1)S(1)} async-done(((bf16[32,64,256]{2,1,0:T(8,128)(2,1)}), bf16[32,64,256]{2,1,0:T(8,128)(2,1)S(1)}, u32[]{:S(2)}, u32[]{:S(2)}) %all-to-all-start.8) | async-done | bytes 1048608 | tf_op jit(solution)/shard_map/all_to_all | solution.py:964
  526.1 11.2 %collective-permute-done.54.refs_1_ = bf16[128,2048]{1,0:T(8,128)(2,1)S(1)} collective-permute-done((bf16[128,2048]{1,0:T(8,128)(2,1)}, bf16[128,2048]{1,0:T(8,128)(2,1)S(1)}, u32[]{:S(2)}, u32[]{:S(2)}) %collective-permute-start.54) | collective-permute-done | bytes 524320 | tf_op jit(solution)/shard_map/ppermute | solution.py:977
  537.4 11.8 %collective-permute-done.55.refs_2_ = bf16[128,2048]{1,0:T(8,128)(2,1)S(1)} collective-permute-done((bf16[128,2048]{1,0:T(8,128)(2,1)}, bf16[128,2048]{1,0:T(8,128)(2,1)S(1)}, u32[]{:S(2)}, u32[]{:S(2)}) %collective-permute-start.55) | collective-permute-done | bytes 524320 | tf_op jit(solution)/shard_map/ppermute | solution.py:977
  549.2 13.9 %all-to-all-done.9 = bf16[8,128,512]{2,1,0:T(8,128)(2,1)S(1)} async-done(((bf16[8,128,512]{2,1,0:T(8,128)(2,1)}), bf16[8,128,512]{2,1,0:T(8,128)(2,1)S(1)}, u32[]{:S(2)}, u32[]{:S(2)}) %all-to-all-start.9) | async-done | bytes 1048608 | tf_op jit(solution)/shard_map/all_to_all | solution.py:964
  579.5 14.2 %all-to-all-done.10 = bf16[32,64,256]{2,1,0:T(8,128)(2,1)S(1)} async-done(((bf16[32,64,256]{2,1,0:T(8,128)(2,1)}), bf16[32,64,256]{2,1,0:T(8,128)(2,1)S(1)}, u32[]{:S(2)}, u32[]{:S(2)}) %all-to-all-start.10) | async-done | bytes 1048608 | tf_op jit(solution)/shard_map/all_to_all | solution.py:964
  (336 shorter events, 232.7 us)
Async XLA Ops:
  22.4 45.1 %all-to-all-start.1 = ((bf16[8,128,512]{2,1,0:T(8,128)(2,1)}), bf16[8,128,512]{2,1,0:T(8,128)(2,1)S(1)}, u32[]{:S(2)}, u32[]{:S(2)}) async-start(bf16[8,128,512]{2,1,0:T(8,128)(2,1)} %bitcast.112), calls=%async_computation.1 | async-start | bytes 2097152 | tf_op jit(solution)/shard_map/all_to_all | solution.py:964
  27.3 109.0 %all-gather.5.cloned.1.call-start = ((), (), s32[]{:S(2)}) async-start(), calls=%async_computation.16 | async-start | bytes 1310720 | tf_op jit(solution)/shard_map/all_gather | solution.py:1066
  28.0 218.6 %all-gather.7.cloned.1.call-start = ((), (), s32[]{:S(2)}) async-start(), calls=%async_computation.17 | async-start | bytes 5242880 | tf_op jit(solution)/shard_map/all_gather | solution.py:1064
  68.5 52.4 %all-to-all-start.2 = ((bf16[32,64,512]{2,1,0:T(8,128)(2,1)}), bf16[32,64,512]{2,1,0:T(8,128)(2,1)S(1)}, u32[]{:S(2)}, u32[]{:S(2)}) async-start(bf16[32,64,512]{2,1,0:T(8,128)(2,1)} %bitcast.110), calls=%async_computation.2 | async-start | bytes 4194304 | tf_op jit(solution)/shard_map/all_to_all | solution.py:964
  124.5 124.4 %all-gather.9.cloned.1.call-start = ((), (), s32[]{:S(2)}) async-start(), calls=%async_computation.18 | async-start | bytes 5242880 | tf_op jit(solution)/shard_map/all_gather | solution.py:1064
  152.0 41.7 %all-to-all-start.4 = ((bf16[8,128,512]{2,1,0:T(8,128)(2,1)}), bf16[8,128,512]{2,1,0:T(8,128)(2,1)S(1)}, u32[]{:S(2)}, u32[]{:S(2)}) async-start(bf16[8,128,512]{2,1,0:T(8,128)(2,1)} %bitcast.17), calls=%async_computation.4 | async-start | bytes 2097152 | tf_op jit(solution)/shard_map/all_to_all | solution.py:964
  155.6 123.4 %all-gather.11.cloned.1.call-start = ((), (), s32[]{:S(2)}) async-start(), calls=%async_computation.19 | async-start | bytes 5242880 | tf_op jit(solution)/shard_map/all_gather | solution.py:1064
  157.3 35.7 %collective-permute-start.13 = (bf16[128,2048]{1,0:T(8,128)(2,1)}, bf16[128,2048]{1,0:T(8,128)(2,1)S(1)}, u32[]{:S(2)}, u32[]{:S(2)}) collective-permute-start(bf16[128,2048]{1,0:T(8,128)(2,1)} %get-tuple-element.279), channel_id=1, source_target_pairs={{0,4},{4,0},{1,5},{5,1},{2,6},{6,2},{3,7},{7,3},{8,12},{12,8},{9,1... | collective-permute-start | bytes 1572872 | tf_op jit(solution)/shard_map/ppermute | solution.py:977
  158.9 34.8 %collective-permute-start.14 = (bf16[128,2048]{1,0:T(8,128)(2,1)}, bf16[128,2048]{1,0:T(8,128)(2,1)S(1)}, u32[]{:S(2)}, u32[]{:S(2)}) collective-permute-start(bf16[128,2048]{1,0:T(8,128)(2,1)} %get-tuple-element.280), channel_id=1, source_target_pairs={{0,5},{1,4},{4,1},{5,0},{2,7},{3,6},{6,3},{7,2},{8,13},{9,12},{12,... | collective-permute-start | bytes 1572872 | tf_op jit(solution)/shard_map/ppermute | solution.py:977
  159.4 34.3 %collective-permute-start.15 = (bf16[128,2048]{1,0:T(8,128)(2,1)S(1)}, bf16[128,2048]{1,0:T(8,128)(2,1)}, u32[]{:S(2)}, u32[]{:S(2)}) collective-permute-start(bf16[128,2048]{1,0:T(8,128)(2,1)S(1)} %copy-done.14), channel_id=1, source_target_pairs={{0,24},{8,0},{16,8},{24,16},{1,25},{9,1},{17,9},{25,17},{2,26},{10... | collective-permute-start | bytes 1572872 | tf_op jit(solution)/shard_map/ppermute | solution.py:990
  197.9 209.7 %reduce-scatter.5.cloned.1.call-start = ((), (), s32[]{:S(2)}) async-start(), calls=%async_computation.20 | async-start | bytes 5242880 | tf_op jit(solution)/shard_map/reduce_scatter | solution.py:1128
  201.5 44.6 %collective-permute-start.17 = (bf16[128,2048]{1,0:T(8,128)(2,1)}, bf16[128,2048]{1,0:T(8,128)(2,1)S(1)}, u32[]{:S(2)}, u32[]{:S(2)}) collective-permute-start(bf16[128,2048]{1,0:T(8,128)(2,1)} %get-tuple-element.297.refs_0_), channel_id=1, source_target_pairs={{0,16},{8,24},{16,0},{24,8},{1,17},{9,25},{17,1},{25,9},{2,18},{10... | collective-permute-start | bytes 1572872 | tf_op jit(solution)/shard_map/ppermute | solution.py:990
  201.5 44.6 %collective-permute-start.16 = (bf16[128,2048]{1,0:T(8,128)(2,1)}, bf16[128,2048]{1,0:T(8,128)(2,1)S(1)}, u32[]{:S(2)}, u32[]{:S(2)}) collective-permute-start(bf16[128,2048]{1,0:T(8,128)(2,1)} %get-tuple-element.297.refs_0_), channel_id=1, source_target_pairs={{0,8},{8,16},{16,24},{24,0},{1,9},{9,17},{17,25},{25,1},{2,10},{10... | collective-permute-start | bytes 1572872 | tf_op jit(solution)/shard_map/ppermute | solution.py:990
  202.6 44.0 %collective-permute-start.19 = (bf16[128,2048]{1,0:T(8,128)(2,1)}, bf16[128,2048]{1,0:T(8,128)(2,1)S(1)}, u32[]{:S(2)}, u32[]{:S(2)}) collective-permute-start(bf16[128,2048]{1,0:T(8,128)(2,1)} %get-tuple-element.297.refs_0_), channel_id=1, source_target_pairs={{0,2},{2,0},{1,3},{3,1},{4,6},{6,4},{5,7},{7,5},{8,10},{10,8},{9,1... | collective-permute-start | bytes 1572872 | tf_op jit(solution)/shard_map/ppermute | solution.py:977
  315.5 129.5 %reduce-scatter.7.cloned.1.call-start = ((), (), s32[]{:S(2)}) async-start(), calls=%async_computation.21 | async-start | bytes 5242880 | tf_op jit(solution)/shard_map/reduce_scatter | solution.py:1128
  359.0 48.5 %collective-permute-start.40 = (bf16[128,2048]{1,0:T(8,128)(2,1)}, bf16[128,2048]{1,0:T(8,128)(2,1)S(1)}, u32[]{:S(2)}, u32[]{:S(2)}) collective-permute-start(bf16[128,2048]{1,0:T(8,128)(2,1)} %get-tuple-element.376), channel_id=1, source_target_pairs={{0,24},{8,0},{16,8},{24,16},{1,25},{9,1},{17,9},{25,17},{2,26},{10... | collective-permute-start | bytes 1572872 | tf_op jit(solution)/shard_map/ppermute | solution.py:990
  361.9 45.6 %collective-permute-start.41 = (bf16[128,2048]{1,0:T(8,128)(2,1)S(1)}, bf16[128,2048]{1,0:T(8,128)(2,1)S(1)}, u32[]{:S(2)}, u32[]{:S(2)}) collective-permute-start(bf16[128,2048]{1,0:T(8,128)(2,1)S(1)} %copy-done.66), channel_id=1, source_target_pairs={{0,16},{8,24},{16,0},{24,8},{1,17},{9,25},{17,1},{25,9},{2,18},{10... | collective-permute-start | bytes 1572872 | tf_op jit(solution)/shard_map/ppermute | solution.py:990
  361.9 45.6 %collective-permute-start.42 = (bf16[128,2048]{1,0:T(8,128)(2,1)S(1)}, bf16[128,2048]{1,0:T(8,128)(2,1)S(1)}, u32[]{:S(2)}, u32[]{:S(2)}) collective-permute-start(bf16[128,2048]{1,0:T(8,128)(2,1)S(1)} %copy-done.65), channel_id=1, source_target_pairs={{0,8},{8,16},{16,24},{24,0},{1,9},{9,17},{17,25},{25,1},{2,10},{10... | collective-permute-start | bytes 1572872 | tf_op jit(solution)/shard_map/ppermute | solution.py:990
  366.2 41.3 %all-to-all-start.5 = ((f32[32,1,128]{2,1,0:T(1,128)}), f32[32,1,128]{2,1,0:T(1,128)S(1)}, u32[]{:S(2)}, u32[]{:S(2)}) async-start(f32[32,1,128]{2,1,0:T(1,128)} %bitcast.132), calls=%async_computation.6 | async-start | bytes 32768 | tf_op jit(solution)/shard_map/all_to_all | solution.py:964
  407.5 37.5 %all-to-all-start.6 = ((bf16[8,128,512]{2,1,0:T(8,128)(2,1)}), bf16[8,128,512]{2,1,0:T(8,128)(2,1)S(1)}, u32[]{:S(2)}, u32[]{:S(2)}) async-start(bf16[8,128,512]{2,1,0:T(8,128)(2,1)} %bitcast.124), calls=%async_computation.8 | async-start | bytes 2097152 | tf_op jit(solution)/shard_map/all_to_all | solution.py:964
  413.4 105.2 %reduce-scatter.9.cloned.1.call-start = ((), (), s32[]{:S(2)}) async-start(), calls=%async_computation.22 | async-start | bytes 5242880 | tf_op jit(solution)/shard_map/reduce_scatter | solution.py:1128
  450.2 37.0 %all-to-all-start.7 = ((bf16[8,128,512]{2,1,0:T(8,128)(2,1)}), bf16[8,128,512]{2,1,0:T(8,128)(2,1)S(1)}, u32[]{:S(2)}, u32[]{:S(2)}) async-start(bf16[8,128,512]{2,1,0:T(8,128)(2,1)} %bitcast.123), calls=%async_computation.9 | async-start | bytes 2097152 | tf_op jit(solution)/shard_map/all_to_all | solution.py:964
  518.5 44.6 %all-to-all-start.9 = ((bf16[8,128,512]{2,1,0:T(8,128)(2,1)}), bf16[8,128,512]{2,1,0:T(8,128)(2,1)S(1)}, u32[]{:S(2)}, u32[]{:S(2)}) async-start(bf16[8,128,512]{2,1,0:T(8,128)(2,1)} %bitcast.126), calls=%async_computation.12 | async-start | bytes 2097152 | tf_op jit(solution)/shard_map/all_to_all | solution.py:964
  522.3 57.2 %reduce-scatter.11.cloned.1.call-start = ((), (), s32[]{:S(2)}) async-start(), calls=%async_computation.23 | async-start | bytes 1310720 | tf_op jit(solution)/shard_map/reduce_scatter | solution.py:1172
  (122 other events, 1103.7 us)
Sparse Core Ops, SparseCore 0:
  29.7 41.3 all-gather.4
  73.5 65.1 all-gather.6
  152.2 72.4 all-gather.8
  226.3 52.6 all-gather.10
  314.8 52.6 reduce-scatter.4
  371.3 64.7 reduce-scatter.6
  450.2 62.3 reduce-scatter.8
  526.1 40.1 reduce-scatter.10

commit v7 on v6

--- a/solution.py
+++ b/solution.py
@@ -667,28 +667,17 @@
     out[...] = low(dot32(rows, columns[...], BY_ROWS))
 
 
-def term_halves_body(*refs):
-    pieces, columns, outs = refs[:-3], refs[-3], refs[-2:]
-    rows = jnp.concatenate([piece[...] for piece in pieces], axis=0)
-    term = low(dot32(rows, columns[...], BY_ROWS))
-    for number, out in enumerate(outs):
-
-        @pl.when(pl.program_id(1) == number)
-        def _(out=out):
-            out[...] = term
-
-
-def term_halves(pieces, columns):
+def term_half(pieces, columns, part):
     tokens, width = pieces[0].shape
     depth, chunk = width // 2, columns.shape[1] // 2
     return pl.pallas_call(
-        term_halves_body,
-        grid=(2, 2),
-        out_shape=(low_shape(width, chunk),) * 2,
-        in_specs=[pl.BlockSpec((tokens, depth), lambda y, x: (0, y))] * len(pieces)
-        + [pl.BlockSpec((columns.shape[0], chunk), lambda y, x: (0, x))],
-        out_specs=(pl.BlockSpec((depth, chunk), lambda y, x: (y, 0)),) * 2,
-        name="term_halves",
+        term_body,
+        grid=(2,),
+        out_shape=low_shape(width, chunk),
+        in_specs=[pl.BlockSpec((tokens, depth), lambda y: (0, y))] * len(pieces)
+        + [pl.BlockSpec((columns.shape[0], chunk), lambda y: (0, part))],
+        out_specs=pl.BlockSpec((depth, chunk), lambda y: (y, 0)),
+        name="term_half",
         **KERNEL,
     )(*pieces, columns)
 
@@ -1157,12 +1146,13 @@
     gate_back = exchange(gate_t, GROUP_AXES)
     grad_qkv = attention_backward(grad_out_p, wo, query, key, value, *rows_info)
     gx_parts = core_back(by_cols_pass(grad_qkv, wq, 1, plane, "qkv_back_pass"))
-    query_term, rest_term = term_halves(normed_p, grad_qkv)
-    gx_parts, query_term, rest_term, gate_back, down_back, heads = together(
-        gx_parts, query_term, rest_term, gate_back, down_back, heads
+    query_term = term_half(normed_p, grad_qkv, 0)
+    gx_parts, query_term, grad_qkv, gate_back, down_back, heads = together(
+        gx_parts, query_term, grad_qkv, gate_back, down_back, heads
     )
 
     query_sum = exchange(query_term, ALL_AXES)
+    rest_term = term_half(normed_p, grad_qkv, 1)
     out_term = term_pass(grad_out_p, heads, 2, 1)
     down_grad = side_by_side(down_back, hgroups)
     query_sum, up_t, out_term, down_grad, rest_term, gx_parts = together(

time: 623 us -> 620 us (level)
  transfers between devices with their start and end apart: 78 -> 78, of which waited for: 35 -> 35; matrix products, arithmetic and copies ran while one was open for 2% -> 2% of each run, Pallas kernels for 28% -> 29%
where the time goes in v7:
time: 620 us; the launch traced here: 610 us
  waiting for transfers between devices  297 us (48%)
  Pallas kernels  176 us (28%)
  starting transfers between devices  97.4 us (16%)
  local copies, waits for them, and re-layouts  15.6 us (3%)
  between operations  15.4 us (2%)
  other arithmetic  8.84 us (1%)
    all_to_all x12, waiting for transfers between devices, exchange(): return lax.all_to_all(values, axes, split_axis=0, concat_axis=0, tiled=True)  124 us
    ppermute x46, waiting for transfers between devices, swap(): return lax.ppermute(values, axes if len(axes) > 1 else axes[0], pairs)  103 us
    ppermute x12, waiting for transfers between devices, shift(): lax.ppermute(values, 'dp', [(i, (i + by) % count) for i in range(count)])  65.5 us
    all_to_all x12, starting transfers between devices, exchange(): return lax.all_to_all(values, axes, split_axis=0, concat_axis=0, tiled=True)  51 us
    pallas_call x4, Pallas kernels, term_pass(): pl.pallas_call(term_body, grid=(row_parts, col_parts), out_shape=low_shap...  31.8 us
    ppermute x46, starting transfers between devices, swap(): return lax.ppermute(values, axes if len(axes) > 1 else axes[0], pairs)  27 us
    pallas_call x1, Pallas kernels, grad_hidden_pass(): pl.pallas_call(grad_hidden_body, grid=(4 + width // STRIPE,), out_shape=(...  21.3 us
    ppermute x12, starting transfers between devices, shift(): lax.ppermute(values, 'dp', [(i, (i + by) % count) for i in range(count)])  18.3 us
  transfers between devices with their start and end apart: 78, of which 35 were waited for; matrix products, arithmetic and copies ran while one was open for 2% of the time, Pallas kernels for 29%

profile of v7, /device:TPU:0, one launch (start us, length us, event | category | flops | bytes accessed | tf_op | source)
XLA Modules:
  0.0 610.0 jit_solution(4527929562267552134)
XLA Ops:
  44.0 10.9 %collective-permute-done.2.refs_2_ = bf16[128,2048]{1,0:T(8,128)(2,1)S(1)} collective-permute-done((bf16[128,2048]{1,0:T(8,128)(2,1)S(1)}, bf16[128,2048]{1,0:T(8,128)(2,1)S(1)}, u32[]{:S(2)}, u32[]{:S(2)}) %collective-permute-start.2) | collective-permute-done | bytes 524320 | tf_op jit(solution)/shard_map/ppermute | solution.py:966
  55.2 12.4 %all-to-all-done.1 = bf16[8,128,512]{2,1,0:T(8,128)(2,1)S(1)} async-done(((bf16[8,128,512]{2,1,0:T(8,128)(2,1)}), bf16[8,128,512]{2,1,0:T(8,128)(2,1)S(1)}, u32[]{:S(2)}, u32[]{:S(2)}) %all-to-all-start.1) | async-done | bytes 1048608 | tf_op jit(solution)/shard_map/all_to_all | solution.py:953
  79.5 41.6 %all-to-all-done.2 = bf16[32,64,512]{2,1,0:T(8,128)(2,1)S(1)} async-done(((bf16[32,64,512]{2,1,0:T(8,128)(2,1)}), bf16[32,64,512]{2,1,0:T(8,128)(2,1)S(1)}, u32[]{:S(2)}, u32[]{:S(2)}) %all-to-all-start.2) | async-done | bytes 2097184 | tf_op jit(solution)/shard_map/all_to_all | solution.py:953
  124.6 11.7 %attention_forward.1 = (bf16[1024,256]{1,0:T(8,128)(2,1)}, bf16[1024,128]{1,0:T(8,128)(2,1)}, bf16[1024,128]{1,0:T(8,128)(2,1)}, bf16[1024,256]{1,0:T(8,128)(2,1)}) custom-call(s32[16]{0:T(128)} %pad_add_fusion.place, bf16[2048,512]{1,0:T(8,128)(2,1)} %bitcast.108, f32[1024,128]{1,0:T(8,128)} %get-tuple-element.249.cosine, ...), custom_call_target="tpu_custom_call" | custom-call | flops 1000 | bytes 1000 | tf_op jit(solution)/shard_map/attention_forward/pallas_call | solution.py:461
  163.4 17.3 %collective-permute-done.12.refs_1_ = bf16[128,2048]{1,0:T(8,128)(2,1)S(1)} collective-permute-done((bf16[128,2048]{1,0:T(8,128)(2,1)}, bf16[128,2048]{1,0:T(8,128)(2,1)S(1)}, u32[]{:S(2)}, u32[]{:S(2)}) %collective-permute-start.12) | collective-permute-done | bytes 524320 | tf_op jit(solution)/shard_map/ppermute | solution.py:966
  180.7 12.7 %collective-permute-done.13.refs_2_ = bf16[128,2048]{1,0:T(8,128)(2,1)S(1)} collective-permute-done((bf16[128,2048]{1,0:T(8,128)(2,1)}, bf16[128,2048]{1,0:T(8,128)(2,1)S(1)}, u32[]{:S(2)}, u32[]{:S(2)}) %collective-permute-start.13) | collective-permute-done | bytes 524320 | tf_op jit(solution)/shard_map/ppermute | solution.py:966
  202.9 11.6 %collective-permute-done.18.refs_3_ = bf16[128,2048]{1,0:T(8,128)(2,1)S(1)} collective-permute-done((bf16[128,2048]{1,0:T(8,128)(2,1)}, bf16[128,2048]{1,0:T(8,128)(2,1)S(1)}, u32[]{:S(2)}, u32[]{:S(2)}) %collective-permute-start.18) | collective-permute-done | bytes 524320 | tf_op jit(solution)/shard_map/ppermute | solution.py:979
  214.5 31.9 %collective-permute-done.17.refs_2_ = bf16[128,2048]{1,0:T(8,128)(2,1)S(1)} collective-permute-done((bf16[128,2048]{1,0:T(8,128)(2,1)}, bf16[128,2048]{1,0:T(8,128)(2,1)S(1)}, u32[]{:S(2)}, u32[]{:S(2)}) %collective-permute-start.17) | collective-permute-done | bytes 524320 | tf_op jit(solution)/shard_map/ppermute | solution.py:979
  251.2 14.4 %hidden_pass.1 = (bf16[1024,1024]{1,0:T(8,128)(2,1)}, bf16[1024,1024]{1,0:T(8,128)(2,1)}, bf16[1024,1024]{1,0:T(8,128)(2,1)}) custom-call(bf16[2,2,1024,512]{3,2,1,0:T(8,128)(2,1)} %bitcast.105, bf16[2,2,1024,512]{3,2,1,0:T(8,128)(2,1)} %bitcast.106, bf16[128,2048]{1,0:T(8,128)(2,1)} %get-tuple-element.295.refs_0_, bf16[128,2048]{1,0:T(8,128)(2,1)} %copy-done.4, ...), custom_call_target="tpu_custom_call" | custom-call | flops 1000 | bytes 1000 | tf_op jit(solution)/shard_map/hidden_pass/pallas_call | solution.py:601
  265.6 9.6 %collective-permute-done.23.refs_6_.refs_2_ = bf16[128,2048]{1,0:T(8,128)(2,1)} collective-permute-done((bf16[128,2048]{1,0:T(8,128)(2,1)}, bf16[128,2048]{1,0:T(8,128)(2,1)}, u32[]{:S(2)}, u32[]{:S(2)}) %collective-permute-start.23) | collective-permute-done | bytes 524320 | tf_op jit(solution)/shard_map/ppermute | solution.py:979
  280.8 8.3 %down_pass.1 = (bf16[128,2048]{1,0:T(8,128)(2,1)}, bf16[128,2048]{1,0:T(8,128)(2,1)}, bf16[128,2048]{1,0:T(8,128)(2,1)}, bf16[128,2048]{1,0:T(8,128)(2,1)}, bf16...) custom-call(bf16[1024,1024]{1,0:T(8,128)(2,1)} %get-tuple-element.313., ...), custom_call_target="tpu_custom_call" | custom-call | flops 1000 | bytes 1000 | tf_op jit(solution)/shard_map/down_pass/pallas_call | solution.py:556
  302.3 9.0 %term_pass.4 = bf16[4096,512]{1,0:T(8,128)(2,1)} custom-call(bf16[128,2048]{1,0:T(8,128)(2,1)} %get-tuple-element.326.refs_4_.refs_0_, bf16[128,2048]{1,0:T(8,128)(2,1)} %copy-done.23, bf16[128,2048]{1,0:T(8,128)(2,1)} %collective-permute-done.23.refs_6_.refs_2_, bf16[128,2048]{1,0:T(8,128)(2,1)} %collective-permute-done.15.refs_7_.refs_3_, ...), custom_call_target="tpu_custom_call" | custom-call | flops 1000 | bytes 1000 | tf_op jit(solution)/shard_map/term_pass/pallas_call | solution.py:688
  316.6 21.3 %grad_hidden_pass.1 = (bf16[1024,1024]{1,0:T(8,128)(2,1)}, bf16[1024,1024]{1,0:T(8,128)(2,1)}, bf16[128,2048]{1,0:T(8,128)(2,1)}, bf16[128,2048]{1,0:T(8,128)(2,...) custom-call(bf16[2,2,1024,512]{3,2,1,0:T(8,128)(2,1)} %bitcast.107, ...), custom_call_target="tpu_custom_call" | custom-call | flops 1000 | bytes 1000 | tf_op jit(solution)/shard_map/grad_hidden_pass/pallas_call | solution.py:647
  342.8 9.2 %term_pass.5 = bf16[4096,512]{1,0:T(8,128)(2,1)} custom-call(bf16[128,2048]{1,0:T(8,128)(2,1)} %get-tuple-element.295.refs_0_, bf16[128,2048]{1,0:T(8,128)(2,1)} %copy-done.4, bf16[128,2048]{1,0:T(8,128)(2,1)} %copy-done.3, bf16[128,2048]{1,0:T(8,128)(2,1)} %copy-done.2, bf16[128,2048]{1,0:T(8,128)(2,1)} %copy-done.5, ...), custom_call_target="tpu_custom_call" | custom-call | flops 1000 | bytes 1000 | tf_op jit(solution)/shard_map/term_pass/pallas_call | solution.py:688
  370.6 9.1 %term_pass.6 = bf16[4096,512]{1,0:T(8,128)(2,1)} custom-call(bf16[128,2048]{1,0:T(8,128)(2,1)} %get-tuple-element.295.refs_0_, bf16[128,2048]{1,0:T(8,128)(2,1)} %copy-done.4, bf16[128,2048]{1,0:T(8,128)(2,1)} %copy-done.3, bf16[128,2048]{1,0:T(8,128)(2,1)} %copy-done.2, bf16[128,2048]{1,0:T(8,128)(2,1)} %copy-done.5, ...), custom_call_target="tpu_custom_call" | custom-call | flops 1000 | bytes 1000 | tf_op jit(solution)/shard_map/term_pass/pallas_call | solution.py:688
  379.7 27.9 %all-to-all-done.5 = f32[32,1,128]{2,1,0:T(1,128)S(1)} async-done(((f32[32,1,128]{2,1,0:T(1,128)}), f32[32,1,128]{2,1,0:T(1,128)S(1)}, u32[]{:S(2)}, u32[]{:S(2)}) %all-to-all-start.5) | async-done | bytes 16416 | tf_op jit(solution)/shard_map/all_to_all | solution.py:953
  421.3 13.7 %collective-permute-done.45.refs_3_ = bf16[128,2048]{1,0:T(8,128)(2,1)S(1)} collective-permute-done((bf16[128,2048]{1,0:T(8,128)(2,1)}, bf16[128,2048]{1,0:T(8,128)(2,1)S(1)}, u32[]{:S(2)}, u32[]{:S(2)}) %collective-permute-start.45) | collective-permute-done | bytes 524320 | tf_op jit(solution)/shard_map/ppermute | solution.py:966
  435.1 10.2 %collective-permute-done.44.refs_2_ = bf16[128,2048]{1,0:T(8,128)(2,1)S(1)} collective-permute-done((bf16[128,2048]{1,0:T(8,128)(2,1)}, bf16[128,2048]{1,0:T(8,128)(2,1)S(1)}, u32[]{:S(2)}, u32[]{:S(2)}) %collective-permute-start.44) | collective-permute-done | bytes 524320 | tf_op jit(solution)/shard_map/ppermute | solution.py:966
  455.1 13.9 %attention_backward.1.rows.refs_8_ = bf16[1024,512]{1,0:T(8,128)(2,1)} custom-call(s32[16]{0:T(128)} %pad_add_fusion.place, bf16[2048,256]{1,0:T(8,128)(2,1)} %all-gather.5.cloned.1.call-done.refs_0_.weight, bf16[1024,256]{1,0:T(8,128)(2,1)} %get-tuple-element.370.query, bf16[1024,128]{1,0:T(8,128)(2,1)} %get-tuple-element.371.key, ...), custom_call_target="tpu_custom_call" | custom-call | flops 1000 | bytes 1000 | tf_op jit(solution)/shard_map/attention_backward/pallas_call | solution.py:514
  504.4 11.9 %all-to-all-done.8 = bf16[32,64,256]{2,1,0:T(8,128)(2,1)S(1)} async-done(((bf16[32,64,256]{2,1,0:T(8,128)(2,1)}), bf16[32,64,256]{2,1,0:T(8,128)(2,1)S(1)}, u32[]{:S(2)}, u32[]{:S(2)}) %all-to-all-start.8) | async-done | bytes 1048608 | tf_op jit(solution)/shard_map/all_to_all | solution.py:953
  523.7 11.2 %collective-permute-done.54.refs_1_ = bf16[128,2048]{1,0:T(8,128)(2,1)S(1)} collective-permute-done((bf16[128,2048]{1,0:T(8,128)(2,1)}, bf16[128,2048]{1,0:T(8,128)(2,1)S(1)}, u32[]{:S(2)}, u32[]{:S(2)}) %collective-permute-start.54) | collective-permute-done | bytes 524320 | tf_op jit(solution)/shard_map/ppermute | solution.py:966
  535.0 11.9 %collective-permute-done.55.refs_2_ = bf16[128,2048]{1,0:T(8,128)(2,1)} collective-permute-done((bf16[128,2048]{1,0:T(8,128)(2,1)}, bf16[128,2048]{1,0:T(8,128)(2,1)}, u32[]{:S(2)}, u32[]{:S(2)}) %collective-permute-start.55) | collective-permute-done | bytes 524320 | tf_op jit(solution)/shard_map/ppermute | solution.py:966
  546.9 13.8 %all-to-all-done.9 = bf16[8,128,512]{2,1,0:T(8,128)(2,1)S(1)} async-done(((bf16[8,128,512]{2,1,0:T(8,128)(2,1)}), bf16[8,128,512]{2,1,0:T(8,128)(2,1)S(1)}, u32[]{:S(2)}, u32[]{:S(2)}) %all-to-all-start.9) | async-done | bytes 1048608 | tf_op jit(solution)/shard_map/all_to_all | solution.py:953
  577.1 14.2 %all-to-all-done.10 = bf16[32,64,256]{2,1,0:T(8,128)(2,1)S(1)} async-done(((bf16[32,64,256]{2,1,0:T(8,128)(2,1)}), bf16[32,64,256]{2,1,0:T(8,128)(2,1)S(1)}, u32[]{:S(2)}, u32[]{:S(2)}) %all-to-all-start.10) | async-done | bytes 1048608 | tf_op jit(solution)/shard_map/all_to_all | solution.py:953
  (335 shorter events, 235.1 us)
Async XLA Ops:
  22.5 45.1 %all-to-all-start.1 = ((bf16[8,128,512]{2,1,0:T(8,128)(2,1)}), bf16[8,128,512]{2,1,0:T(8,128)(2,1)S(1)}, u32[]{:S(2)}, u32[]{:S(2)}) async-start(bf16[8,128,512]{2,1,0:T(8,128)(2,1)} %bitcast.112), calls=%async_computation.1 | async-start | bytes 2097152 | tf_op jit(solution)/shard_map/all_to_all | solution.py:953
  27.4 108.9 %all-gather.5.cloned.1.call-start = ((), (), s32[]{:S(2)}) async-start(), calls=%async_computation.16 | async-start | bytes 1310720 | tf_op jit(solution)/shard_map/all_gather | solution.py:1055
  28.1 218.8 %all-gather.7.cloned.1.call-start = ((), (), s32[]{:S(2)}) async-start(), calls=%async_computation.17 | async-start | bytes 5242880 | tf_op jit(solution)/shard_map/all_gather | solution.py:1053
  68.6 52.4 %all-to-all-start.2 = ((bf16[32,64,512]{2,1,0:T(8,128)(2,1)}), bf16[32,64,512]{2,1,0:T(8,128)(2,1)S(1)}, u32[]{:S(2)}, u32[]{:S(2)}) async-start(bf16[32,64,512]{2,1,0:T(8,128)(2,1)} %bitcast.110), calls=%async_computation.2 | async-start | bytes 4194304 | tf_op jit(solution)/shard_map/all_to_all | solution.py:953
  124.6 124.6 %all-gather.9.cloned.1.call-start = ((), (), s32[]{:S(2)}) async-start(), calls=%async_computation.18 | async-start | bytes 5242880 | tf_op jit(solution)/shard_map/all_gather | solution.py:1053
  152.1 41.9 %all-to-all-start.4 = ((bf16[8,128,512]{2,1,0:T(8,128)(2,1)}), bf16[8,128,512]{2,1,0:T(8,128)(2,1)S(1)}, u32[]{:S(2)}, u32[]{:S(2)}) async-start(bf16[8,128,512]{2,1,0:T(8,128)(2,1)} %bitcast.17), calls=%async_computation.4 | async-start | bytes 2097152 | tf_op jit(solution)/shard_map/all_to_all | solution.py:953
  155.7 123.7 %all-gather.11.cloned.1.call-start = ((), (), s32[]{:S(2)}) async-start(), calls=%async_computation.19 | async-start | bytes 5242880 | tf_op jit(solution)/shard_map/all_gather | solution.py:1053
  157.7 35.7 %collective-permute-start.13 = (bf16[128,2048]{1,0:T(8,128)(2,1)}, bf16[128,2048]{1,0:T(8,128)(2,1)S(1)}, u32[]{:S(2)}, u32[]{:S(2)}) collective-permute-start(bf16[128,2048]{1,0:T(8,128)(2,1)} %get-tuple-element.277), channel_id=1, source_target_pairs={{0,4},{4,0},{1,5},{5,1},{2,6},{6,2},{3,7},{7,3},{8,12},{12,8},{9,1... | collective-permute-start | bytes 1572872 | tf_op jit(solution)/shard_map/ppermute | solution.py:966
  159.2 34.8 %collective-permute-start.14 = (bf16[128,2048]{1,0:T(8,128)(2,1)}, bf16[128,2048]{1,0:T(8,128)(2,1)S(1)}, u32[]{:S(2)}, u32[]{:S(2)}) collective-permute-start(bf16[128,2048]{1,0:T(8,128)(2,1)} %get-tuple-element.278), channel_id=1, source_target_pairs={{0,5},{1,4},{4,1},{5,0},{2,7},{3,6},{6,3},{7,2},{8,13},{9,12},{12,... | collective-permute-start | bytes 1572872 | tf_op jit(solution)/shard_map/ppermute | solution.py:966
  159.8 34.3 %collective-permute-start.15 = (bf16[128,2048]{1,0:T(8,128)(2,1)S(1)}, bf16[128,2048]{1,0:T(8,128)(2,1)}, u32[]{:S(2)}, u32[]{:S(2)}) collective-permute-start(bf16[128,2048]{1,0:T(8,128)(2,1)S(1)} %copy-done.21), channel_id=1, source_target_pairs={{0,24},{8,0},{16,8},{24,16},{1,25},{9,1},{17,9},{25,17},{2,26},{10... | collective-permute-start | bytes 1572872 | tf_op jit(solution)/shard_map/ppermute | solution.py:979
  198.2 209.4 %reduce-scatter.5.cloned.1.call-start = ((), (), s32[]{:S(2)}) async-start(), calls=%async_computation.20 | async-start | bytes 5242880 | tf_op jit(solution)/shard_map/reduce_scatter | solution.py:1117
  201.8 44.6 %collective-permute-start.17 = (bf16[128,2048]{1,0:T(8,128)(2,1)}, bf16[128,2048]{1,0:T(8,128)(2,1)S(1)}, u32[]{:S(2)}, u32[]{:S(2)}) collective-permute-start(bf16[128,2048]{1,0:T(8,128)(2,1)} %get-tuple-element.295.refs_0_), channel_id=1, source_target_pairs={{0,16},{8,24},{16,0},{24,8},{1,17},{9,25},{17,1},{25,9},{2,18},{10... | collective-permute-start | bytes 1572872 | tf_op jit(solution)/shard_map/ppermute | solution.py:979
  201.8 44.6 %collective-permute-start.16 = (bf16[128,2048]{1,0:T(8,128)(2,1)}, bf16[128,2048]{1,0:T(8,128)(2,1)S(1)}, u32[]{:S(2)}, u32[]{:S(2)}) collective-permute-start(bf16[128,2048]{1,0:T(8,128)(2,1)} %get-tuple-element.295.refs_0_), channel_id=1, source_target_pairs={{0,8},{8,16},{16,24},{24,0},{1,9},{9,17},{17,25},{25,1},{2,10},{10... | collective-permute-start | bytes 1572872 | tf_op jit(solution)/shard_map/ppermute | solution.py:979
  202.9 44.0 %collective-permute-start.19 = (bf16[128,2048]{1,0:T(8,128)(2,1)}, bf16[128,2048]{1,0:T(8,128)(2,1)S(1)}, u32[]{:S(2)}, u32[]{:S(2)}) collective-permute-start(bf16[128,2048]{1,0:T(8,128)(2,1)} %get-tuple-element.295.refs_0_), channel_id=1, source_target_pairs={{0,2},{2,0},{1,3},{3,1},{4,6},{6,4},{5,7},{7,5},{8,10},{10,8},{9,1... | collective-permute-start | bytes 1572872 | tf_op jit(solution)/shard_map/ppermute | solution.py:966
  315.8 129.5 %reduce-scatter.7.cloned.1.call-start = ((), (), s32[]{:S(2)}) async-start(), calls=%async_computation.21 | async-start | bytes 5242880 | tf_op jit(solution)/shard_map/reduce_scatter | solution.py:1117
  359.0 48.5 %collective-permute-start.40 = (bf16[128,2048]{1,0:T(8,128)(2,1)}, bf16[128,2048]{1,0:T(8,128)(2,1)S(1)}, u32[]{:S(2)}, u32[]{:S(2)}) collective-permute-start(bf16[128,2048]{1,0:T(8,128)(2,1)} %get-tuple-element.374), channel_id=1, source_target_pairs={{0,24},{8,0},{16,8},{24,16},{1,25},{9,1},{17,9},{25,17},{2,26},{10... | collective-permute-start | bytes 1572872 | tf_op jit(solution)/shard_map/ppermute | solution.py:979
  361.9 45.6 %collective-permute-start.41 = (bf16[128,2048]{1,0:T(8,128)(2,1)S(1)}, bf16[128,2048]{1,0:T(8,128)(2,1)S(1)}, u32[]{:S(2)}, u32[]{:S(2)}) collective-permute-start(bf16[128,2048]{1,0:T(8,128)(2,1)S(1)} %copy-done.65), channel_id=1, source_target_pairs={{0,16},{8,24},{16,0},{24,8},{1,17},{9,25},{17,1},{25,9},{2,18},{10... | collective-permute-start | bytes 1572872 | tf_op jit(solution)/shard_map/ppermute | solution.py:979
  361.9 45.6 %collective-permute-start.42 = (bf16[128,2048]{1,0:T(8,128)(2,1)S(1)}, bf16[128,2048]{1,0:T(8,128)(2,1)S(1)}, u32[]{:S(2)}, u32[]{:S(2)}) collective-permute-start(bf16[128,2048]{1,0:T(8,128)(2,1)S(1)} %copy-done.64), channel_id=1, source_target_pairs={{0,8},{8,16},{16,24},{24,0},{1,9},{9,17},{17,25},{25,1},{2,10},{10... | collective-permute-start | bytes 1572872 | tf_op jit(solution)/shard_map/ppermute | solution.py:979
  366.3 41.3 %all-to-all-start.5 = ((f32[32,1,128]{2,1,0:T(1,128)}), f32[32,1,128]{2,1,0:T(1,128)S(1)}, u32[]{:S(2)}, u32[]{:S(2)}) async-start(f32[32,1,128]{2,1,0:T(1,128)} %bitcast.132), calls=%async_computation.6 | async-start | bytes 32768 | tf_op jit(solution)/shard_map/all_to_all | solution.py:953
  407.6 37.7 %all-to-all-start.6 = ((bf16[8,128,512]{2,1,0:T(8,128)(2,1)}), bf16[8,128,512]{2,1,0:T(8,128)(2,1)S(1)}, u32[]{:S(2)}, u32[]{:S(2)}) async-start(bf16[8,128,512]{2,1,0:T(8,128)(2,1)} %bitcast.125), calls=%async_computation.8 | async-start | bytes 2097152 | tf_op jit(solution)/shard_map/all_to_all | solution.py:953
  413.6 102.7 %reduce-scatter.9.cloned.1.call-start = ((), (), s32[]{:S(2)}) async-start(), calls=%async_computation.22 | async-start | bytes 5242880 | tf_op jit(solution)/shard_map/reduce_scatter | solution.py:1117
  450.5 34.2 %all-to-all-start.7 = ((bf16[8,128,512]{2,1,0:T(8,128)(2,1)}), bf16[8,128,512]{2,1,0:T(8,128)(2,1)S(1)}, u32[]{:S(2)}, u32[]{:S(2)}) async-start(bf16[8,128,512]{2,1,0:T(8,128)(2,1)} %bitcast.124), calls=%async_computation.9 | async-start | bytes 2097152 | tf_op jit(solution)/shard_map/all_to_all | solution.py:953
  516.3 44.4 %all-to-all-start.9 = ((bf16[8,128,512]{2,1,0:T(8,128)(2,1)}), bf16[8,128,512]{2,1,0:T(8,128)(2,1)S(1)}, u32[]{:S(2)}, u32[]{:S(2)}) async-start(bf16[8,128,512]{2,1,0:T(8,128)(2,1)} %bitcast.127), calls=%async_computation.12 | async-start | bytes 2097152 | tf_op jit(solution)/shard_map/all_to_all | solution.py:953
  519.9 57.2 %reduce-scatter.11.cloned.1.call-start = ((), (), s32[]{:S(2)}) async-start(), calls=%async_computation.23 | async-start | bytes 1310720 | tf_op jit(solution)/shard_map/reduce_scatter | solution.py:1162
  (121 other events, 1032.8 us)
Sparse Core Ops, SparseCore 0:
  29.8 41.3 all-gather.4
  73.6 65.1 all-gather.6
  152.2 72.6 all-gather.8
  226.6 52.6 all-gather.10
  315.1 52.6 reduce-scatter.4
  371.5 64.8 reduce-scatter.6
  450.6 62.7 reduce-scatter.8
  523.7 40.1 reduce-scatter.10
